TPU v7x, 32 devices: a whole 2x2x4 slice. The times are simulated.
32 devices in a mesh: wide: 8 (over z, x), narrow: 4 (over y, core).
Axes of the slice: x: 2, y: 2, z: 4, core: 2. Of those that a mesh axis runs over, the one named last changes fastest.
Arguments:
- tokens: bfloat16 [32768, 768], P(('wide', 'narrow')), may hold values from -6 to 6
- features: bfloat16 [32, 24, 24, 1024], P(('wide', 'narrow'))
- segments: int32 [32, 1024], P(('wide', 'narrow')), may hold values from 0 to 7, never falling along the last dimension, each value on 1 to 512 neighbouring positions
- positions: int32 [32, 576], P(('wide', 'narrow')), may hold values from 0 to 1023, as said below
- w_qkv: bfloat16 [768, 2304], P(('wide', 'narrow')), may hold values from -0.21875 to 0.21875
- w_out: bfloat16 [768, 768], P(('wide', 'narrow')), may hold values from -0.21875 to 0.21875
- w_up: bfloat16 [768, 3072], P(('wide', 'narrow')), may hold values from -0.21875 to 0.21875
- w_down: bfloat16 [3072, 768], P(('wide', 'narrow')), may hold values from -0.109375 to 0.109375
- gain_pre: bfloat16 [768], P(('wide', 'narrow')), may hold values from 0.099609375 to 1.8984375
- gain_attn: bfloat16 [768], P(('wide', 'narrow')), may hold values from 0.099609375 to 1.8984375
- gain_mid: bfloat16 [768], P(('wide', 'narrow')), may hold values from 0.099609375 to 1.8984375
- gain_ffn: bfloat16 [3072], P(('wide', 'narrow')), may hold values from 0.099609375 to 1.8984375
- rel_table: bfloat16 [12, 256], P(None, ('wide', 'narrow')), may hold values from -4 to 4
- head_scale: float32 [12], replicated, may hold values from 0.3 to 3
- w_reduce: bfloat16 [1024, 256], P(('wide', 'narrow')), may hold values from -0.1875 to 0.1875
- w_spatial: bfloat16 [2304, 256], P(('wide', 'narrow')), may hold values from -0.125 to 0.125
- w_expand: bfloat16 [256, 1024], P(('wide', 'narrow')), may hold values from -0.375 to 0.375
- w_embed: bfloat16 [1024, 768], P(('wide', 'narrow')), may hold values from -0.1875 to 0.1875
- bn_gain: bfloat16 [1024], P(('wide', 'narrow')), may hold values from 0.099609375 to 1.8984375
- bn_shift: bfloat16 [1024], P(('wide', 'narrow')), may hold values from -3 to 3
- d_out: bfloat16 [32768, 768], P(('wide', 'narrow')), may hold values from -6 to 6
Outputs:
- mixed: bfloat16 [32768, 768], P(('wide', 'narrow'))
- d_tokens: float32 [32768, 768], P(('wide', 'narrow'))
- d_features: float32 [32, 24, 24, 1024], P(('wide', 'narrow'))
- d_w_qkv: float32 [768, 2304], P('wide', 'narrow')
- d_w_out: float32 [768, 768], P(('wide', 'narrow'))
- d_w_up: float32 [768, 3072], P('wide', 'narrow')
- d_w_down: float32 [3072, 768], P('narrow', 'wide')
- d_gain_pre: float32 [768], P(('wide', 'narrow'))
- d_gain_attn: float32 [768], P(('wide', 'narrow'))
- d_gain_mid: float32 [768], P(('wide', 'narrow'))
- d_gain_ffn: float32 [3072], P(('wide', 'narrow'))
- d_rel_table: float32 [12, 256], P(None, ('wide', 'narrow'))
- d_head_scale: float32 [12], replicated
- d_w_reduce: float32 [1024, 256], P(('wide', 'narrow'))
- d_w_spatial: float32 [2304, 256], P(('wide', 'narrow'))
- d_w_expand: float32 [256, 1024], P(('wide', 'narrow'))
- d_w_embed: float32 [1024, 768], P(('wide', 'narrow'))
- d_bn_gain: float32 [1024], P(('wide', 'narrow'))
- d_bn_shift: float32 [1024], P(('wide', 'narrow'))
Inputs may be any that keep to these rules, and one draw needn't show every extreme that they name: `segments`: each row's segment numbers never fall; a segment has 1 to 512 tokens. Each image's patches take 576 consecutive positions of its own row, in row-major order; the first row's image begins at 0 and the last row's ends at 1023.
All inputs are finite; a program needn't handle non-finite values.
Results may differ from a plain program's by a relative error of at most 0.017.
Values may be sent and summed in bfloat16 or wider, within the bound.
A program may use at most 320 MiB of HBM per device.

v0:
```python
import jax
import jax.numpy as jnp
from jax import lax
from jax.experimental import pallas as pl
from jax.experimental.pallas import tpu as pltpu
from jax.sharding import PartitionSpec as P

D = 768
HEADS = 12
HDIM = 64
RSPAN = 128


epsilon = 1e-05


def product(lhs_matrix, rhs_matrix):
    return jnp.dot(lhs_matrix, rhs_matrix, preferred_element_type=jnp.float32)


def product_tn(lhs_matrix, rhs_matrix):
    return lax.dot_general(
        lhs_matrix, rhs_matrix, (((0,), (0,)), ((), ())), preferred_element_type=jnp.float32
    )


def product_nt(lhs_matrix, rhs_matrix):
    return lax.dot_general(
        lhs_matrix, rhs_matrix, (((1,), (1,)), ((), ())), preferred_element_type=jnp.float32
    )


def layer_norm(values, gain):
    average = jnp.mean(values, axis=-1, keepdims=True)
    centred = values - average
    inv_std = lax.rsqrt(jnp.mean(centred * centred, axis=-1, keepdims=True) + epsilon)
    unit_rows = centred * inv_std
    return (unit_rows * gain, unit_rows, inv_std)


def layer_norm_back(cotangent, unit_rows, inv_std, gain):
    weighted = cotangent * gain
    inner = (
        weighted
        - jnp.mean(weighted, axis=-1, keepdims=True)
        - unit_rows * jnp.mean(weighted * unit_rows, axis=-1, keepdims=True)
    )
    return (inv_std * inner, jnp.sum(cotangent * unit_rows, axis=0))


def smooth(values):
    return jax.nn.gelu(values, approximate=True)


def smooth_back(values, cotangent):
    unused, pullback = jax.vjp(smooth, values)
    return pullback(cotangent)[0]


def unfold(grid):
    side = grid.shape[1]
    padded = jnp.pad(grid, ((0, 0), (1, 1), (1, 1), (0, 0)))
    pieces = [
        padded[:, row_off : row_off + side, col_off : col_off + side, :]
        for row_off in range(3)
        for col_off in range(3)
    ]
    return jnp.concatenate(pieces, axis=-1)


def fold(columns):
    channels = columns.shape[-1] // 9
    side = columns.shape[1]
    total = jnp.zeros((columns.shape[0], side + 2, side + 2, channels), jnp.float32)
    for row_off in range(3):
        for col_off in range(3):
            which = row_off * 3 + col_off
            piece = columns[..., which * channels : (which + 1) * channels]
            total = total + jnp.pad(
                piece, ((0, 0), (row_off, 2 - row_off), (col_off, 2 - col_off), (0, 0))
            )
    return total[:, 1:-1, 1:-1, :]


PAIRS = HEADS // 2
BLK = 128
NEG = -1e30


def dot_nn(a, b):
    return lax.dot_general(a, b, (((1,), (0,)), ((), ())), preferred_element_type=jnp.float32)


def dot_nt(a, b):
    return lax.dot_general(a, b, (((1,), (1,)), ((), ())), preferred_element_type=jnp.float32)


def split_heads(pair, scale):
    lane = lax.broadcasted_iota(jnp.int32, pair.shape, 1)
    vals = pair * jnp.asarray(scale, pair.dtype)
    zero = jnp.zeros_like(vals)
    return jnp.concatenate([jnp.where(lane < HDIM, vals, zero), jnp.where(lane < HDIM, zero, vals)], axis=0)


def join_heads(both):
    row = lax.broadcasted_iota(jnp.int32, (2 * HDIM, BLK), 0)
    return jnp.where(row < HDIM, both[:, :BLK], both[:, BLK:])


def bias_strips(table):
    rev = jnp.flip(table.astype(jnp.float32), axis=1)
    first, last = rev[:, 255:256], rev[:, 0:1]
    below = jnp.concatenate([jnp.broadcast_to(first, (HEADS, 129)), rev[:, 128:255]], axis=1)
    middle = jnp.concatenate([rev[:, 127:256], rev[:, 0:127]], axis=1)
    above = jnp.concatenate([last, rev[:, 0:127], jnp.broadcast_to(last, (HEADS, 128))], axis=1)
    low = jnp.broadcast_to(first, (HEADS, 256))
    high = jnp.broadcast_to(last, (HEADS, 256))
    return jnp.stack([low, below, middle, above, high], axis=1)


def table_from_strips(sums):
    low, below, middle, above, high = (sums[:, i] for i in range(5))
    total = jnp.concatenate([middle[:, 129:256], middle[:, 0:129]], axis=1)
    zero = jnp.zeros((HEADS, 127), jnp.float32)
    first = jnp.sum(low, axis=1, keepdims=True) + jnp.sum(below[:, :129], axis=1, keepdims=True)
    last = jnp.sum(high, axis=1, keepdims=True) + above[:, 0:1] + jnp.sum(above[:, 128:], axis=1, keepdims=True)
    total = total + jnp.concatenate([jnp.zeros((HEADS, 128), jnp.float32), below[:, 129:], first], axis=1)
    head = jnp.concatenate([above[:, 1:128], jnp.zeros((HEADS, 129), jnp.float32)], axis=1)
    total = total + head + jnp.concatenate([last, jnp.zeros((HEADS, 255), jnp.float32)], axis=1)
    return jnp.flip(total, axis=1)


def windows(segments):
    seg = segments.reshape(-1)
    starts = seg[::BLK]
    ends = seg[BLK - 1 :: BLK]
    low = jnp.sum((seg[None, :] < starts[:, None]).astype(jnp.int32), axis=1) // BLK
    high = (jnp.sum((seg[None, :] <= ends[:, None]).astype(jnp.int32), axis=1) + BLK - 1) // BLK
    return jnp.stack([low, high])


def attend_kernel(win, packed, segk, segq, strips, out, logsum, bias, vt, qm, acc, stat):
    i = pl.program_id(0)

    @pl.when(i == 0)
    def _():
        for hp in range(PAIRS):
            vt[pl.ds(hp * 128, 128), :] = packed[:, pl.ds(2 * D + hp * 128, 128)].T
            for d in range(5):
                for half in range(2):
                    row = strips[2 * hp + half, pl.ds(d, 1), :]
                    tile = jnp.broadcast_to(row, (BLK, 256))
                    if 0 < d < 4:
                        tile = pltpu.roll(tile, 0, 1, stride=1, stride_axis=0)
                    bias[hp, d, :, pl.ds(half * BLK, BLK)] = tile[:, :BLK]

    rows = pl.ds(pl.multiple_of(i * BLK, BLK), BLK)
    for hp in range(PAIRS):
        qm[hp] = split_heads(packed[rows, pl.ds(hp * 128, 128)], HDIM ** -0.5)
        acc[hp] = jnp.zeros((128, 256), jnp.float32)
        stat[hp, 0] = jnp.full((1, 256), NEG, jnp.float32)
        stat[hp, 1] = jnp.zeros((1, 256), jnp.float32)
    sq = segq[:, rows]
    sq2 = jnp.concatenate([sq, sq], axis=1)

    def body(kb, carry):
        keys = pl.ds(pl.multiple_of(kb * BLK, BLK), BLK)
        allowed = segk[keys, :] == sq2
        d = jnp.clip(kb - i, -2, 2) + 2
        for hp in range(PAIRS):
            s = dot_nt(packed[keys, pl.ds(D + hp * 128, 128)], qm[hp])
            s = jnp.where(allowed, s + bias[hp, d], NEG)
            old = stat[hp, 0]
            new = jnp.maximum(old, jnp.max(s, axis=0, keepdims=True))
            p = jnp.exp(s - new)
            alpha = jnp.exp(old - new)
            stat[hp, 0] = new
            stat[hp, 1] = stat[hp, 1] * alpha + jnp.sum(p, axis=0, keepdims=True)
            acc[hp] = acc[hp] * alpha + dot_nn(vt[pl.ds(hp * 128, 128), keys], p.astype(jnp.bfloat16))
        return carry

    lax.fori_loop(win[0, i], win[1, i], body, 0)
    for hp in range(PAIRS):
        total = stat[hp, 1]
        out[:, pl.ds(hp * 128, 128)] = join_heads(acc[hp] / total).T
        logsum[0, pl.ds(hp, 1), :] = stat[hp, 0] + jnp.log(total)


def attend(packed, segments, strips, win):
    length = packed.shape[0]
    blocks = length // BLK
    seg = segments.reshape(1, length)
    whole = lambda shape: pl.BlockSpec(shape, lambda i, w: (0,) * len(shape))
    return pl.pallas_call(
        attend_kernel,
        out_shape=(
            jax.ShapeDtypeStruct((length, D), jnp.float32),
            jax.ShapeDtypeStruct((blocks, PAIRS, 256), jnp.float32),
            jax.ShapeDtypeStruct((PAIRS, 5, BLK, 256), jnp.float32),
        ),
        grid_spec=pltpu.PrefetchScalarGridSpec(
            num_scalar_prefetch=1,
            grid=(blocks,),
            in_specs=[whole((length, 3 * D)), whole((length, 1)), whole((1, length)), whole((HEADS, 5, 256))],
            out_specs=(
                pl.BlockSpec((BLK, D), lambda i, w: (i, 0)),
                pl.BlockSpec((1, PAIRS, 256), lambda i, w: (i, 0, 0)),
                whole((PAIRS, 5, BLK, 256)),
            ),
            scratch_shapes=[
                pltpu.VMEM((D, length), jnp.bfloat16),
                pltpu.VMEM((PAIRS, 256, 128), jnp.bfloat16),
                pltpu.VMEM((PAIRS, 128, 256), jnp.float32),
                pltpu.VMEM((PAIRS, 2, 1, 256), jnp.float32),
            ],
        ),
        compiler_params=pltpu.CompilerParams(vmem_limit_bytes=48 * 2**20),
        cost_estimate=pl.CostEstimate(flops=2 * 10**10, bytes_accessed=10**7, transcendentals=6 * 10**6),
        name="attend",
    )(win, packed, seg.reshape(length, 1), seg, strips)


def unskew(tile):
    row = lax.broadcasted_iota(jnp.int32, tile.shape, 0)
    width = tile.shape[1]
    for bit in range(7):
        step = 1 << bit
        tile = jnp.where((row & step) != 0, pltpu.roll(tile, width - step, 1), tile)
    return tile


def attend_back_kernel(win, packed, grads, attended, segk, segq, bias, logsum, out, tab, kt, qm, om, dqt, dk, dv, gt):
    i = pl.program_id(0)
    last = pl.num_programs(0) - 1

    @pl.when(i == 0)
    def _():
        for hp in range(PAIRS):
            kt[pl.ds(hp * 128, 128), :] = packed[:, pl.ds(D + hp * 128, 128)].T
        dk[...] = jnp.zeros_like(dk)
        dv[...] = jnp.zeros_like(dv)
        gt[...] = jnp.zeros_like(gt)

    rows = pl.ds(pl.multiple_of(i * BLK, BLK), BLK)
    dots = []
    for hp in range(PAIRS):
        cols = pl.ds(hp * 128, 128)
        qm[hp] = split_heads(packed[rows, cols], HDIM ** -0.5)
        om[hp] = split_heads(grads[:, cols], 1.0)
        cross = (grads[:, cols].astype(jnp.float32) * attended[:, cols]).T
        dots.append(jnp.concatenate([
            jnp.sum(cross[:HDIM], axis=0, keepdims=True),
            jnp.sum(cross[HDIM:], axis=0, keepdims=True)], axis=1))
        dqt[hp] = jnp.zeros((128, 256), jnp.float32)
    sq = segq[:, rows]
    sq2 = jnp.concatenate([sq, sq], axis=1)

    def body(kb, carry):
        keys = pl.ds(pl.multiple_of(kb * BLK, BLK), BLK)
        allowed = segk[keys, :] == sq2
        d = jnp.clip(kb - i, -2, 2) + 2
        for hp in range(PAIRS):
            cols = pl.ds(hp * 128, 128)
            s = dot_nt(packed[keys, pl.ds(D + hp * 128, 128)], qm[hp]) + bias[hp, d]
            p = jnp.exp(jnp.where(allowed, s, NEG) - logsum[0, pl.ds(hp, 1), :])
            dp = dot_nt(packed[keys, pl.ds(2 * D + hp * 128, 128)], om[hp])
            ds = p * (dp - dots[hp])
            gt[hp, d] += ds
            low = ds.astype(jnp.bfloat16)
            dv[keys, cols] += dot_nn(p.astype(jnp.bfloat16), om[hp])
            dk[keys, cols] += dot_nn(low, qm[hp])
            dqt[hp] += dot_nn(kt[cols, keys], low)
        return carry

    lax.fori_loop(win[0, i], win[1, i], body, 0)
    for hp in range(PAIRS):
        out[rows, pl.ds(hp * 128, 128)] = (join_heads(dqt[hp]).T * (HDIM ** -0.5)).astype(jnp.bfloat16)

    @pl.when(i == last)
    def _():
        out[:, pl.ds(D, D)] = dk[...].astype(jnp.bfloat16)
        out[:, pl.ds(2 * D, D)] = dv[...].astype(jnp.bfloat16)
        for hp in range(PAIRS):
            for half in range(2):
                for d in range(5):
                    tile = gt[hp, d, :, pl.ds(half * BLK, BLK)]
                    tile = jnp.concatenate([tile, jnp.zeros_like(tile)], axis=1)
                    if 0 < d < 4:
                        tile = unskew(tile)
                    tab[2 * hp + half, pl.ds(d, 1), :] = jnp.sum(tile, axis=0, keepdims=True)


def attend_back(packed, grads, attended, segments, bias, logsum, win):
    length = packed.shape[0]
    blocks = length // BLK
    seg = segments.reshape(1, length)
    whole = lambda shape: pl.BlockSpec(shape, lambda i, w: (0,) * len(shape))
    return pl.pallas_call(
        attend_back_kernel,
        out_shape=(
            jax.ShapeDtypeStruct((length, 3 * D), jnp.bfloat16),
            jax.ShapeDtypeStruct((HEADS, 5, 256), jnp.float32),
        ),
        grid_spec=pltpu.PrefetchScalarGridSpec(
            num_scalar_prefetch=1,
            grid=(blocks,),
            in_specs=[
                whole((length, 3 * D)),
                pl.BlockSpec((BLK, D), lambda i, w: (i, 0)),
                pl.BlockSpec((BLK, D), lambda i, w: (i, 0)),
                whole((length, 1)),
                whole((1, length)),
                whole((PAIRS, 5, BLK, 256)),
                pl.BlockSpec((1, PAIRS, 256), lambda i, w: (i, 0, 0)),
            ],
            out_specs=(whole((length, 3 * D)), whole((HEADS, 5, 256))),
            scratch_shapes=[
                pltpu.VMEM((D, length), jnp.bfloat16),
                pltpu.VMEM((PAIRS, 256, 128), jnp.bfloat16),
                pltpu.VMEM((PAIRS, 256, 128), jnp.bfloat16),
                pltpu.VMEM((PAIRS, 128, 256), jnp.float32),
                pltpu.VMEM((length, D), jnp.float32),
                pltpu.VMEM((length, D), jnp.float32),
                pltpu.VMEM((PAIRS, 5, BLK, 256), jnp.float32),
            ],
        ),
        compiler_params=pltpu.CompilerParams(vmem_limit_bytes=56 * 2**20),
        cost_estimate=pl.CostEstimate(flops=5 * 10**10, bytes_accessed=2 * 10**7, transcendentals=6 * 10**6),
        name="attend_back",
    )(win, packed, grads, attended, seg.reshape(length, 1), seg, bias, logsum)


def local(
    tokens,
    features,
    segments,
    positions,
    w_qkv,
    w_out,
    w_up,
    w_down,
    gain_pre,
    gain_attn,
    gain_mid,
    gain_ffn,
    rel_table,
    head_scale,
    w_reduce,
    w_spatial,
    w_expand,
    w_embed,
    bn_gain,
    bn_shift,
    d_out,
):
    gathered = (
        lax.all_gather(w_qkv, ("wide", "narrow"), axis=0, tiled=True),
        lax.all_gather(w_out, ("wide", "narrow"), axis=0, tiled=True),
        lax.all_gather(w_up, ("wide", "narrow"), axis=0, tiled=True),
        lax.all_gather(w_down, ("wide", "narrow"), axis=0, tiled=True),
        lax.all_gather(gain_pre, ("wide", "narrow"), axis=0, tiled=True),
        lax.all_gather(gain_attn, ("wide", "narrow"), axis=0, tiled=True),
        lax.all_gather(gain_mid, ("wide", "narrow"), axis=0, tiled=True),
        lax.all_gather(gain_ffn, ("wide", "narrow"), axis=0, tiled=True),
        lax.all_gather(rel_table, ("wide", "narrow"), axis=1, tiled=True),
        lax.all_gather(w_reduce, ("wide", "narrow"), axis=0, tiled=True),
        lax.all_gather(w_spatial, ("wide", "narrow"), axis=0, tiled=True),
        lax.all_gather(w_expand, ("wide", "narrow"), axis=0, tiled=True),
        lax.all_gather(w_embed, ("wide", "narrow"), axis=0, tiled=True),
        lax.all_gather(bn_gain, ("wide", "narrow"), axis=0, tiled=True),
        lax.all_gather(bn_shift, ("wide", "narrow"), axis=0, tiled=True),
    )
    (
        full_qkv,
        full_out,
        full_up,
        full_down,
        full_pre,
        full_attn,
        full_mid,
        full_ffn,
        full_table,
        full_reduce,
        full_spatial,
        full_expand,
        full_embed,
        full_bn_gain,
        full_bn_shift,
    ) = gathered
    rows, length = (segments.shape[0], segments.shape[1])
    images, side = (features.shape[0], features.shape[1])
    patch_count = images * side * side
    whole = patch_count * lax.axis_size(("wide", "narrow"))
    stem_in = features.reshape(patch_count, features.shape[3])
    pre_first = product(stem_in, full_reduce)
    first = smooth(pre_first).astype(jnp.bfloat16)
    columns = unfold(first.reshape(images, side, side, first.shape[1])).reshape(
        patch_count, 9 * first.shape[1]
    )
    pre_second = product(columns, full_spatial)
    second = smooth(pre_second).astype(jnp.bfloat16)
    third = product(second, full_expand)
    bn_total, bn_squares = lax.psum(
        (jnp.sum(third, axis=0), jnp.sum(third * third, axis=0)), ("wide", "narrow")
    )
    bn_mean = bn_total / whole
    bn_inv = lax.rsqrt(bn_squares / whole - bn_mean * bn_mean + epsilon)
    bn_unit = (third - bn_mean) * bn_inv
    pre_joined = (
        bn_unit * full_bn_gain.astype(jnp.float32)
        + full_bn_shift.astype(jnp.float32)
        + stem_in.astype(jnp.float32)
    )
    joined = smooth(pre_joined).astype(jnp.bfloat16)
    embedded = product(joined, full_embed).reshape(images, side * side, -1)
    row_index = jnp.arange(rows, dtype=jnp.int32)[:, None]
    start_rows = (
        tokens.astype(jnp.float32).reshape(rows, length, -1).at[row_index, positions].add(embedded)
    )
    start = start_rows.reshape(rows * length, -1)
    normed0, unit0, inv0 = layer_norm(start, full_pre.astype(jnp.float32))
    normed0_low = normed0.astype(jnp.bfloat16)
    packed = product(normed0_low, full_qkv).astype(jnp.bfloat16)
    win = windows(segments)
    attended, logsums, bias = attend(packed, segments, bias_strips(full_table), win)
    scale_row = jnp.repeat(head_scale, HDIM)[None, :]
    scaled = attended * scale_row
    mixed_in, unit1, inv1 = layer_norm(scaled, full_attn.astype(jnp.float32))
    mixed_low = mixed_in.astype(jnp.bfloat16)
    middle = start + product(mixed_low, full_out)
    normed2, unit2, inv2 = layer_norm(middle, full_mid.astype(jnp.float32))
    normed2_low = normed2.astype(jnp.bfloat16)
    pre_up = product(normed2_low, full_up)
    activ = smooth(pre_up)
    narrowed, unit3, inv3 = layer_norm(activ, full_ffn.astype(jnp.float32))
    narrowed_low = narrowed.astype(jnp.bfloat16)
    result = middle + product(narrowed_low, full_down)
    mixed = result.astype(jnp.bfloat16)
    group_norm0, group_norm2, group_out = (
        lax.all_gather(normed0_low, "narrow", axis=0, tiled=True),
        lax.all_gather(normed2_low, "narrow", axis=0, tiled=True),
        lax.all_gather(d_out, "narrow", axis=0, tiled=True),
    )
    again = (
        lax.all_gather(w_qkv, ("wide", "narrow"), axis=0, tiled=True),
        lax.all_gather(w_out, ("wide", "narrow"), axis=0, tiled=True),
        lax.all_gather(w_up, ("wide", "narrow"), axis=0, tiled=True),
        lax.all_gather(w_down, ("wide", "narrow"), axis=0, tiled=True),
        lax.all_gather(gain_pre, ("wide", "narrow"), axis=0, tiled=True),
        lax.all_gather(gain_attn, ("wide", "narrow"), axis=0, tiled=True),
        lax.all_gather(gain_mid, ("wide", "narrow"), axis=0, tiled=True),
        lax.all_gather(gain_ffn, ("wide", "narrow"), axis=0, tiled=True),
        lax.all_gather(rel_table, ("wide", "narrow"), axis=1, tiled=True),
        lax.all_gather(w_reduce, ("wide", "narrow"), axis=0, tiled=True),
        lax.all_gather(w_spatial, ("wide", "narrow"), axis=0, tiled=True),
        lax.all_gather(w_expand, ("wide", "narrow"), axis=0, tiled=True),
        lax.all_gather(w_embed, ("wide", "narrow"), axis=0, tiled=True),
        lax.all_gather(bn_gain, ("wide", "narrow"), axis=0, tiled=True),
        lax.all_gather(bn_shift, ("wide", "narrow"), axis=0, tiled=True),
    )
    (
        back_qkv,
        back_out,
        back_up,
        back_down,
        back_pre,
        back_attn,
        back_mid,
        back_ffn,
        back_table,
        back_reduce,
        back_spatial,
        back_expand,
        back_embed,
        back_bn_gain,
        back_bn_shift,
    ) = again
    grad_result = d_out.astype(jnp.float32)
    grad_narrowed = product_nt(d_out, back_down)
    grad_activ, grad_gain_ffn = layer_norm_back(
        grad_narrowed, unit3, inv3, back_ffn.astype(jnp.float32)
    )
    grad_pre_up = smooth_back(pre_up, grad_activ).astype(jnp.bfloat16)
    ffn_grad_cols, ffn_act_cols = (
        lax.all_to_all(grad_pre_up, "narrow", split_axis=1, concat_axis=0, tiled=True),
        lax.all_to_all(narrowed_low, "narrow", split_axis=1, concat_axis=0, tiled=True),
    )
    grad_w_down = product_tn(ffn_act_cols, group_out)
    grad_w_up = product_tn(group_norm2, ffn_grad_cols)
    grad_normed2 = product_nt(grad_pre_up, back_up)
    grad_mid_in, grad_gain_mid = layer_norm_back(
        grad_normed2, unit2, inv2, back_mid.astype(jnp.float32)
    )
    grad_middle = grad_result + grad_mid_in
    grad_branch = grad_middle.astype(jnp.bfloat16)
    grad_w_out = product_tn(mixed_low, grad_branch)
    grad_mixed_in = product_nt(grad_branch, back_out)
    grad_scaled, grad_gain_attn = layer_norm_back(
        grad_mixed_in, unit1, inv1, back_attn.astype(jnp.float32)
    )
    grad_head_local = jnp.sum(jnp.sum(grad_scaled * attended, axis=0).reshape(HEADS, HDIM), axis=1)
    grad_attended = (grad_scaled * scale_row).astype(jnp.bfloat16)
    grad_packed, grad_strips = attend_back(packed, grad_attended, attended, segments, bias, logsums, win)
    grad_table = table_from_strips(grad_strips)
    qkv_cols = lax.all_to_all(grad_packed, "narrow", split_axis=1, concat_axis=0, tiled=True)
    grad_w_qkv = product_tn(group_norm0, qkv_cols)
    sum_qkv, sum_up, sum_down = (
        lax.psum_scatter(
            grad_w_qkv.astype(jnp.bfloat16), "wide", scatter_dimension=0, tiled=True
        ).astype(jnp.float32),
        lax.psum_scatter(
            grad_w_up.astype(jnp.bfloat16), "wide", scatter_dimension=0, tiled=True
        ).astype(jnp.float32),
        lax.psum_scatter(
            grad_w_down.astype(jnp.bfloat16), "wide", scatter_dimension=1, tiled=True
        ).astype(jnp.float32),
    )
    grad_normed0 = product_nt(grad_packed, back_qkv)
    grad_start_in, grad_gain_pre = layer_norm_back(
        grad_normed0, unit0, inv0, back_pre.astype(jnp.float32)
    )
    grad_tokens = grad_middle + grad_start_in
    grad_embedded = (
        grad_tokens.reshape(rows, length, -1)[row_index, positions]
        .reshape(patch_count, -1)
        .astype(jnp.bfloat16)
    )
    grad_w_embed = product_tn(joined, grad_embedded)
    grad_joined = product_nt(grad_embedded, back_embed)
    grad_pre_joined = smooth_back(pre_joined, grad_joined)
    grad_bn_shift = jnp.sum(grad_pre_joined, axis=0)
    grad_bn_gain = jnp.sum(grad_pre_joined * bn_unit, axis=0)
    grad_unit = grad_pre_joined * back_bn_gain.astype(jnp.float32)
    sum_unit, sum_cross, grad_head = lax.psum(
        (jnp.sum(grad_unit, axis=0), jnp.sum(grad_unit * bn_unit, axis=0), grad_head_local),
        ("wide", "narrow"),
    )
    grad_third = (bn_inv * (grad_unit - sum_unit / whole - bn_unit * (sum_cross / whole))).astype(
        jnp.bfloat16
    )
    grad_w_expand = product_tn(second, grad_third)
    grad_second = product_nt(grad_third, back_expand)
    grad_pre_second = smooth_back(pre_second, grad_second).astype(jnp.bfloat16)
    grad_w_spatial = product_tn(columns, grad_pre_second)
    grad_columns = product_nt(grad_pre_second, back_spatial)
    grad_first = fold(grad_columns.reshape(images, side, side, -1)).reshape(patch_count, -1)
    grad_pre_first = smooth_back(pre_first, grad_first).astype(jnp.bfloat16)
    grad_w_reduce = product_tn(stem_in, grad_pre_first)
    grad_features = (grad_pre_joined + product_nt(grad_pre_first, back_reduce)).reshape(
        features.shape
    )
    summed = (
        lax.psum_scatter(grad_w_out, ("wide", "narrow"), scatter_dimension=0, tiled=True),
        lax.psum_scatter(grad_gain_pre, ("wide", "narrow"), scatter_dimension=0, tiled=True),
        lax.psum_scatter(grad_gain_attn, ("wide", "narrow"), scatter_dimension=0, tiled=True),
        lax.psum_scatter(grad_gain_mid, ("wide", "narrow"), scatter_dimension=0, tiled=True),
        lax.psum_scatter(grad_gain_ffn, ("wide", "narrow"), scatter_dimension=0, tiled=True),
        lax.psum_scatter(grad_table, ("wide", "narrow"), scatter_dimension=1, tiled=True),
        lax.psum_scatter(grad_w_reduce, ("wide", "narrow"), scatter_dimension=0, tiled=True),
        lax.psum_scatter(grad_w_spatial, ("wide", "narrow"), scatter_dimension=0, tiled=True),
        lax.psum_scatter(grad_w_expand, ("wide", "narrow"), scatter_dimension=0, tiled=True),
        lax.psum_scatter(grad_w_embed, ("wide", "narrow"), scatter_dimension=0, tiled=True),
        lax.psum_scatter(grad_bn_gain, ("wide", "narrow"), scatter_dimension=0, tiled=True),
        lax.psum_scatter(grad_bn_shift, ("wide", "narrow"), scatter_dimension=0, tiled=True),
    )
    (
        sum_out,
        sum_pre,
        sum_attn,
        sum_mid,
        sum_ffn,
        sum_table,
        sum_reduce,
        sum_spatial,
        sum_expand,
        sum_embed,
        sum_bn_gain,
        sum_bn_shift,
    ) = summed
    return (
        mixed,
        grad_tokens,
        grad_features,
        sum_qkv,
        sum_out,
        sum_up,
        sum_down,
        sum_pre,
        sum_attn,
        sum_mid,
        sum_ffn,
        sum_table,
        grad_head,
        sum_reduce,
        sum_spatial,
        sum_expand,
        sum_embed,
        sum_bn_gain,
        sum_bn_shift,
    )


def solution(mesh):
    placed = (
        P(("wide", "narrow"), None),
        P(("wide", "narrow"), None, None, None),
        P(("wide", "narrow"), None),
        P(("wide", "narrow"), None),
        P(("wide", "narrow"), None),
        P(("wide", "narrow"), None),
        P(("wide", "narrow"), None),
        P(("wide", "narrow"), None),
        P(("wide", "narrow")),
        P(("wide", "narrow")),
        P(("wide", "narrow")),
        P(("wide", "narrow")),
        P(None, ("wide", "narrow")),
        P(),
        P(("wide", "narrow"), None),
        P(("wide", "narrow"), None),
        P(("wide", "narrow"), None),
        P(("wide", "narrow"), None),
        P(("wide", "narrow")),
        P(("wide", "narrow")),
        P(("wide", "narrow"), None),
    )
    return jax.shard_map(
        local,
        mesh=mesh,
        in_specs=placed,
        out_specs=(
            P(("wide", "narrow"), None),
            P(("wide", "narrow"), None),
            P(("wide", "narrow"), None, None, None),
            P("wide", "narrow"),
            P(("wide", "narrow"), None),
            P("wide", "narrow"),
            P("narrow", "wide"),
            P(("wide", "narrow")),
            P(("wide", "narrow")),
            P(("wide", "narrow")),
            P(("wide", "narrow")),
            P(None, ("wide", "narrow")),
            P(),
            P(("wide", "narrow"), None),
            P(("wide", "narrow"), None),
            P(("wide", "narrow"), None),
            P(("wide", "narrow"), None),
            P(("wide", "narrow")),
            P(("wide", "narrow")),
        ),
        check_vma=False,
    )
```

profile of v0, /device:TPU:0, one launch (start us, length us, event | category | flops | bytes accessed | tf_op | source)
XLA Modules:
  0.0 1496.9 jit_solution(7297005486382550842)
XLA Ops:
  16.3 42.3 %all-reduce.28 = (bf16[1024]{0:T(1024)(128)(2,1)S(1)}, bf16[1024]{0:T(1024)(128)(2,1)S(1)}, bf16[768]{0:T(1024)(128)(2,1)S(1)}, bf16[768]{0:T(1024)(128)(2,1)S(1...) all-reduce(bf16[1024]{0:T(1024)(128)(2,1)S(1)} %dynamic-update-slic, ...), channel_id=1, replica_groups=mesh['wide'=8,'narrow'=4] {'wide','narrow'}, use_global_device_ids=true, to_apply=%add.14 | all-reduce | flops 7424 | bytes 29696
  58.6 1.7 reshape.325
  61.0 41.8 %all_gather.67 = bf16[1024,256]{1,0:T(8,128)(2,1)S(1)} all-gather(bf16[32,256]{1,0:T(8,128)(2,1)S(1)} %copy-done.45), channel_id=1, replica_groups=mesh['wide'=8,'narrow'=4] {'wide','narrow'}, dimensions={0}, use_global_device_ids=true | all-gather | bytes 540672 | tf_op jit(solution)/shard_map/all_gather | solution.py:366
  106.2 41.1 %all_gather.69 = bf16[256,1024]{1,0:T(8,128)(2,1)} all-gather(bf16[8,1024]{1,0:T(8,128)(2,1)S(1)} %copy-done.46), channel_id=1, replica_groups=mesh['wide'=8,'narrow'=4] {'wide','narrow'}, dimensions={0}, use_global_device_ids=true | all-gather | bytes 540672 | tf_op jit(solution)/shard_map/all_gather | solution.py:368
  147.3 3.0 fusion.52
  150.3 2.0 fusion.48
  152.3 37.8 %all-reduce.27 = (f32[1024]{0:T(1024)S(1)}, f32[1024]{0:T(1024)S(1)}) all-reduce(f32[1024]{0:T(1024)S(1)} %get-tuple-element.142, f32[1024]{0:T(1024)S(1)} %get-tuple-element.141), channel_id=1, replica_groups=mesh['wide'=8,'narrow'=4] {'wide','narrow'}, use_global_device_ids=true, to_apply=%region_3.4 | all-reduce | flops 2048 | bytes 16384 | tf_op jit(solution)/shard_map/psum | solution.py:403
  190.7 4.2 multiply_convert_fusion.6
  194.9 4.1 fusion.53
  199.0 9.6 scatter_fusion
  208.5 2.4 copy.125
  211.2 2.4 multiply_reduce_fusion.13
  216.3 41.5 %all_gather.75 = bf16[12,256]{0,1:T(8,128)(2,1)S(1)} all-gather(bf16[12,8]{0,1:T(8,128)(2,1)S(1)} %copy-done.49), channel_id=1, replica_groups=mesh['wide'=8,'narrow'=4] {'wide','narrow'}, dimensions={1}, use_global_device_ids=true | all-gather | bytes 6336 | tf_op jit(solution)/shard_map/all_gather | solution.py:365
  258.3 1.6 copy.127
  262.6 7.7 convolution_convert_fusion.packed
  270.3 36.4 %attend.1 = (f32[1024,768]{1,0:T(8,128)S(1)}, f32[8,6,256]{2,1,0:T(8,128)S(1)}, f32[6,5,128,256]{3,2,1,0:T(8,128)}) custom-call(s32[2,8]{1,0:T(2,128)S(1)} %pad_add_fusion.7.win, bf16[1024,2304]{1,0:T(8,128)(2,1)} %convolution_convert_fusion.packed, s32[1024,1]{1,0:T(8,128)S(1)} %copy-done.2, s32[1,1024]{1,0:T(1,128)S(1)} %copy-done.3, ...), custom_call_target="tpu_custom_call" | custom-call | flops 20000000000 | bytes 10000000 | tf_op jit(solution)/shard_map/attend/pallas_call | solution.py:194
  307.6 4.4 fusion.51
  315.2 11.0 fusion.47
  326.2 5.6 multiply_reduce_fusion.2
  331.8 42.1 %all-gather.20.cloned.1.call-done = bf16[3072,768]{1,0:T(8,128)(2,1)} async-done(((bf16[96,768]{1,0:T(8,128)(2,1)}), bf16[3072,768]{1,0:T(8,128)(2,1)}) %all-gather.20.cloned.1.call-update) | async-done | bytes 4718608 | tf_op jit(solution)/shard_map/all_gather | solution.py:360
  373.9 17.0 %multiply_reduce_fusion = (f32[3072]{0:T(1024)}, f32[1024]{0:T(1024)S(1)}, f32[1024]{0:T(1024)S(1)}, f32[1024,3072]{1,0:T(8,128)}) fusion(f32[1024]{0:T(1024)S(1)} %add_rsqrt_fusion, f32[1024]{0:T(1024)S(1)} %broadcast_multiply_fusion.2, f32[1024,3072]{1,0:T(8,128)} %copy-done.8, f32[3072]{0:T(1024)S(1)} %convert_element_type.144, ...), kind=kOutput, calls=%fused_computation.11 | convolution fusion | flops 4882164736 | bytes 31498240 | tf_op jit(solution)/shard_map/dot_general | solution.py:28
  390.9 17.8 %fusion.6 = (bf16[1024,3072]{1,0:T(8,128)(2,1)S(1)}, bf16[1024,3072]{1,0:T(8,128)(2,1)}) fusion(f32[1024,3072]{1,0:T(8,128)} %copy-done.8, f32[1024,3072]{1,0:T(8,128)} %get-tuple-element.205, f32[1024]{0:T(1024)S(1)} %broadcast_multiply_fusion, f32[1024]{0:T(1024)S(1)} %broadcast_multiply_fusion.1, f32[3072]{0:T(1024)S(1)} %convert_element_type.144, ...), kind=kLoop, calls=%fused_computation.10 | loop fusion | flops 94371840 | bytes 37777408 | tf_op jit(solution)/shard_map/convert_element_type | solution.py:483
  408.7 10.0 multiply_reduce_fusion.5
  420.0 2.3 multiply_reduce_fusion.15
  422.4 3.2 multiply_reduce_fusion.4
  425.5 79.3 %attend_back.1 = (bf16[1024,2304]{1,0:T(8,128)(2,1)}, f32[12,5,256]{2,1,0:T(8,128)}) custom-call(s32[2,8]{1,0:T(2,128)} %copy-done.4, bf16[1024,2304]{1,0:T(8,128)(2,1)} %convolution_convert_fusion.packed, bf16[1024,768]{1,0:T(8,128)(2,1)} %get-tuple-element.171.grads, f32[1024,768]{1,0:T(8,128)} %copy-done, s32[1024,1]{1,0:T(8,128)} %copy.124.segk, ...), custom_call_target="tpu_custom_call" | custom-call | flops 49999998976 | bytes 20000000 | tf_op jit(solution)/shard_map/attend_back/pallas_call | solution.py:298
  504.9 6.6 copy.130
  511.5 4.9 all-to-all-start
  517.2 5.8 copy.155
  522.9 81.1 %all-to-all-done = bf16[1024,4,576]{0,2,1:T(8,128)(2,1)} async-done(((bf16[1024,4,576]{0,2,1:T(8,128)(2,1)}), bf16[1024,4,576]{0,2,1:T(8,128)(2,1)}, u32[]{:S(2)}, u32[]{:S(2)}) %all-to-all-start) | async-done | bytes 4718624 | tf_op jit(solution)/shard_map/all_to_all | solution.py:505
  604.0 5.4 all-to-all-start.2
  609.4 5.8 copy.156
  615.5 64.6 %all-to-all-done.2 = bf16[1024,4,768]{2,0,1:T(8,128)(2,1)} async-done(((bf16[1024,4,768]{2,0,1:T(8,128)(2,1)}), bf16[1024,4,768]{2,0,1:T(8,128)(2,1)}, u32[]{:S(2)}, u32[]{:S(2)}) %all-to-all-start.2) | async-done | bytes 6291488 | tf_op jit(solution)/shard_map/all_to_all | solution.py:486
  680.1 5.5 all-to-all-start.1
  686.1 9.8 multiply_reduce_fusion.7
  696.0 5.3 copy.151
  701.3 9.4 convolution_convert_fusion.3
  711.0 9.9 convolution_convert_fusion.1
  721.8 34.5 %all-to-all-done.1 = bf16[1024,4,768]{2,0,1:T(8,128)(2,1)} async-done(((bf16[1024,4,768]{2,0,1:T(8,128)(2,1)}), bf16[1024,4,768]{2,0,1:T(8,128)(2,1)}, u32[]{:S(2)}, u32[]{:S(2)}) %all-to-all-start.1) | async-done | bytes 6291488 | tf_op jit(solution)/shard_map/all_to_all | solution.py:485
  756.3 9.8 convolution_convert_fusion.2
  766.4 5.4 multiply_add_fusion
  771.8 2.2 copy.129
  774.7 9.1 gather_fusion
  783.8 7.9 multiply_reduce_fusion.18
  791.7 39.8 %all-reduce.26 = (f32[1024]{0:T(1024)}, f32[1024]{0:T(1024)}, f32[768]{0:T(1024)}, f32[768]{0:T(1024)}, f32[768]{0:T(1024)}, /*index=5*/f32[3072]{0:T(1024)}, f3...) all-reduce(f32[1024]{0:T(1024)} %get-tuple-element.134, ...), channel_id=1, replica_groups=mesh['wide'=8,'narrow'=4] {'wide','narrow'}, use_global_device_ids=true, to_apply=%region_26.27 | all-reduce | flops 12556 | bytes 100448 | tf_op jit(solution)/shard_map/psum | solution.py:534
  832.9 2.3 multiply_convert_fusion.5
  836.2 1.6 fusion.45
  838.2 2.2 fusion.30
  845.4 4.4 fusion.55
  849.9 5.2 fusion.13
  855.1 4.6 fusion.56
  859.8 3.7 copy.140
  870.6 9.5 add_convert_fusion
  880.1 2.7 copy.139
  884.1 3.0 convolution_add_fusion.1
  887.1 1.6 convert_element_type.157
  888.7 1.6 convert_element_type.161
  890.3 17.0 %reduce-scatter.16.cloned.1.call-done = bf16[96,768]{1,0:T(8,128)(2,1)} async-done(((bf16[768,768]{1,0:T(8,128)(2,1)}), bf16[96,768]{1,0:T(8,128)(2,1)}) %reduce-scatter.16.cloned.1.call-update) | async-done | bytes 147472 | tf_op jit(solution)/shard_map/reduce_scatter | solution.py:511
  907.3 1.6 convert_element_type.159
  909.0 135.0 %reduce-scatter.22.cloned.1.call-done = f32[8,1024]{1,0:T(8,128)} async-done(((f32[256,1024]{1,0:T(8,128)}), f32[8,1024]{1,0:T(8,128)}) %reduce-scatter.22.cloned.1.call-update) | async-done | bytes 32784 | tf_op jit(solution)/shard_map/reduce_scatter | solution.py:561
  1044.0 133.4 %reduce-scatter.26.cloned.1.call-done = f32[32,256]{1,0:T(8,128)} async-done(((f32[1024,256]{1,0:T(8,128)}), f32[32,256]{1,0:T(8,128)}) %reduce-scatter.26.cloned.1.call-update) | async-done | bytes 32784
  1177.3 101.5 %reduce-scatter.20.cloned.1.call-done = f32[72,256]{1,0:T(8,128)} async-done(((f32[2304,256]{1,0:T(8,128)}), f32[72,256]{1,0:T(8,128)}) %reduce-scatter.20.cloned.1.call-update) | async-done | bytes 73744 | tf_op jit(solution)/shard_map/reduce_scatter | solution.py:560
  1278.9 103.7 %reduce-scatter.14.cloned.1.call-done = f32[24,768]{1,0:T(8,128)} async-done(((f32[768,768]{1,0:T(8,128)}), f32[24,768]{1,0:T(8,128)}) %reduce-scatter.14.cloned.1.call-update) | async-done | bytes 73744 | tf_op jit(solution)/shard_map/reduce_scatter | solution.py:553
  1382.6 107.4 %reduce-scatter.24.cloned.1.call-done = f32[32,768]{1,0:T(8,128)} async-done(((f32[1024,768]{1,0:T(8,128)}), f32[32,768]{1,0:T(8,128)}) %reduce-scatter.24.cloned.1.call-update) | async-done | bytes 98320 | tf_op jit(solution)/shard_map/reduce_scatter | solution.py:562
  (271 shorter events, 44.6 us)
Async XLA Ops:
  7.2 53.1 %copy-start.48 = (s32[1,576]{1,0:T(1,128)S(1)}, s32[1,576]{1,0:T(1,128)}, u32[]{:S(2)}) copy-start(s32[1,576]{1,0:T(1,128)} %param.24) | copy-start | bytes 6916
  7.2 53.8 %copy-start.45 = (bf16[32,256]{1,0:T(8,128)(2,1)S(1)}, bf16[32,256]{1,0:T(8,128)(2,1)}, u32[]{:S(2)}) copy-start(bf16[32,256]{1,0:T(8,128)(2,1)} %param.35) | copy-start | bytes 49156
  7.2 140.1 %all-gather.10.cloned.1.call-start = ((), (), s32[]{:S(2)}) async-start(), calls=%async_computation.11 | async-start | bytes 1216512 | tf_op jit(solution)/shard_map/all_gather | solution.py:367
  7.9 187.0 %all-gather.12.cloned.1.call-start = ((), (), s32[]{:S(2)}) async-start(), calls=%async_computation.12 | async-start | bytes 1622016 | tf_op jit(solution)/shard_map/all_gather | solution.py:369
  8.7 253.9 %all-gather.14.cloned.1.call-start = ((), (), s32[]{:S(2)}) async-start(), calls=%async_computation.13 | async-start | bytes 3649536 | tf_op jit(solution)/shard_map/all_gather | solution.py:357
  9.4 298.2 %all-gather.16.cloned.1.call-start = ((), (), s32[]{:S(2)}) async-start(), calls=%async_computation.14 | async-start | bytes 1216512 | tf_op jit(solution)/shard_map/all_gather | solution.py:358
  10.0 305.2 %all-gather.18.cloned.1.call-start = ((), (), s32[]{:S(2)}) async-start(), calls=%async_computation.15 | async-start | bytes 4866048 | tf_op jit(solution)/shard_map/all_gather | solution.py:359
  10.6 363.3 %all-gather.20.cloned.1.call-start = ((), (), s32[]{:S(2)}) async-start(), calls=%async_computation.16 | async-start | bytes 4866048 | tf_op jit(solution)/shard_map/all_gather | solution.py:360
  11.2 690.1 %all-gather.22.cloned.1.call-start = ((), (), s32[]{:S(2)}) async-start(), calls=%async_computation.17 | async-start | bytes 7864320 | tf_op jit(solution)/shard_map/all_gather | solution.py:440
  58.5 44.2 %copy-start.21 = (bf16[1,24,24,1024]{3,2,1,0:T(8,128)(2,1)S(1)}, bf16[1,24,24,1024]{3,2,1,0:T(8,128)(2,1)}, u32[]{:S(2)}) copy-start(bf16[1,24,24,1024]{3,2,1,0:T(8,128)(2,1)} %param.22) | copy-start | bytes 3538948
  58.5 131.5 %copy-start.36 = (f32[1024]{0:T(1024)}, f32[1024]{0:T(1024)S(1)}, u32[]{:S(2)}) copy-start(f32[1024]{0:T(1024)S(1)} %convert_element_type.130) | copy-start | bytes 12292
  58.6 131.5 %copy-start.44 = (f32[1024]{0:T(1024)}, f32[1024]{0:T(1024)S(1)}, u32[]{:S(2)}) copy-start(f32[1024]{0:T(1024)S(1)} %convert_element_type.131) | copy-start | bytes 12292
  60.3 153.2 %copy-start.39 = (f32[768]{0:T(1024)}, f32[768]{0:T(1024)S(1)}, u32[]{:S(2)}) copy-start(f32[768]{0:T(1024)S(1)} %convert_element_type.136) | copy-start | bytes 9220
  104.4 1.8 copy-start.46
  104.7 1.5 copy-start.43
  147.3 3.0 copy-start.31
  150.3 2.0 copy-start.51
  211.1 2.8 copy-start.6
  211.1 2.4 copy-start.34
  214.0 1.5 copy-start.41
  214.0 2.3 copy-start.49
  214.0 44.1 %copy-start.3 = (s32[1,1024]{1,0:T(1,128)S(1)}, s32[1,1024]{1,0:T(1,128)}, u32[]{:S(2)}) copy-start(s32[1,1024]{1,0:T(1,128)} %segq.3) | copy-start | bytes 12292
  214.0 44.3 %copy-start.17 = (bf16[1024,768]{1,0:T(8,128)(2,1)S(1)}, bf16[1024,768]{1,0:T(8,128)(2,1)}, u32[]{:S(2)}) copy-start(bf16[1024,768]{1,0:T(8,128)(2,1)} %param.41) | copy-start | bytes 4718596
  215.5 46.4 %copy-start.50 = (f32[12]{0:T(128)S(1)}, f32[12]{0:T(128)}, u32[]{:S(2)}) copy-start(f32[12]{0:T(128)} %param.34) | copy-start | bytes 148
  215.5 47.1 %copy-start.19 = (bf16[1024,768]{0,1:T(8,128)(2,1)S(1)}, bf16[1024,768]{0,1:T(8,128)(2,1)}, u32[]{:S(2)}) copy-start(bf16[1024,768]{0,1:T(8,128)(2,1)} %multiply_convert_fusion.4) | copy-start | bytes 4718596
  215.6 495.5 %all-gather.26.cloned.1.call-start = ((), (), s32[]{:S(2)}) async-start(), calls=%async_computation.22 | async-start | bytes 7864320 | tf_op jit(solution)/shard_map/all_gather | solution.py:442
  262.3 8.0 copy-start.4
  262.6 7.7 copy-start.2
  306.7 115.7 %copy-start = (f32[1024,768]{1,0:T(8,128)}, f32[1024,768]{1,0:T(8,128)S(1)}, u32[]{:S(2)}) copy-start(f32[1024,768]{1,0:T(8,128)S(1)} %get-tuple-element.24.attended) | copy-start | bytes 9437188
  312.0 1.6 copy-start.9
  326.1 5.6 copy-start.8
  390.9 17.8 %copy-start.10 = (f32[1024,768]{0,1:T(8,128)S(1)}, f32[1024,768]{0,1:T(8,128)}, u32[]{:S(2)}) copy-start(f32[1024,768]{0,1:T(8,128)} %copy-done.9) | copy-start | bytes 9437188
  408.7 10.1 copy-start.13
  408.7 10.1 copy-start.18
  420.0 2.3 copy-start.12
  511.5 92.5 %all-to-all-start = ((bf16[1024,4,576]{0,2,1:T(8,128)(2,1)}), bf16[1024,4,576]{0,2,1:T(8,128)(2,1)}, u32[]{:S(2)}, u32[]{:S(2)}) async-start(bf16[1024,4,576]{0,2,1:T(8,128)(2,1)} %bitcast.139), calls=%async_computation | async-start | bytes 9437184 | tf_op jit(solution)/shard_map/all_to_all | solution.py:505
  516.4 239.9 %all-gather.24.cloned.1.call-start = ((), (), s32[]{:S(2)}) async-start(), calls=%async_computation.20 | async-start | bytes 7864320 | tf_op jit(solution)/shard_map/all_gather | solution.py:441
  604.0 76.1 %all-to-all-start.2 = ((bf16[1024,4,768]{2,0,1:T(8,128)(2,1)}), bf16[1024,4,768]{2,0,1:T(8,128)(2,1)}, u32[]{:S(2)}, u32[]{:S(2)}) async-start(bf16[1024,4,768]{2,0,1:T(8,128)(2,1)} %bitcast.138), calls=%async_computation.5 | async-start | bytes 12582912 | tf_op jit(solution)/shard_map/all_to_all | solution.py:486
  609.4 5.8 copy-start.33
  680.1 6.0 copy-start.7
  680.1 6.0 copy-start.35
  680.1 6.0 copy-start.40
  680.1 6.0 copy-start.42
  680.1 76.2 %all-to-all-start.1 = ((bf16[1024,4,768]{2,0,1:T(8,128)(2,1)}), bf16[1024,4,768]{2,0,1:T(8,128)(2,1)}, u32[]{:S(2)}, u32[]{:S(2)}) async-start(bf16[1024,4,768]{2,0,1:T(8,128)(2,1)} %bitcast.136), calls=%async_computation.3 | async-start | bytes 12582912 | tf_op jit(solution)/shard_map/all_to_all | solution.py:485
  685.6 201.4 %reduce-scatter.12.cloned.1.call-start = ((), (), s32[]{:S(2)}) async-start(), calls=%async_computation.18 | async-start | bytes 1105920 | tf_op jit(solution)/shard_map/reduce_scatter | solution.py:508
  710.7 178.0 %reduce-scatter.18.cloned.1.call-start = ((), (), s32[]{:S(2)}) async-start(), calls=%async_computation.23 | async-start | bytes 1327104 | tf_op jit(solution)/shard_map/reduce_scatter | solution.py:514
  720.9 186.4 %reduce-scatter.16.cloned.1.call-start = ((), (), s32[]{:S(2)}) async-start(), calls=%async_computation.21 | async-start | bytes 1327104 | tf_op jit(solution)/shard_map/reduce_scatter | solution.py:511
  766.1 277.9 %reduce-scatter.22.cloned.1.call-start = ((), (), s32[]{:S(2)}) async-start(), calls=%async_computation.25 | async-start | bytes 1081344 | tf_op jit(solution)/shard_map/reduce_scatter | solution.py:561
  771.8 2.9 copy-start.14
  774.7 9.1 copy-start.22
  783.8 49.2 %copy-start.15 = (f32[576,1024]{1,0:T(8,128)S(1)}, f32[576,1024]{1,0:T(8,128)}, u32[]{:S(2)}) copy-start(f32[576,1024]{1,0:T(8,128)} %get-tuple-element.200) | copy-start | bytes 7077892
  831.5 4.8 copy-start.52
  836.2 2.0 copy-start.32
  837.9 2.5 copy-start.27
  837.9 339.4 %reduce-scatter.26.cloned.1.call-start = ((), (), s32[]{:S(2)}) async-start(), calls=%async_computation.27 | async-start | bytes 1081344
  843.3 1.9 copy-start.23
  845.3 4.6 copy-start.1
  845.3 433.6 %reduce-scatter.20.cloned.1.call-start = ((), (), s32[]{:S(2)}) async-start(), calls=%async_computation.24 | async-start | bytes 2433024 | tf_op jit(solution)/shard_map/reduce_scatter | solution.py:560
  849.8 532.8 %reduce-scatter.14.cloned.1.call-start = ((), (), s32[]{:S(2)}) async-start(), calls=%async_computation.19 | async-start | bytes 2433024 | tf_op jit(solution)/shard_map/reduce_scatter | solution.py:553
  855.1 634.9 %reduce-scatter.24.cloned.1.call-start = ((), (), s32[]{:S(2)}) async-start(), calls=%async_computation.26 | async-start | bytes 3244032 | tf_op jit(solution)/shard_map/reduce_scatter | solution.py:562
  859.8 3.7 copy-start.47
  859.8 10.7 copy-start.11
  880.1 4.0 copy-start.16
  880.1 4.0 copy-start.24
  (9 other events, 9.1 us)
Sparse Core Ops, SparseCore 0:
  11.0 56.8 all-gather.9
  70.7 54.6 all-gather.11
  128.3 59.3 all-gather.13
  190.4 52.8 all-gather.15
  246.1 62.6 all-gather.17
  311.5 62.3 all-gather.19
  376.1 45.1 all-gather.21
  422.8 46.3 all-gather.25
  518.8 79.7 all-gather.23
  710.8 62.8 reduce-scatter.11
  777.5 63.0 reduce-scatter.17
  844.2 63.0 reduce-scatter.15
  910.2 133.7 reduce-scatter.21
  1046.6 130.6 reduce-scatter.25
  1183.9 94.9 reduce-scatter.19
  1284.6 97.9 reduce-scatter.13
  1389.3 100.5 reduce-scatter.23
where the time goes:
time: 1510 us; the launch traced here: 1500 us
  waiting for transfers between devices  825 us (55%)
  blocking collectives  244 us (16%)
  matrix products  142 us (9%)
  Pallas kernels  116 us (8%)
  local copies, waits for them, and re-layouts  70.4 us (5%)
  other arithmetic  67.3 us (4%)
  starting transfers between devices  17 us (1%)
  between operations  15.3 us (1%)
    unnamed x18, waiting for transfers between devices  139 us
    reduce_scatter x1, waiting for transfers between devices, local(): lax.psum_scatter(grad_w_expand, ('wide', 'narrow'), scatter_dimension=0,...  135 us
    reduce_scatter x1, waiting for transfers between devices, local(): lax.psum_scatter(grad_w_embed, ('wide', 'narrow'), scatter_dimension=0, t...  107 us
    reduce_scatter x1, waiting for transfers between devices, local(): lax.psum_scatter(grad_w_out, ('wide', 'narrow'), scatter_dimension=0, til...  104 us
    reduce_scatter x1, waiting for transfers between devices, local(): lax.psum_scatter(grad_w_spatial, ('wide', 'narrow'), scatter_dimension=0,...  102 us
    all_to_all x1, waiting for transfers between devices, local(): lax.all_to_all(grad_packed, 'narrow', split_axis=1, concat_axis=0, tiled=...  81.1 us
    pallas_call x1, Pallas kernels, attend_back(): pl.pallas_call(attend_back_kernel, out_shape=(jax.ShapeDtypeStruct((lengt...  79.3 us
    all_to_all x1, waiting for transfers between devices, local(): lax.all_to_all(narrowed_low, 'narrow', split_axis=1, concat_axis=0, tiled...  64.6 us
  transfers between devices with their start and end apart: 20, of which 10 were waited for; matrix products, arithmetic and copies ran while one was open for 18% of the time, Pallas kernels for 8%

commit v1 on v0

--- a/solution.py
+++ b/solution.py
@@ -1,3 +1,5 @@
+import functools
+
 import jax
 import jax.numpy as jnp
 from jax import lax
@@ -330,6 +332,363 @@
     )(win, packed, grads, attended, seg.reshape(length, 1), seg, bias, logsum)
 
 
+MESH = pl.DeviceIdType.MESH
+
+
+class Place:
+    def __init__(self, lines, rows):
+        self.lines, self.rows = lines, rows
+        wide, narrow = lax.axis_index("wide"), lax.axis_index("narrow")
+        self.line, self.side = wide // 2, wide % 2
+        self.row, self.core = narrow // 2, narrow % 2
+
+    def device(self, line=None, side=None, row=None, core=None):
+        line = self.line if line is None else line
+        side = self.side if side is None else side
+        row = self.row if row is None else row
+        core = self.core if core is None else core
+        return (line * 2 + side, row * 2 + core)
+
+    def line_peer(self, k):
+        return lax.rem(self.line + k, self.lines)
+
+    def line_source(self, k):
+        return lax.rem(self.line + self.lines - k, self.lines)
+
+    def row_peer(self, k):
+        return lax.rem(self.row + k, self.rows)
+
+    def row_source(self, k):
+        return lax.rem(self.row + self.rows - k, self.rows)
+
+    def greet(self):
+        barrier = pltpu.get_barrier_semaphore()
+        targets = [self.device(line=self.line_peer(k)) for k in range(1, self.lines)]
+        targets += [self.device(row=self.row_peer(k)) for k in range(1, self.rows)]
+        targets += [self.device(side=1 - self.side), self.device(core=1 - self.core)]
+        for target in targets:
+            pl.semaphore_signal(barrier, inc=1, device_id=target, device_id_type=MESH)
+        pl.semaphore_wait(barrier, len(targets))
+
+
+class Sends:
+    def __init__(self, send_sems, recv_sems):
+        self.send_sems, self.recv_sems, self.used = send_sems, recv_sems, 0
+        self.started = []
+
+    def start(self, src, dst, device):
+        copy = pltpu.make_async_remote_copy(
+            src_ref=src, dst_ref=dst, send_sem=self.send_sems.at[self.used], recv_sem=self.recv_sems.at[self.used],
+            device_id=device, device_id_type=MESH)
+        copy.start()
+        self.used += 1
+        self.started.append(copy)
+        return copy
+
+    def finish(self):
+        for copy in self.started:
+            copy.wait_send()
+
+
+def gather_copies(lines, rows):
+    return (lines - 1) + 1 + (rows - 1) + (rows - 1) + 1 + 1 + rows + rows
+
+
+class Gather:
+    def __init__(self, place, sends, shard, out, local_sem):
+        self.p, self.s, self.shard, self.out = place, sends, shard, out
+        self.local_sem = local_sem
+        cols = out.shape[-1]
+        cut = cols // 256 * 128
+        self.low, self.high = pl.ds(0, cut), pl.ds(cut, cols - cut)
+        self.cores = []
+
+    def begin(self):
+        p = self.p
+        mine = self.out.at[p.line, p.side, p.row, p.core]
+        self.local = pltpu.make_async_copy(self.shard, mine, self.local_sem)
+        self.local.start()
+        self.stage = [self.s.start(self.shard, mine, p.device(line=p.line_peer(k))) for k in range(1, p.lines)]
+
+    def across(self, src):
+        self.cores.append(self.s.start(src, src, self.p.device(core=1 - self.p.core)))
+
+    def second(self):
+        p, out = self.p, self.out
+        self.local.wait()
+        for copy in self.stage:
+            copy.wait_recv()
+        low = out.at[:, p.side, p.row, p.core, :, self.low]
+        high = out.at[:, p.side, p.row, p.core, :, self.high]
+        self.stage = [self.s.start(low, low, p.device(side=1 - p.side))]
+        self.stage += [self.s.start(high, high, p.device(row=p.row_peer(k))) for k in range(1, p.rows)]
+        self.across(out.at[:, p.side, p.row, p.core])
+
+    def third(self):
+        p, out = self.p, self.out
+        for copy in self.stage:
+            copy.wait_recv()
+        low = out.at[:, :, p.row, p.core, :, self.low]
+        high = out.at[:, p.side, :, p.core, :, self.high]
+        self.stage = [self.s.start(high, high, p.device(side=1 - p.side))]
+        self.stage += [self.s.start(low, low, p.device(row=p.row_peer(k))) for k in range(1, p.rows)]
+        self.across(out.at[:, 1 - p.side, p.row, p.core, :, self.low])
+        for k in range(1, p.rows):
+            self.across(out.at[:, p.side, p.row_source(k), p.core, :, self.high])
+
+    def fourth(self):
+        p, out = self.p, self.out
+        for copy in self.stage:
+            copy.wait_recv()
+        for k in range(1, p.rows):
+            self.across(out.at[:, :, p.row_source(k), p.core, :, self.low])
+        self.across(out.at[:, 1 - p.side, :, p.core, :, self.high])
+
+    def last(self):
+        for copy in self.cores:
+            copy.wait_recv()
+
+
+def gather_kernel(count, lines, rows, *refs):
+    shards, outs = refs[:count], refs[count : 2 * count]
+    send_sems, recv_sems, local_sems = refs[2 * count :]
+    place = Place(lines, rows)
+    place.greet()
+    sends = Sends(send_sems, recv_sems)
+    parts = [Gather(place, sends, shards[i], outs[i], local_sems.at[i]) for i in range(count)]
+    for part in parts:
+        part.begin()
+    for i in range(count + 3):
+        for lag, step in ((0, "second"), (1, "third"), (2, "fourth"), (3, "last")):
+            if 0 <= i - lag < count:
+                getattr(parts[i - lag], step)()
+    sends.finish()
+
+
+def gather_all(shards, collective_id):
+    wide, narrow = lax.axis_size("wide"), lax.axis_size("narrow")
+    lines, rows = wide // 2, narrow // 2
+    count = len(shards)
+    copies = count * gather_copies(lines, rows)
+    outs = pl.pallas_call(
+        functools.partial(gather_kernel, count, lines, rows),
+        out_shape=[jax.ShapeDtypeStruct((lines, 2, rows, 2) + s.shape, s.dtype) for s in shards],
+        in_specs=[pl.BlockSpec(memory_space=pl.ANY)] * count,
+        out_specs=[pl.BlockSpec(memory_space=pl.ANY)] * count,
+        scratch_shapes=[pltpu.SemaphoreType.DMA((copies,)), pltpu.SemaphoreType.DMA((copies,)), pltpu.SemaphoreType.DMA((count,))],
+        compiler_params=pltpu.CompilerParams(collective_id=collective_id, has_side_effects=True),
+        cost_estimate=pl.CostEstimate(flops=0, bytes_accessed=4 * 10**7, transcendentals=0),
+        name="gather_weights",
+    )(*shards)
+    return outs
+
+
+def scatter_copies(lines, rows):
+    return 1 + (rows - 1) + 1 + 1 + (rows - 1) + (lines - 1)
+
+
+def add_loop(lead, fn):
+    total = 1
+    for size in lead:
+        total *= size
+
+    def body(i, carry):
+        index = []
+        for size in reversed(lead):
+            index.append(lax.rem(i, size))
+            i = i // size
+        fn(tuple(reversed(index)))
+        return carry
+
+    lax.fori_loop(0, total, body, 0)
+
+
+def plus(*terms):
+    total = terms[0].astype(jnp.float32)
+    for term in terms[1:]:
+        total = total + term.astype(jnp.float32)
+    return total
+
+
+class Scatter:
+    def __init__(self, place, sends, grad, out, buffers, local_sem):
+        self.p, self.s, self.grad, self.out, self.local_sem = place, sends, grad, out, local_sem
+        self.own, self.other, self.low1, self.high1, self.low2, self.high2, self.line0, self.lines_in = buffers
+        cols = grad.shape[-1]
+        cut = cols // 256 * 128
+        self.low, self.high = pl.ds(0, cut), pl.ds(cut, cols - cut)
+
+    def begin(self):
+        p = self.p
+        self.local = pltpu.make_async_copy(self.grad.at[:, :, :, p.core], self.own, self.local_sem)
+        self.local.start()
+        self.stage = [self.s.start(self.grad.at[:, :, :, 1 - p.core], self.other, p.device(core=1 - p.core))]
+
+    def second(self):
+        p, own = self.p, self.own
+        self.local.wait()
+        for copy in self.stage:
+            copy.wait_recv()
+
+        def add(i):
+            own[i] = plus(own[i], self.other[i]).astype(own.dtype)
+
+        add_loop(own.shape[:3], add)
+        self.stage = [self.s.start(own.at[:, 1 - p.side, :, :, self.high], self.high1, p.device(side=1 - p.side))]
+        for k in range(1, p.rows):
+            to = p.row_peer(k)
+            self.stage.append(self.s.start(own.at[:, :, to, :, self.low], self.low1.at[k - 1], p.device(row=to)))
+
+    def third(self):
+        p, own = self.p, self.own
+        for copy in self.stage:
+            copy.wait_recv()
+
+        def add_low(i):
+            l, x = i
+            terms = [own[l, x, p.row, :, self.low]] + [self.low1[k, l, x] for k in range(p.rows - 1)]
+            own[l, x, p.row, :, self.low] = plus(*terms).astype(own.dtype)
+
+        def add_high(i):
+            l, y = i
+            own[l, p.side, y, :, self.high] = plus(own[l, p.side, y, :, self.high], self.high1[l, y]).astype(own.dtype)
+
+        add_loop((p.lines, 2), add_low)
+        add_loop((p.lines, p.rows), add_high)
+        self.stage = [self.s.start(own.at[:, 1 - p.side, p.row, :, self.low], self.low2, p.device(side=1 - p.side))]
+        for k in range(1, p.rows):
+            to = p.row_peer(k)
+            self.stage.append(self.s.start(own.at[:, p.side, to, :, self.high], self.high2.at[k - 1], p.device(row=to)))
+
+    def fourth(self):
+        p, own = self.p, self.own
+        for copy in self.stage:
+            copy.wait_recv()
+
+        def add(i):
+            (l,) = i
+            self.line0[l, :, self.low] = plus(own[l, p.side, p.row, :, self.low], self.low2[l]).astype(own.dtype)
+            terms = [own[l, p.side, p.row, :, self.high]] + [self.high2[k, l] for k in range(p.rows - 1)]
+            self.line0[l, :, self.high] = plus(*terms).astype(own.dtype)
+
+        add_loop((p.lines,), add)
+        self.stage = []
+        for k in range(1, p.lines):
+            to = p.line_peer(k)
+            self.stage.append(self.s.start(self.line0.at[to], self.lines_in.at[k - 1], p.device(line=to)))
+
+    def last(self):
+        p = self.p
+        for copy in self.stage:
+            copy.wait_recv()
+        self.out[...] = plus(self.line0[p.line], *[self.lines_in[k] for k in range(p.lines - 1)])
+
+
+def scatter_buffers(lines, rows, r, c, dtype):
+    low = c // 256 * 128
+    high = c - low
+    return [
+        pltpu.VMEM((lines, 2, rows, r, c), dtype),
+        pltpu.VMEM((lines, 2, rows, r, c), dtype),
+        pltpu.VMEM((max(rows - 1, 1), lines, 2, r, low), dtype),
+        pltpu.VMEM((lines, rows, r, high), dtype),
+        pltpu.VMEM((lines, r, low), dtype),
+        pltpu.VMEM((max(rows - 1, 1), lines, r, high), dtype),
+        pltpu.VMEM((lines, r, c), dtype),
+        pltpu.VMEM((max(lines - 1, 1), r, c), dtype),
+    ]
+
+
+def scatter_kernel(count, lines, rows, *refs):
+    grads, outs = refs[:count], refs[count : 2 * count]
+    buffers = refs[2 * count : 2 * count + 8 * count]
+    send_sems, recv_sems, local_sems = refs[10 * count :]
+    place = Place(lines, rows)
+    place.greet()
+    sends = Sends(send_sems, recv_sems)
+    parts = [Scatter(place, sends, grads[i], outs[i], buffers[8 * i : 8 * i + 8], local_sems.at[i]) for i in range(count)]
+    for part in parts:
+        part.begin()
+    for i in range(count + 3):
+        for lag, step in ((0, "second"), (1, "third"), (2, "fourth"), (3, "last")):
+            if 0 <= i - lag < count:
+                getattr(parts[i - lag], step)()
+    sends.finish()
+
+
+def scatter_all(grads, collective_id):
+    wide, narrow = lax.axis_size("wide"), lax.axis_size("narrow")
+    lines, rows = wide // 2, narrow // 2
+    count = len(grads)
+    copies = count * scatter_copies(lines, rows)
+    buffers = []
+    for g in grads:
+        buffers += scatter_buffers(lines, rows, g.shape[-2], g.shape[-1], g.dtype)
+    return pl.pallas_call(
+        functools.partial(scatter_kernel, count, lines, rows),
+        out_shape=[jax.ShapeDtypeStruct(g.shape[-2:], jnp.float32) for g in grads],
+        in_specs=[pl.BlockSpec(memory_space=pl.ANY)] * count,
+        out_specs=[pl.BlockSpec(memory_space=pltpu.VMEM)] * count,
+        scratch_shapes=buffers + [pltpu.SemaphoreType.DMA((copies,)), pltpu.SemaphoreType.DMA((copies,)), pltpu.SemaphoreType.DMA((count,))],
+        compiler_params=pltpu.CompilerParams(collective_id=collective_id, has_side_effects=True, vmem_limit_bytes=60 * 2**20),
+        cost_estimate=pl.CostEstimate(flops=0, bytes_accessed=4 * 10**7, transcendentals=0),
+        name="scatter_grads",
+    )(*grads)
+
+
+def total_kernel(lines, rows, x_ref, o_ref, core_in, plane, line_in, send_sems, recv_sems):
+    p = Place(lines, rows)
+    barrier = pltpu.get_barrier_semaphore()
+    plane_peers = [(k // rows, k % rows) for k in range(1, 2 * rows)]
+    targets = [p.device(core=1 - p.core)]
+    targets += [p.device(side=lax.rem(p.side + a, 2), row=p.row_peer(b)) for a, b in plane_peers]
+    targets += [p.device(line=p.line_peer(k)) for k in range(1, lines)]
+    for target in targets:
+        pl.semaphore_signal(barrier, inc=1, device_id=target, device_id_type=MESH)
+    pl.semaphore_wait(barrier, len(targets))
+    sends = Sends(send_sems, recv_sems)
+    sends.start(x_ref, core_in, targets[0]).wait_recv()
+    here = p.side * rows + p.row
+    plane[here] = x_ref[...] + core_in[...]
+    stage = [sends.start(plane.at[here], plane.at[here], t) for t in targets[1 : 2 * rows]]
+    for copy in stage:
+        copy.wait_recv()
+    total = plane[0]
+    for k in range(1, 2 * rows):
+        total = total + plane[k]
+    line_in[p.line] = total
+    stage = [sends.start(line_in.at[p.line], line_in.at[p.line], t) for t in targets[2 * rows :]]
+    for copy in stage:
+        copy.wait_recv()
+    total = line_in[0]
+    for k in range(1, lines):
+        total = total + line_in[k]
+    o_ref[...] = total
+    sends.finish()
+
+
+def total_sum(x, collective_id):
+    wide, narrow = lax.axis_size("wide"), lax.axis_size("narrow")
+    lines, rows = wide // 2, narrow // 2
+    copies = 1 + 2 * rows - 1 + lines - 1
+    return pl.pallas_call(
+        functools.partial(total_kernel, lines, rows),
+        out_shape=jax.ShapeDtypeStruct(x.shape, x.dtype),
+        in_specs=[pl.BlockSpec(memory_space=pltpu.VMEM)],
+        out_specs=pl.BlockSpec(memory_space=pltpu.VMEM),
+        scratch_shapes=[
+            pltpu.VMEM(x.shape, x.dtype),
+            pltpu.VMEM((2 * rows,) + x.shape, x.dtype),
+            pltpu.VMEM((lines,) + x.shape, x.dtype),
+            pltpu.SemaphoreType.DMA((copies,)),
+            pltpu.SemaphoreType.DMA((copies,)),
+        ],
+        compiler_params=pltpu.CompilerParams(collective_id=collective_id, has_side_effects=True),
+        cost_estimate=pl.CostEstimate(flops=0, bytes_accessed=10**6, transcendentals=0),
+        name="total_sum",
+    )(x)
+
+
 def local(
     tokens,
     features,
@@ -353,40 +712,25 @@
     bn_shift,
     d_out,
 ):
-    gathered = (
-        lax.all_gather(w_qkv, ("wide", "narrow"), axis=0, tiled=True),
-        lax.all_gather(w_out, ("wide", "narrow"), axis=0, tiled=True),
-        lax.all_gather(w_up, ("wide", "narrow"), axis=0, tiled=True),
-        lax.all_gather(w_down, ("wide", "narrow"), axis=0, tiled=True),
-        lax.all_gather(gain_pre, ("wide", "narrow"), axis=0, tiled=True),
-        lax.all_gather(gain_attn, ("wide", "narrow"), axis=0, tiled=True),
-        lax.all_gather(gain_mid, ("wide", "narrow"), axis=0, tiled=True),
-        lax.all_gather(gain_ffn, ("wide", "narrow"), axis=0, tiled=True),
-        lax.all_gather(rel_table, ("wide", "narrow"), axis=1, tiled=True),
-        lax.all_gather(w_reduce, ("wide", "narrow"), axis=0, tiled=True),
-        lax.all_gather(w_spatial, ("wide", "narrow"), axis=0, tiled=True),
-        lax.all_gather(w_expand, ("wide", "narrow"), axis=0, tiled=True),
-        lax.all_gather(w_embed, ("wide", "narrow"), axis=0, tiled=True),
-        lax.all_gather(bn_gain, ("wide", "narrow"), axis=0, tiled=True),
-        lax.all_gather(bn_shift, ("wide", "narrow"), axis=0, tiled=True),
-    )
-    (
-        full_qkv,
-        full_out,
-        full_up,
-        full_down,
-        full_pre,
-        full_attn,
-        full_mid,
-        full_ffn,
-        full_table,
-        full_reduce,
-        full_spatial,
-        full_expand,
-        full_embed,
-        full_bn_gain,
-        full_bn_shift,
-    ) = gathered
+    both = ("wide", "narrow")
+    devices = lax.axis_size(both)
+    me = lax.axis_index("wide") * lax.axis_size("narrow") + lax.axis_index("narrow")
+    vectors = (gain_pre, gain_attn, gain_mid, gain_ffn, bn_gain, bn_shift, rel_table.reshape(-1))
+    held = jnp.concatenate(vectors)
+    held = jnp.pad(held, (0, 16 * 256 - held.shape[0])).reshape(16, 256)
+    gathered = gather_all([held, w_reduce, w_spatial, w_expand, w_embed, w_qkv, w_out, w_up, w_down], 1)
+    full_held = gathered[0].reshape(devices, -1)
+    full_reduce, full_spatial, full_expand, full_embed, full_qkv, full_out, full_up, full_down = (
+        item.reshape(-1, item.shape[-1]) for item in gathered[1:]
+    )
+    full_vectors, at = [], 0
+    for item in vectors:
+        full_vectors.append(full_held[:, at : at + item.shape[0]])
+        at += item.shape[0]
+    full_pre, full_attn, full_mid, full_ffn, full_bn_gain, full_bn_shift = (
+        item.reshape(-1) for item in full_vectors[:6]
+    )
+    full_table = full_vectors[6].reshape(devices, HEADS, -1).transpose(1, 0, 2).reshape(HEADS, -1)
     rows, length = (segments.shape[0], segments.shape[1])
     images, side = (features.shape[0], features.shape[1])
     patch_count = images * side * side
@@ -400,9 +744,8 @@
     pre_second = product(columns, full_spatial)
     second = smooth(pre_second).astype(jnp.bfloat16)
     third = product(second, full_expand)
-    bn_total, bn_squares = lax.psum(
-        (jnp.sum(third, axis=0), jnp.sum(third * third, axis=0)), ("wide", "narrow")
-    )
+    sums = jnp.concatenate([jnp.sum(third, axis=0), jnp.sum(third * third, axis=0)])
+    bn_total, bn_squares = jnp.split(total_sum(sums.reshape(16, -1), 3).reshape(-1), 2)
     bn_mean = bn_total / whole
     bn_inv = lax.rsqrt(bn_squares / whole - bn_mean * bn_mean + epsilon)
     bn_unit = (third - bn_mean) * bn_inv
@@ -436,88 +779,33 @@
     narrowed_low = narrowed.astype(jnp.bfloat16)
     result = middle + product(narrowed_low, full_down)
     mixed = result.astype(jnp.bfloat16)
-    group_norm0, group_norm2, group_out = (
-        lax.all_gather(normed0_low, "narrow", axis=0, tiled=True),
-        lax.all_gather(normed2_low, "narrow", axis=0, tiled=True),
-        lax.all_gather(d_out, "narrow", axis=0, tiled=True),
-    )
-    again = (
-        lax.all_gather(w_qkv, ("wide", "narrow"), axis=0, tiled=True),
-        lax.all_gather(w_out, ("wide", "narrow"), axis=0, tiled=True),
-        lax.all_gather(w_up, ("wide", "narrow"), axis=0, tiled=True),
-        lax.all_gather(w_down, ("wide", "narrow"), axis=0, tiled=True),
-        lax.all_gather(gain_pre, ("wide", "narrow"), axis=0, tiled=True),
-        lax.all_gather(gain_attn, ("wide", "narrow"), axis=0, tiled=True),
-        lax.all_gather(gain_mid, ("wide", "narrow"), axis=0, tiled=True),
-        lax.all_gather(gain_ffn, ("wide", "narrow"), axis=0, tiled=True),
-        lax.all_gather(rel_table, ("wide", "narrow"), axis=1, tiled=True),
-        lax.all_gather(w_reduce, ("wide", "narrow"), axis=0, tiled=True),
-        lax.all_gather(w_spatial, ("wide", "narrow"), axis=0, tiled=True),
-        lax.all_gather(w_expand, ("wide", "narrow"), axis=0, tiled=True),
-        lax.all_gather(w_embed, ("wide", "narrow"), axis=0, tiled=True),
-        lax.all_gather(bn_gain, ("wide", "narrow"), axis=0, tiled=True),
-        lax.all_gather(bn_shift, ("wide", "narrow"), axis=0, tiled=True),
-    )
-    (
-        back_qkv,
-        back_out,
-        back_up,
-        back_down,
-        back_pre,
-        back_attn,
-        back_mid,
-        back_ffn,
-        back_table,
-        back_reduce,
-        back_spatial,
-        back_expand,
-        back_embed,
-        back_bn_gain,
-        back_bn_shift,
-    ) = again
     grad_result = d_out.astype(jnp.float32)
-    grad_narrowed = product_nt(d_out, back_down)
+    grad_narrowed = product_nt(d_out, full_down)
     grad_activ, grad_gain_ffn = layer_norm_back(
-        grad_narrowed, unit3, inv3, back_ffn.astype(jnp.float32)
+        grad_narrowed, unit3, inv3, full_ffn.astype(jnp.float32)
     )
     grad_pre_up = smooth_back(pre_up, grad_activ).astype(jnp.bfloat16)
-    ffn_grad_cols, ffn_act_cols = (
-        lax.all_to_all(grad_pre_up, "narrow", split_axis=1, concat_axis=0, tiled=True),
-        lax.all_to_all(narrowed_low, "narrow", split_axis=1, concat_axis=0, tiled=True),
-    )
-    grad_w_down = product_tn(ffn_act_cols, group_out)
-    grad_w_up = product_tn(group_norm2, ffn_grad_cols)
-    grad_normed2 = product_nt(grad_pre_up, back_up)
+    grad_w_down = product_tn(d_out, narrowed_low)
+    grad_w_up = product_tn(normed2_low, grad_pre_up)
+    grad_normed2 = product_nt(grad_pre_up, full_up)
     grad_mid_in, grad_gain_mid = layer_norm_back(
-        grad_normed2, unit2, inv2, back_mid.astype(jnp.float32)
+        grad_normed2, unit2, inv2, full_mid.astype(jnp.float32)
     )
     grad_middle = grad_result + grad_mid_in
     grad_branch = grad_middle.astype(jnp.bfloat16)
     grad_w_out = product_tn(mixed_low, grad_branch)
-    grad_mixed_in = product_nt(grad_branch, back_out)
+    grad_mixed_in = product_nt(grad_branch, full_out)
     grad_scaled, grad_gain_attn = layer_norm_back(
-        grad_mixed_in, unit1, inv1, back_attn.astype(jnp.float32)
+        grad_mixed_in, unit1, inv1, full_attn.astype(jnp.float32)
     )
     grad_head_local = jnp.sum(jnp.sum(grad_scaled * attended, axis=0).reshape(HEADS, HDIM), axis=1)
     grad_attended = (grad_scaled * scale_row).astype(jnp.bfloat16)
     grad_packed, grad_strips = attend_back(packed, grad_attended, attended, segments, bias, logsums, win)
     grad_table = table_from_strips(grad_strips)
-    qkv_cols = lax.all_to_all(grad_packed, "narrow", split_axis=1, concat_axis=0, tiled=True)
-    grad_w_qkv = product_tn(group_norm0, qkv_cols)
-    sum_qkv, sum_up, sum_down = (
-        lax.psum_scatter(
-            grad_w_qkv.astype(jnp.bfloat16), "wide", scatter_dimension=0, tiled=True
-        ).astype(jnp.float32),
-        lax.psum_scatter(
-            grad_w_up.astype(jnp.bfloat16), "wide", scatter_dimension=0, tiled=True
-        ).astype(jnp.float32),
-        lax.psum_scatter(
-            grad_w_down.astype(jnp.bfloat16), "wide", scatter_dimension=1, tiled=True
-        ).astype(jnp.float32),
-    )
-    grad_normed0 = product_nt(grad_packed, back_qkv)
+    grad_w_qkv = product_tn(normed0_low, grad_packed)
+    grad_normed0 = product_nt(grad_packed, full_qkv)
     grad_start_in, grad_gain_pre = layer_norm_back(
-        grad_normed0, unit0, inv0, back_pre.astype(jnp.float32)
+        grad_normed0, unit0, inv0, full_pre.astype(jnp.float32)
     )
     grad_tokens = grad_middle + grad_start_in
     grad_embedded = (
@@ -526,57 +814,84 @@
         .astype(jnp.bfloat16)
     )
     grad_w_embed = product_tn(joined, grad_embedded)
-    grad_joined = product_nt(grad_embedded, back_embed)
+    grad_joined = product_nt(grad_embedded, full_embed)
     grad_pre_joined = smooth_back(pre_joined, grad_joined)
     grad_bn_shift = jnp.sum(grad_pre_joined, axis=0)
     grad_bn_gain = jnp.sum(grad_pre_joined * bn_unit, axis=0)
-    grad_unit = grad_pre_joined * back_bn_gain.astype(jnp.float32)
-    sum_unit, sum_cross, grad_head = lax.psum(
-        (jnp.sum(grad_unit, axis=0), jnp.sum(grad_unit * bn_unit, axis=0), grad_head_local),
-        ("wide", "narrow"),
-    )
+    smalls = (
+        grad_gain_pre,
+        grad_gain_attn,
+        grad_gain_mid,
+        grad_gain_ffn,
+        grad_bn_gain,
+        grad_bn_shift,
+        grad_table.reshape(-1),
+        grad_head_local,
+    )
+    small = jnp.concatenate(smalls)
+    small = jnp.pad(small, (0, -small.shape[0] % 1024)).reshape(-1, 128)
+    small = total_sum(small, 4).reshape(-1)
+    totals, at = [], 0
+    for item in smalls:
+        totals.append(small[at : at + item.shape[0]])
+        at += item.shape[0]
+    sum_pre, sum_attn, sum_mid, sum_ffn, sum_bn_gain, sum_bn_shift = (
+        lax.dynamic_slice_in_dim(item, me * (item.shape[0] // devices), item.shape[0] // devices)
+        for item in totals[:6]
+    )
+    breadth = 2 * RSPAN // devices
+    sum_table = lax.dynamic_slice_in_dim(totals[6].reshape(HEADS, -1), me * breadth, breadth, 1)
+    grad_head = totals[7]
+    bn_gain_row = full_bn_gain.astype(jnp.float32)
+    grad_unit = grad_pre_joined * bn_gain_row
+    sum_unit, sum_cross = totals[5] * bn_gain_row, totals[4] * bn_gain_row
     grad_third = (bn_inv * (grad_unit - sum_unit / whole - bn_unit * (sum_cross / whole))).astype(
         jnp.bfloat16
     )
     grad_w_expand = product_tn(second, grad_third)
-    grad_second = product_nt(grad_third, back_expand)
+    grad_second = product_nt(grad_third, full_expand)
     grad_pre_second = smooth_back(pre_second, grad_second).astype(jnp.bfloat16)
     grad_w_spatial = product_tn(columns, grad_pre_second)
-    grad_columns = product_nt(grad_pre_second, back_spatial)
+    grad_columns = product_nt(grad_pre_second, full_spatial)
     grad_first = fold(grad_columns.reshape(images, side, side, -1)).reshape(patch_count, -1)
     grad_pre_first = smooth_back(pre_first, grad_first).astype(jnp.bfloat16)
     grad_w_reduce = product_tn(stem_in, grad_pre_first)
-    grad_features = (grad_pre_joined + product_nt(grad_pre_first, back_reduce)).reshape(
+    grad_features = (grad_pre_joined + product_nt(grad_pre_first, full_reduce)).reshape(
         features.shape
     )
-    summed = (
-        lax.psum_scatter(grad_w_out, ("wide", "narrow"), scatter_dimension=0, tiled=True),
-        lax.psum_scatter(grad_gain_pre, ("wide", "narrow"), scatter_dimension=0, tiled=True),
-        lax.psum_scatter(grad_gain_attn, ("wide", "narrow"), scatter_dimension=0, tiled=True),
-        lax.psum_scatter(grad_gain_mid, ("wide", "narrow"), scatter_dimension=0, tiled=True),
-        lax.psum_scatter(grad_gain_ffn, ("wide", "narrow"), scatter_dimension=0, tiled=True),
-        lax.psum_scatter(grad_table, ("wide", "narrow"), scatter_dimension=1, tiled=True),
-        lax.psum_scatter(grad_w_reduce, ("wide", "narrow"), scatter_dimension=0, tiled=True),
-        lax.psum_scatter(grad_w_spatial, ("wide", "narrow"), scatter_dimension=0, tiled=True),
-        lax.psum_scatter(grad_w_expand, ("wide", "narrow"), scatter_dimension=0, tiled=True),
-        lax.psum_scatter(grad_w_embed, ("wide", "narrow"), scatter_dimension=0, tiled=True),
-        lax.psum_scatter(grad_bn_gain, ("wide", "narrow"), scatter_dimension=0, tiled=True),
-        lax.psum_scatter(grad_bn_shift, ("wide", "narrow"), scatter_dimension=0, tiled=True),
-    )
-    (
-        sum_out,
-        sum_pre,
-        sum_attn,
-        sum_mid,
-        sum_ffn,
-        sum_table,
-        sum_reduce,
-        sum_spatial,
-        sum_expand,
-        sum_embed,
-        sum_bn_gain,
-        sum_bn_shift,
-    ) = summed
+    lines, planes = lax.axis_size("wide") // 2, lax.axis_size("narrow") // 2
+
+    def by_rows(grad):
+        return grad.astype(jnp.bfloat16).reshape(lines, 2, planes, 2, -1, grad.shape[1])
+
+    def by_blocks(grad):
+        low = grad.astype(jnp.bfloat16).reshape(lines, 2, -1, planes, 2, grad.shape[1] // (2 * planes))
+        return low.transpose(0, 1, 3, 4, 2, 5)
+
+    def by_windows(grad):
+        low = grad.astype(jnp.bfloat16).reshape(lines, 2, -1, planes, grad.shape[1] // planes)
+        width = grad.shape[1] // (2 * planes)
+        window = -(-width // 128) * 128
+        span = 2 * width
+        pieces = [low[..., :window], low[..., span - window :]]
+        return jnp.stack(pieces, axis=4).transpose(0, 1, 3, 4, 2, 5)
+
+    grads = [
+        by_blocks(grad_w_down),
+        by_blocks(grad_w_up),
+        by_rows(grad_w_out),
+        by_windows(grad_w_qkv),
+        by_rows(grad_w_embed),
+        by_rows(grad_w_expand),
+        by_rows(grad_w_spatial),
+        by_rows(grad_w_reduce),
+    ]
+    sum_down, sum_up, sum_out, sum_qkv, sum_embed, sum_expand, sum_spatial, sum_reduce = scatter_all(grads, 2)
+    sum_down = sum_down.T
+    width = 3 * D // (2 * planes)
+    sum_qkv = jnp.where(
+        lax.axis_index("narrow") % 2 == 0, sum_qkv[:, :width], sum_qkv[:, sum_qkv.shape[1] - width :]
+    )
     return (
         mixed,
         grad_tokens,

time: 1510 us -> 682 us (0.45)
  waiting for transfers between devices: 825 us -> 0 us
  blocking collectives: 244 us -> 0 us
  Pallas kernels: 116 us -> 352 us
  local copies, waits for them, and re-layouts: 70.4 us -> 127 us
  starting transfers between devices: 17 us -> 0 us
  matrix products: 142 us -> 126 us
    reduce_scatter x7 -> x0, waiting for transfers between devices: 465 us -> none  [the longest x1 135 us: local(): lax.psum_scatter(grad_w_expand, ('wide', 'narrow'), scatter_dimension=0,...]
    pallas_call x0 -> x4, Pallas kernels: none -> 258 us  [the longest x1 105 us: scatter_all(): pl.pallas_call(functools.partial(scatter_kernel, count, lines, rows), out...]
    all_to_all x3 -> x0, waiting for transfers between devices: 180 us -> none  [the longest x1 81.1 us: local(): lax.all_to_all(grad_packed, 'narrow', split_axis=1, concat_axis=0, tiled=...]
    unnamed x18 -> x0, waiting for transfers between devices: 139 us -> none
    all_gather x3 -> x0, blocking collectives: 124 us -> none  [the longest x1 41.8 us: local(): lax.all_gather(w_reduce, ('wide', 'narrow'), axis=0, tiled=True)]
    psum x2 -> x0, blocking collectives: 77.6 us -> none  [the longest x1 39.8 us: local(): lax.psum((jnp.sum(grad_unit, axis=0), jnp.sum(grad_unit * bn_unit, axis=0...]
    reshape x0 -> x10, local copies, waits for them, and re-layouts: none -> 63.3 us  [the longest x4 52.7 us: by_blocks(): grad.astype(jnp.bfloat16)]
    unnamed x1 -> x0, blocking collectives: 42.3 us -> none
  transfers between devices with their start and end apart: 20 -> 0, of which waited for: 10 -> 0; matrix products, arithmetic and copies ran while one was open for 18% -> 0% of each run, Pallas kernels for 8% -> 0%
where the time goes in v1:
time: 682 us; the launch traced here: 672 us
  Pallas kernels  352 us (52%)
  local copies, waits for them, and re-layouts  127 us (19%)
  matrix products  126 us (18%)
  other arithmetic  65.3 us (10%)
    pallas_call x1, Pallas kernels, scatter_all(): pl.pallas_call(functools.partial(scatter_kernel, count, lines, rows), out...  105 us
    pallas_call x1, Pallas kernels, gather_all(): pl.pallas_call(functools.partial(gather_kernel, count, lines, rows), out_...  98.1 us
    pallas_call x1, Pallas kernels, attend_back(): pl.pallas_call(attend_back_kernel, out_shape=(jax.ShapeDtypeStruct((lengt...  64.7 us
    pallas_call x2, Pallas kernels, total_sum(): pl.pallas_call(functools.partial(total_kernel, lines, rows), out_shape=ja...  55 us
    reshape x4, local copies, waits for them, and re-layouts, by_blocks(): grad.astype(jnp.bfloat16)  52.7 us
    dot_general x8, matrix products, product_nt(): lax.dot_general(lhs_matrix, rhs_matrix, (((1,), (1,)), ((), ())), preferr...  51 us
    dot_general x8, matrix products, product(): return jnp.dot(lhs_matrix, rhs_matrix, preferred_element_type=jnp.float32)  39.3 us
    dot_general x8, matrix products, product_tn(): lax.dot_general(lhs_matrix, rhs_matrix, (((0,), (0,)), ((), ())), preferr...  35.6 us

profile of v1, /device:TPU:0, one launch (start us, length us, event | category | flops | bytes accessed | tf_op | source)
XLA Modules:
  0.0 672.2 jit_solution(3083513216698139180)
XLA Ops:
  1.5 4.1 concatenate.60
  6.2 98.1 %gather_weights.1 = (bf16[4,2,2,2,16,256]{5,4,3,2,1,0:T(8,128)(2,1)}, bf16[4,2,2,2,32,256]{5,4,3,2,1,0:T(8,128)(2,1)}, bf16[4,2,2,2,72,256]{5,4,3,2,1,0:T(8,128)...) custom-call(bf16[16,256]{1,0:T(8,128)(2,1)} %reshape.511.refs_0_, ...), custom_call_target="tpu_custom_call" | custom-call | bytes 40000000 | tf_op jit(solution)/shard_map/gather_weights/pallas_call | solution.py:473
  104.4 2.8 multiply_convert_fusion.11
  107.7 1.2 copy-done.21
  111.2 20.6 %total_sum.2 = f32[16,128]{1,0:T(8,128)} custom-call(f32[16,128]{1,0:T(8,128)} %pad_maximum_fusion.3.x_ref), custom_call_target="tpu_custom_call" | custom-call | bytes 1000000 | tf_op jit(solution)/shard_map/total_sum/pallas_call | solution.py:674
  133.1 1.0 copy.141
  137.1 1.3 multiply_convert_fusion.6
  138.6 2.3 fusion.71
  141.7 9.3 %scatter_fusion = f32[1024,768]{1,0:T(8,128)S(1)} fusion(f32[1024,768]{1,0:T(8,128)S(1)} %reshape.543, s32[576]{0:T(1024)S(1)} %get-tuple-element.161, f32[576,768]{1,0:T(8,128)} %fusion.71), kind=kCustom, calls=%fused_computation.1 | custom fusion | flops 442368 | bytes 5310720 | tf_op jit(solution)/shard_map/scatter-add | solution.py:761
  151.1 2.4 copy.112
  153.7 2.3 multiply_reduce_fusion.11
  157.0 7.8 %convolution_convert_fusion.packed = bf16[1024,2304]{1,0:T(8,128)(2,1)} fusion(bf16[768,2304]{1,0:T(8,128)(2,1)} %bitcast.259, f32[1024,768]{1,0:T(8,128)S(1)} %scatter_fusion, f32[768]{0:T(1024)S(1)} %reshape.547, f32[1024]{0:T(1024)S(1)} %add_rsqrt_fusion.3, f32[1024]{0:T(1024)S(1)} %broadcast_multiply_fusion.11), kind=kOutput, calls=%fused_computation.20 | convolution fusion | flops 3629383680 | bytes 11414528 | tf_op jit(solution)/shard_map/dot_general | solution.py:20
  167.7 1.0 copy.111.segk
  168.8 1.0 copy-done.2
  169.8 29.1 %attend.1 = (f32[1024,768]{1,0:T(8,128)S(1)}, f32[8,6,256]{2,1,0:T(8,128)S(1)}, f32[6,5,128,256]{3,2,1,0:T(8,128)}) custom-call(s32[2,8]{1,0:T(2,128)S(1)} %pad_add_fusion.7.win, bf16[1024,2304]{1,0:T(8,128)(2,1)} %convolution_convert_fusion.packed, s32[1024,1]{1,0:T(8,128)S(1)} %copy-done.2, s32[1,1024]{1,0:T(1,128)S(1)} %copy-done.3, ...), custom_call_target="tpu_custom_call" | custom-call | flops 20000000000 | bytes 10000000 | tf_op jit(solution)/shard_map/attend/pallas_call | solution.py:196
  200.7 4.0 fusion.69
  204.7 1.6 copy-done.9
  206.8 11.9 %fusion.62 = (f32[1024]{0:T(1024)S(1)}, f32[1024,3072]{1,0:T(8,128)S(1)}) fusion(bf16[768,3072]{1,0:T(8,128)(2,1)} %bitcast.257, f32[1024,768]{0,1:T(8,128)} %copy-done.9, f32[768]{0:T(1024)S(1)} %reshape.550, f32[1024]{0:T(1024)S(1)} %add_rsqrt_fusion.1, f32[1024]{0:T(1024)S(1)} %broadcast_multiply_fusion.9), kind=kOutput, calls=%fused_computation.230 | convolution fusion | flops 4863294464 | bytes 20462592 | tf_op jit(solution)/shard_map/dot_general | solution.py:20
  218.7 5.8 multiply_reduce_fusion.1
  224.6 16.8 %fusion.7 = (f32[3072]{0:T(1024)S(1)}, f32[1024]{0:T(1024)S(1)}, f32[1024]{0:T(1024)S(1)}, f32[3072,1024]{0,1:T(8,128)}) fusion(f32[1024]{0:T(1024)S(1)} %add_rsqrt_fusion, f32[1024]{0:T(1024)S(1)} %broadcast_multiply_fusion.2, f32[1024,3072]{1,0:T(8,128)} %copy-done.6, f32[3072]{0:T(1024)S(1)} %reshape.551, bf16[3072,768]{1,0:T(8,128)(2,1)} %bitcast.255, ...), kind=kOutput, calls=%fused_computation.13 | convolution fusion | flops 4882164736 | bytes 31498240 | tf_op jit(solution)/shard_map/dot_general | solution.py:30
  241.5 16.2 %fusion.6 = (bf16[1024,3072]{1,0:T(8,128)(2,1)S(1)}, bf16[1024,3072]{1,0:T(8,128)(2,1)}) fusion(f32[1024,3072]{1,0:T(8,128)S(1)} %bitcast.208, f32[3072,1024]{0,1:T(8,128)} %get-tuple-element.217, f32[1024]{0:T(1024)S(1)} %broadcast_multiply_fusion, f32[1024]{0:T(1024)S(1)} %broadcast_multiply_fusion.1, f32[3072]{0:T(1024)S(1)} %reshape.551, ...), kind=kLoop, calls=%fused_computation.10 | loop fusion | flops 94371840 | bytes 37777408 | tf_op jit(solution)/shard_map/convert_element_type | solution.py:787
  257.7 10.5 %multiply_reduce_fusion.3 = (f32[768]{0:T(1024)S(1)}, f32[1024]{0:T(1024)S(1)}, f32[1024]{0:T(1024)S(1)}, f32[1024,768]{0,1:T(8,128)}) fusion(f32[1024,768]{0,1:T(8,128)S(1)} %copy-done.10, f32[1024]{0:T(1024)S(1)} %add_rsqrt_fusion.1, f32[1024]{0:T(1024)S(1)} %broadcast_multiply_fusion.9, f32[768]{0:T(1024)S(1)} %reshape.550, ...), kind=kOutput, calls=%fused_computation.37 | convolution fusion | flops 4838126592 | bytes 17324032 | tf_op jit(solution)/shard_map/dot_general | solution.py:30
  268.2 2.8 copy.114
  271.0 4.4 multiply_add_fusion.1
  275.4 2.2 multiply_reduce_fusion.13
  277.7 3.1 multiply_reduce_fusion.2
  280.8 64.7 %attend_back.1 = (bf16[1024,2304]{1,0:T(8,128)(2,1)}, f32[12,5,256]{2,1,0:T(8,128)}) custom-call(s32[2,8]{1,0:T(2,128)} %copy-done.4, bf16[1024,2304]{1,0:T(8,128)(2,1)} %convolution_convert_fusion.packed, bf16[1024,768]{1,0:T(8,128)(2,1)} %get-tuple-element.166.grads, f32[1024,768]{1,0:T(8,128)} %copy-done, s32[1024,1]{1,0:T(8,128)} %copy.111.segk, ...), custom_call_target="tpu_custom_call" | custom-call | flops 49999998976 | bytes 20000000 | tf_op jit(solution)/shard_map/attend_back/pallas_call | solution.py:300
  345.5 8.3 %convolution_convert_fusion.3 = bf16[768,2304]{1,0:T(8,128)(2,1)} fusion(bf16[1024,2304]{1,0:T(8,128)(2,1)} %get-tuple-element.53, f32[1024,768]{0,1:T(8,128)S(1)} %copy-done.7, f32[768]{0:T(1024)S(1)} %reshape.547, f32[1024]{0:T(1024)S(1)} %add_rsqrt_fusion.3, f32[1024]{0:T(1024)S(1)} %broadcast_multiply_fusion.11), kind=kOutput, calls=%fused_computation.23 | convolution fusion | flops 3628793856 | bytes 11414528 | tf_op jit(solution)/shard_map/dot_general | solution.py:24
  353.8 7.8 %reshape.536 = bf16[4,2,96,2,1152]{4,3,2,1,0:T(2,128)(2,1)} reshape(bf16[768,2304]{1,0:T(8,128)(2,1)} %convolution_convert_fusion.3) | data formatting | bytes 7077888 | tf_op jit(solution)/shard_map/reshape | solution.py:872
  361.7 4.5 fusion.66
  366.8 2.4 maximum_bitcast_fusion.refs_3_
  371.1 9.2 %multiply_reduce_fusion.5 = (f32[768]{0:T(1024)S(1)}, f32[1024]{0:T(1024)S(1)}, f32[1024]{0:T(1024)S(1)}, f32[1024,768]{0,1:T(8,128)}) fusion(f32[1024,768]{0,1:T(8,128)S(1)} %copy-done.7, f32[1024]{0:T(1024)S(1)} %add_rsqrt_fusion.3, f32[1024]{0:T(1024)S(1)} %broadcast_multiply_fusion.11, f32[768]{0:T(1024)S(1)} %reshape.547, ...), kind=kOutput, calls=%fused_computation.39 | convolution fusion | flops 3630167296 | bytes 14571520 | tf_op jit(solution)/shard_map/dot_general | solution.py:30
  380.4 5.4 multiply_add_fusion
  385.8 2.2 copy.117
  388.0 9.2 %gather_fusion = bf16[576,768]{1,0:T(8,128)(2,1)} fusion(bf16[1,1024,768]{2,1,0:T(8,128)(2,1)S(1)} %copy.117, s32[576]{0:T(1024)S(1)} %copy-done.14), kind=kCustom, calls=%fused_computation | custom fusion | bytes 1774080 | tf_op jit(solution)/shard_map/gather | solution.py:812
  397.3 6.8 %fusion.63 = (f32[1024]{0:T(1024)S(1)}, f32[1024]{0:T(1024)S(1)}, f32[576,1024]{1,0:T(8,128)}) fusion(f32[1024]{0:T(1024)} %copy-done.44, f32[576,1024]{1,0:T(8,128)} %copy-done.15, f32[1024]{0:T(1024)} %copy-done.45, bf16[576,1024]{1,0:T(8,128)(2,1)S(1)} %bitcast.235, f32[1024]{0:T(1024)} %copy-done.54, f32[1024]{0:T(1024)} %copy-done.39, ...), kind=kOutput, calls=%fused_computation.231 | convolution fusion | flops 922482688 | bytes 8380416 | tf_op jit(solution)/shard_map/dot_general | solution.py:30
  404.1 1.3 constant_dynamic-update-slice_fusion.15
  405.4 1.3 constant_dynamic-update-slice_fusion.14
  406.7 1.3 constant_dynamic-update-slice_fusion.13
  408.0 1.4 reshape.528
  409.4 1.3 reduce_sum.322
  410.7 1.3 constant_dynamic-update-slice_fusion.12
  412.0 1.4 pad_bitcast_fusion.x_ref
  413.4 34.5 %total_sum.3 = f32[88,128]{1,0:T(8,128)} custom-call(f32[88,128]{1,0:T(8,128)} %pad_bitcast_fusion.x_ref), custom_call_target="tpu_custom_call" | custom-call | bytes 1000000 | tf_op jit(solution)/shard_map/total_sum/pallas_call | solution.py:674
  448.7 2.3 multiply_convert_fusion.5
  451.8 1.0 copy-done.47
  452.8 2.2 convolution_convert_fusion.4
  455.0 1.5 convolution_convert_fusion.8
  456.5 2.6 convolution_convert_fusion.5
  459.9 2.9 convolution_convert_fusion.6
  462.9 7.0 %convolution_convert_fusion.1 = bf16[768,3072]{1,0:T(8,128)(2,1)} fusion(bf16[1024,3072]{1,0:T(8,128)(2,1)S(1)} %bitcast.215, f32[1024,768]{0,1:T(8,128)S(1)} %copy-done.11, f32[768]{0:T(1024)S(1)} %copy-done.51, f32[1024]{0:T(1024)S(1)} %copy-done.53, f32[1024]{0:T(1024)S(1)} %copy-done.43), kind=kOutput, calls=%fused_computation.21 | convolution fusion | flops 4837343232 | bytes 14167040 | tf_op jit(solution)/shard_map/dot_general | solution.py:24
  469.9 11.8 %reshape.534 = bf16[4,2,96,2,2,768]{5,4,3,2,1,0:T(2,128)(2,1)} reshape(bf16[768,3072]{1,0:T(8,128)(2,1)} %convolution_convert_fusion.1) | data formatting | bytes 9437184 | tf_op jit(solution)/shard_map/reshape | solution.py:868
  481.7 5.5 copy.146
  490.2 1.4 fusion.27
  491.5 2.1 copy.128
  493.6 9.8 %fusion.9 = bf16[768,3072]{0,1:T(8,128)(2,1)} fusion(bf16[1024,3072]{1,0:T(8,128)(2,1)} %get-tuple-element.165, bf16[1024,768]{1,0:T(8,128)(2,1)S(1)} %copy-done.19), kind=kOutput, calls=%fused_computation.26 | convolution fusion | flops 4834197504 | bytes 12582912 | tf_op jit(solution)/shard_map/dot_general | solution.py:24
  503.4 19.6 %reshape.579 = bf16[4,2,96,2,2,768]{2,1,0,5,4,3:T(2,128)(2,1)} reshape(bf16[768,3072]{0,1:T(8,128)(2,1)} %fusion.9) | data formatting | bytes 9437184 | tf_op jit(solution)/shard_map/reshape | solution.py:868
  522.9 15.8 %copy.124 = bf16[4,2,96,2,2,768]{5,2,4,3,1,0:T(8,128)(2,1)} copy(bf16[4,2,96,2,2,768]{2,1,0,5,4,3:T(2,128)(2,1)} %reshape.579) | data formatting | bytes 9437184 | tf_op jit(solution)/shard_map/reshape | solution.py:868
  538.7 104.7 %scatter_grads.1 = (f32[96,768]{1,0:T(8,128)}, f32[96,768]{1,0:T(8,128)}, f32[24,768]{1,0:T(8,128)}, f32[96,640]{1,0:T(8,128)}, f32[32,768]{1,0:T(8,128)}, /*ind...) custom-call(bf16[4,2,2,2,96,768]{5,4,3,2,1,0:T(8,128)(2,1)} %bitcast.211, ...), custom_call_target="tpu_custom_call" | custom-call | bytes 40000000 | tf_op jit(solution)/shard_map/scatter_grads/pallas_call | solution.py:627
  643.5 2.0 slice_select_fusion
  645.5 3.8 convolution_add_fusion.1
  654.1 2.4 copy.131
  656.4 9.1 %add_convert_fusion = bf16[1024,768]{0,1:T(8,128)(2,1)S(1)} fusion(f32[1024,768]{0,1:T(8,128)} %copy-done.9, bf16[1024,3072]{1,0:T(8,128)(2,1)} %get-tuple-element.165, bf16[3072,768]{1,0:T(8,128)(2,1)} %bitcast.256), kind=kOutput, calls=%fused_computation.47 | convolution fusion | flops 4833411072 | bytes 15728640 | tf_op jit(solution)/shard_map/dot_general | solution.py:20
  665.6 1.6 copy.130
  (264 shorter events, 33.2 us)
Async XLA Ops:
  107.4 1.4 copy-start.21
  107.7 2.0 copy-start.46
  108.8 1.0 copy-start.58
  109.7 27.4 %copy-start.23 = (bf16[1,24,24,1024]{3,2,1,0:T(8,128)(2,1)S(1)}, bf16[1,24,24,1024]{3,2,1,0:T(8,128)(2,1)}, u32[]{:S(2)}) copy-start(bf16[1,24,24,1024]{3,2,1,0:T(8,128)(2,1)} %param.22) | copy-start | bytes 3538948
  110.5 30.3 %copy-start.15 = (f32[576,1024]{1,0:T(8,128)}, f32[576,1024]{1,0:T(8,128)S(1)}, u32[]{:S(2)}) copy-start(f32[576,1024]{1,0:T(8,128)S(1)} %get-tuple-element.212) | copy-start | bytes 7077892
  132.4 18.7 %copy-start.44 = (f32[1024]{0:T(1024)}, f32[1024]{0:T(1024)S(1)}, u32[]{:S(2)}) copy-start(f32[1024]{0:T(1024)S(1)} %fusion.57) | copy-start | bytes 12292
  133.1 18.0 %copy-start.45 = (f32[1024]{0:T(1024)}, f32[1024]{0:T(1024)S(1)}, u32[]{:S(2)}) copy-start(f32[1024]{0:T(1024)S(1)} %multiply_bitcast_fusion) | copy-start | bytes 12292
  136.3 4.5 copy-start.39
  137.1 3.7 copy-start.54
  137.1 1.4 copy-start.57
  138.4 2.4 copy-start.25
  138.5 2.3 copy-start.55
  138.5 3.0 copy-start.20
  156.9 10.3 %copy-start.3 = (s32[1,1024]{1,0:T(1,128)S(1)}, s32[1,1024]{1,0:T(1,128)}, u32[]{:S(2)}) copy-start(s32[1,1024]{1,0:T(1,128)} %segq.3) | copy-start | bytes 12292
  167.7 31.2 %copy-start.4 = (s32[2,8]{1,0:T(2,128)}, s32[2,8]{1,0:T(2,128)S(1)}, u32[]{:S(2)}) copy-start(s32[2,8]{1,0:T(2,128)S(1)} %pad_add_fusion.7.win) | copy-start | bytes 196
  168.8 1.0 copy-start.2
  169.8 29.8 %copy-start.56 = (f32[12]{0:T(128)S(1)}, f32[12]{0:T(128)}, u32[]{:S(2)}) copy-start(f32[12]{0:T(128)} %param.34) | copy-start | bytes 148
  199.6 78.1 %copy-start = (f32[1024,768]{1,0:T(8,128)}, f32[1024,768]{1,0:T(8,128)S(1)}, u32[]{:S(2)}) copy-start(f32[1024,768]{1,0:T(8,128)S(1)} %get-tuple-element.47.attended) | copy-start | bytes 9437188
  204.7 1.6 copy-start.9
  204.7 66.3 %copy-start.42 = (f32[1024]{0:T(1024)}, f32[1024]{0:T(1024)S(1)}, u32[]{:S(2)}) copy-start(f32[1024]{0:T(1024)S(1)} %broadcast_multiply_fusion.9) | copy-start | bytes 12292
  206.7 64.3 %copy-start.52 = (f32[1024]{0:T(1024)}, f32[1024]{0:T(1024)S(1)}, u32[]{:S(2)}) copy-start(f32[1024]{0:T(1024)S(1)} %add_rsqrt_fusion.1) | copy-start | bytes 12292
  206.8 64.2 %copy-start.50 = (f32[768]{0:T(1024)}, f32[768]{0:T(1024)S(1)}, u32[]{:S(2)}) copy-start(f32[768]{0:T(1024)S(1)} %reshape.550) | copy-start | bytes 9220
  218.7 5.8 copy-start.6
  224.6 16.9 %slice-start = ((s8[12582912]{0:T(1024)(128)(4,1)}), s8[4194304]{0:T(1024)(128)(4,1)S(1)}, s32[]{:S(2)}) async-start(s8[12582912]{0:T(1024)(128)(4,1)} %bitcast.207), calls=%async_computation | async-start | bytes 8388608
  224.6 16.9 %slice-start.1 = ((s8[12582912]{0:T(1024)(128)(4,1)}), s8[4194304]{0:T(1024)(128)(4,1)S(1)}, s32[]{:S(2)}) async-start(s8[12582912]{0:T(1024)(128)(4,1)} %bitcast.207), calls=%async_computation.1 | async-start | bytes 8388608
  224.6 16.9 %slice-start.2 = ((s8[12582912]{0:T(1024)(128)(4,1)}), s8[4194304]{0:T(1024)(128)(4,1)S(1)}, s32[]{:S(2)}) async-start(s8[12582912]{0:T(1024)(128)(4,1)} %bitcast.207), calls=%async_computation.2 | async-start | bytes 8388608
  241.5 16.2 %copy-start.10 = (f32[1024,768]{0,1:T(8,128)S(1)}, f32[1024,768]{0,1:T(8,128)}, u32[]{:S(2)}) copy-start(f32[1024,768]{0,1:T(8,128)} %copy-done.9) | copy-start | bytes 9437188
  257.7 10.5 %copy-start.17 = (bf16[1024,3072]{1,0:T(8,128)(2,1)}, bf16[1024,3072]{1,0:T(8,128)(2,1)S(1)}, u32[]{:S(2)}) copy-start(bf16[1024,3072]{1,0:T(8,128)(2,1)S(1)} %get-tuple-element.164) | copy-start | bytes 18874372
  271.0 4.4 copy-start.18
  275.4 2.2 copy-start.12
  280.8 64.7 %copy-start.7 = (f32[1024,768]{0,1:T(8,128)S(1)}, f32[1024,768]{0,1:T(8,128)}, u32[]{:S(2)}) copy-start(f32[1024,768]{0,1:T(8,128)} %copy.112) | copy-start | bytes 9437188
  366.8 2.4 copy-start.35
  380.3 7.7 %copy-start.41 = (f32[10508]{0:T(1024)}, f32[10508]{0:T(1024)S(1)}, u32[]{:S(2)}) copy-start(f32[10508]{0:T(1024)S(1)} %constant_dynamic-update-slice_fusion.16) | copy-start | bytes 126100
  385.8 2.2 copy-start.14
  388.0 9.2 %copy-start.24 = (bf16[1,24,24,1024]{3,2,1,0:T(8,128)(2,1)S(1)}, bf16[1,24,24,1024]{3,2,1,0:T(8,128)(2,1)}, u32[]{:S(2)}) copy-start(bf16[1,24,24,1024]{3,2,1,0:T(8,128)(2,1)} %param.22) | copy-start | bytes 3538948
  397.3 9.4 %copy-start.40 = (f32[3072]{0:T(1024)S(1)}, f32[3072]{0:T(1024)}, u32[]{:S(2)}) copy-start(f32[3072]{0:T(1024)} %reshape.527) | copy-start | bytes 36868
  397.3 51.4 %copy-start.16 = (f32[576,1024]{1,0:T(8,128)S(1)}, f32[576,1024]{1,0:T(8,128)}, u32[]{:S(2)}) copy-start(f32[576,1024]{1,0:T(8,128)} %copy-done.15) | copy-start | bytes 7077892
  447.9 3.1 copy-start.59
  447.9 3.1 copy-start.61
  451.0 1.8 copy-start.47
  452.8 10.1 %slice-start.3 = ((s8[6291456]{0:T(1024)(128)(4,1)}), s8[4194304]{0:T(1024)(128)(4,1)S(1)}, s32[]{:S(2)}) async-start(s8[6291456]{0:T(1024)(128)(4,1)} %bitcast.214), calls=%async_computation.3 | async-start | bytes 8388608
  455.0 1.5 copy-start.26
  455.0 1.5 copy-start.29
  456.5 2.6 copy-start.1
  456.5 3.4 copy-start.13
  456.5 6.4 slice-start.4
  459.9 3.0 copy-start.11
  459.9 3.0 copy-start.43
  459.9 3.0 copy-start.51
  459.9 3.0 copy-start.53
  481.7 5.6 copy-start.22
  488.7 1.1 copy-start.30
  489.3 4.4 copy-start.19
  490.1 13.2 %copy-start.27 = (bf16[576,256]{1,0:T(8,128)(2,1)}, bf16[576,256]{1,0:T(8,128)(2,1)S(1)}, u32[]{:S(2)}) copy-start(bf16[576,256]{1,0:T(8,128)(2,1)S(1)} %fusion.37) | copy-start | bytes 884740
  538.7 106.8 %copy-start.28 = (bf16[576,256]{1,0:T(8,128)(2,1)S(1)}, bf16[576,256]{1,0:T(8,128)(2,1)}, u32[]{:S(2)}) copy-start(bf16[576,256]{1,0:T(8,128)(2,1)} %copy-done.27) | copy-start | bytes 884740
  643.4 5.8 copy-start.34
  643.4 10.6 %copy-start.8 = (f32[1024,768]{0,1:T(8,128)S(1)}, f32[1024,768]{0,1:T(8,128)}, u32[]{:S(2)}) copy-start(f32[1024,768]{0,1:T(8,128)} %multiply_add_fusion) | copy-start | bytes 9437188
  665.5 1.6 copy-start.38
  665.5 2.3 copy-start.33
  665.5 3.0 copy-start.32
  665.5 3.7 copy-start.49
  665.6 4.3 copy-start.37
  665.6 4.9 copy-start.48
  665.6 5.5 copy-start.36
  (3 other events, 2.1 us)

commit v2 on v1

--- a/solution.py
+++ b/solution.py
@@ -511,65 +511,63 @@
 
 
 class Scatter:
-    def __init__(self, place, sends, grad, out, buffers, local_sem):
-        self.p, self.s, self.grad, self.out, self.local_sem = place, sends, grad, out, local_sem
-        self.own, self.other, self.low1, self.high1, self.low2, self.high2, self.line0, self.lines_in = buffers
-        cols = grad.shape[-1]
+    def __init__(self, place, sends, full, out, buffers):
+        self.p, self.s, self.full, self.out = place, sends, full, out
+        self.other, self.low1, self.high1, self.low2, self.high2, self.line0, self.lines_in = buffers
+        cols = full.shape[-1]
         cut = cols // 256 * 128
         self.low, self.high = pl.ds(0, cut), pl.ds(cut, cols - cut)
 
     def begin(self):
-        p = self.p
-        self.local = pltpu.make_async_copy(self.grad.at[:, :, :, p.core], self.own, self.local_sem)
-        self.local.start()
-        self.stage = [self.s.start(self.grad.at[:, :, :, 1 - p.core], self.other, p.device(core=1 - p.core))]
+        core = self.p.core
+        self.stage = [self.s.start(self.full.at[:, :, :, 1 - core], self.other, self.p.device(core=1 - core))]
 
     def second(self):
-        p, own = self.p, self.own
-        self.local.wait()
+        p, full, dtype = self.p, self.full, self.full.dtype
         for copy in self.stage:
             copy.wait_recv()
 
         def add(i):
-            own[i] = plus(own[i], self.other[i]).astype(own.dtype)
-
-        add_loop(own.shape[:3], add)
-        self.stage = [self.s.start(own.at[:, 1 - p.side, :, :, self.high], self.high1, p.device(side=1 - p.side))]
+            l, x, y = i
+            full[l, x, y, p.core] = plus(full[l, x, y, p.core], self.other[l, x, y]).astype(dtype)
+
+        add_loop(self.other.shape[:3], add)
+        self.stage = [self.s.start(full.at[:, 1 - p.side, :, p.core, :, self.high], self.high1, p.device(side=1 - p.side))]
         for k in range(1, p.rows):
             to = p.row_peer(k)
-            self.stage.append(self.s.start(own.at[:, :, to, :, self.low], self.low1.at[k - 1], p.device(row=to)))
+            self.stage.append(self.s.start(full.at[:, :, to, p.core, :, self.low], self.low1.at[k - 1], p.device(row=to)))
 
     def third(self):
-        p, own = self.p, self.own
+        p, full, dtype = self.p, self.full, self.full.dtype
         for copy in self.stage:
             copy.wait_recv()
 
         def add_low(i):
             l, x = i
-            terms = [own[l, x, p.row, :, self.low]] + [self.low1[k, l, x] for k in range(p.rows - 1)]
-            own[l, x, p.row, :, self.low] = plus(*terms).astype(own.dtype)
+            terms = [full[l, x, p.row, p.core, :, self.low]] + [self.low1[k, l, x] for k in range(p.rows - 1)]
+            full[l, x, p.row, p.core, :, self.low] = plus(*terms).astype(dtype)
 
         def add_high(i):
             l, y = i
-            own[l, p.side, y, :, self.high] = plus(own[l, p.side, y, :, self.high], self.high1[l, y]).astype(own.dtype)
+            full[l, p.side, y, p.core, :, self.high] = plus(full[l, p.side, y, p.core, :, self.high], self.high1[l, y]).astype(dtype)
 
         add_loop((p.lines, 2), add_low)
         add_loop((p.lines, p.rows), add_high)
-        self.stage = [self.s.start(own.at[:, 1 - p.side, p.row, :, self.low], self.low2, p.device(side=1 - p.side))]
+        self.stage = [self.s.start(full.at[:, 1 - p.side, p.row, p.core, :, self.low], self.low2, p.device(side=1 - p.side))]
         for k in range(1, p.rows):
             to = p.row_peer(k)
-            self.stage.append(self.s.start(own.at[:, p.side, to, :, self.high], self.high2.at[k - 1], p.device(row=to)))
+            self.stage.append(self.s.start(full.at[:, p.side, to, p.core, :, self.high], self.high2.at[k - 1], p.device(row=to)))
 
     def fourth(self):
-        p, own = self.p, self.own
+        p, full, dtype = self.p, self.full, self.full.dtype
         for copy in self.stage:
             copy.wait_recv()
 
         def add(i):
             (l,) = i
-            self.line0[l, :, self.low] = plus(own[l, p.side, p.row, :, self.low], self.low2[l]).astype(own.dtype)
-            terms = [own[l, p.side, p.row, :, self.high]] + [self.high2[k, l] for k in range(p.rows - 1)]
-            self.line0[l, :, self.high] = plus(*terms).astype(own.dtype)
+            self.line0[l, :, self.low] = plus(full[l, p.side, p.row, p.core, :, self.low], self.low2[l]).astype(dtype)
+            terms = [full[l, p.side, p.row, p.core, :, self.high]] + [self.high2[k, l] for k in range(p.rows - 1)]
+            self.line0[l, :, self.high] = plus(*terms).astype(dtype)
 
         add_loop((p.lines,), add)
         self.stage = []
@@ -588,7 +586,6 @@
     low = c // 256 * 128
     high = c - low
     return [
-        pltpu.VMEM((lines, 2, rows, r, c), dtype),
         pltpu.VMEM((lines, 2, rows, r, c), dtype),
         pltpu.VMEM((max(rows - 1, 1), lines, 2, r, low), dtype),
         pltpu.VMEM((lines, rows, r, high), dtype),
@@ -599,41 +596,159 @@
     ]
 
 
-def scatter_kernel(count, lines, rows, *refs):
-    grads, outs = refs[:count], refs[count : 2 * count]
-    buffers = refs[2 * count : 2 * count + 8 * count]
-    send_sems, recv_sems, local_sems = refs[10 * count :]
+NBUF = 7
+
+
+def tile_loop(width, fn):
+    full = width // 256
+
+    def body(j, carry):
+        fn(pl.ds(pl.multiple_of(j * 256, 256), 256))
+        return carry
+
+    lax.fori_loop(0, full, body, 0)
+    if width % 256:
+        fn(pl.ds(full * 256, width % 256))
+
+
+def finish_kernel(lines, rows, products, given, *refs):
+    refs = list(refs)
+
+    def take(n):
+        out = refs[:n]
+        del refs[:n]
+        return out
+
+    number = len(products)
+    lefts, rights, ready = take(number), take(number), take(given)
+    count = number + given
+    outs = take(count)
+    fulls, buffers = take(count), take(count * NBUF)
+    xbuf, gbuf, xsem, gsem, ready_sem, send_sems, recv_sems = refs
     place = Place(lines, rows)
     place.greet()
     sends = Sends(send_sems, recv_sems)
-    parts = [Scatter(place, sends, grads[i], outs[i], buffers[8 * i : 8 * i + 8], local_sems.at[i]) for i in range(count)]
-    for part in parts:
-        part.begin()
-    for i in range(count + 3):
-        for lag, step in ((0, "second"), (1, "third"), (2, "fourth"), (3, "last")):
-            if 0 <= i - lag < count:
-                getattr(parts[i - lag], step)()
+    parts = [Scatter(place, sends, fulls[i], outs[i], buffers[NBUF * i : NBUF * (i + 1)]) for i in range(count)]
+    ready_copies = [pltpu.make_async_copy(ready[i], fulls[number + i], ready_sem.at[i]) for i in range(given)]
+    for copy in ready_copies:
+        copy.start()
+
+    core = place.core
+    tasks = []
+    for a, (kind, width) in enumerate(products):
+        if kind == "rows":
+            tasks.append((a, 0, None, None))
+        else:
+            for c in (1 - core, core):
+                for y in range(rows):
+                    pitch = rights[a].shape[1] // rows
+                    start = y * pitch + c * (pitch - width)
+                    tasks.append((a, start, y, c))
+
+    def fetch_right(t):
+        a, start, y, c = tasks[t]
+        width = products[a][1]
+        start = pl.multiple_of(jnp.int32(start), 128)
+        return pltpu.make_async_copy(rights[a].at[:, pl.ds(start, width)], gbuf.at[t % 2, :, pl.ds(0, width)], gsem.at[t % 2])
+
+    def fetch_left(a):
+        return pltpu.make_async_copy(lefts[a], xbuf.at[a % 2], xsem.at[a % 2])
+
+    fetch_left(0).start()
+    fetch_right(0).start()
+
+    def multiply(t):
+        a, start, y, c = tasks[t]
+        kind, width = products[a]
+        if t + 1 < len(tasks):
+            fetch_right(t + 1).start()
+            if tasks[t + 1][0] != a:
+                fetch_left(a + 1).start()
+        if t == 0 or tasks[t - 1][0] != a:
+            fetch_left(a).wait()
+        fetch_right(t).wait()
+        full = fulls[a]
+
+        def tile(cols):
+            block = dot_nn(xbuf[a % 2], gbuf[t % 2, :, cols])
+            n = block.shape[1]
+            if kind == "rows":
+                full[:, :, :, :, :, cols] = block.reshape(lines, 2, rows, 2, -1, n).astype(full.dtype)
+            else:
+                full[:, :, y, c, :, cols] = block.reshape(lines, 2, -1, n).astype(full.dtype)
+
+        tile_loop(width, tile)
+
+    order = [number + i for i in range(given)] + list(range(number))
+    pending = []
+
+    def advance():
+        for item in list(pending):
+            getattr(parts[item[0]], item[1].pop(0))()
+            if not item[1]:
+                pending.remove(item)
+
+    for i in range(given):
+        ready_copies[i].wait()
+        parts[number + i].begin()
+        pending.append((number + i, ["second", "third", "fourth", "last"]))
+    for t, (a, start, y, c) in enumerate(tasks):
+        multiply(t)
+        sent = products[a][0] == "rows" or (c is not core and y == rows - 1)
+        if sent:
+            parts[a].begin()
+        done = t + 1 == len(tasks) or tasks[t + 1][0] != a
+        if done or sent:
+            advance()
+        if done:
+            pending.append((a, ["second", "third", "fourth", "last"]))
+    while pending:
+        advance()
     sends.finish()
 
 
-def scatter_all(grads, collective_id):
+def finish(products, given, collective_id):
     wide, narrow = lax.axis_size("wide"), lax.axis_size("narrow")
     lines, rows = wide // 2, narrow // 2
-    count = len(grads)
+    shapes, plan = [], []
+    for left, right, kind in products:
+        m, n = left.shape[0], right.shape[1]
+        if kind == "rows":
+            width = n
+            shapes.append((lines, 2, rows, 2, m // (4 * lines * rows), n))
+        else:
+            width = -(-(n // (2 * rows)) // 128) * 128
+            shapes.append((lines, 2, rows, 2, m // (2 * lines), width))
+        plan.append((kind, width))
+    shapes += [g.shape for g in given]
+    count = len(shapes)
     copies = count * scatter_copies(lines, rows)
-    buffers = []
-    for g in grads:
-        buffers += scatter_buffers(lines, rows, g.shape[-2], g.shape[-1], g.dtype)
+    dtype = jnp.bfloat16
+    scratch = [pltpu.VMEM(s, dtype) for s in shapes]
+    for s in shapes:
+        scratch += scatter_buffers(lines, rows, s[-2], s[-1], dtype)
+    m, t = products[0][0].shape
+    widest = max(width for _, width in plan)
+    scratch += [
+        pltpu.VMEM((2, m, t), dtype),
+        pltpu.VMEM((2, t, widest), dtype),
+        pltpu.SemaphoreType.DMA((2,)),
+        pltpu.SemaphoreType.DMA((2,)),
+        pltpu.SemaphoreType.DMA((max(len(given), 1),)),
+        pltpu.SemaphoreType.DMA((copies,)),
+        pltpu.SemaphoreType.DMA((copies,)),
+    ]
+    ins = [p[0] for p in products] + [p[1] for p in products] + list(given)
     return pl.pallas_call(
-        functools.partial(scatter_kernel, count, lines, rows),
-        out_shape=[jax.ShapeDtypeStruct(g.shape[-2:], jnp.float32) for g in grads],
-        in_specs=[pl.BlockSpec(memory_space=pl.ANY)] * count,
+        functools.partial(finish_kernel, lines, rows, plan, len(given)),
+        out_shape=[jax.ShapeDtypeStruct(s[-2:], jnp.float32) for s in shapes],
+        in_specs=[pl.BlockSpec(memory_space=pl.ANY)] * len(ins),
         out_specs=[pl.BlockSpec(memory_space=pltpu.VMEM)] * count,
-        scratch_shapes=buffers + [pltpu.SemaphoreType.DMA((copies,)), pltpu.SemaphoreType.DMA((copies,)), pltpu.SemaphoreType.DMA((count,))],
+        scratch_shapes=scratch,
         compiler_params=pltpu.CompilerParams(collective_id=collective_id, has_side_effects=True, vmem_limit_bytes=60 * 2**20),
-        cost_estimate=pl.CostEstimate(flops=0, bytes_accessed=4 * 10**7, transcendentals=0),
-        name="scatter_grads",
-    )(*grads)
+        cost_estimate=pl.CostEstimate(flops=14 * 10**9, bytes_accessed=6 * 10**7, transcendentals=0),
+        name="finish",
+    )(*ins)
 
 
 def total_kernel(lines, rows, x_ref, o_ref, core_in, plane, line_in, send_sems, recv_sems):
@@ -755,12 +870,11 @@
         + stem_in.astype(jnp.float32)
     )
     joined = smooth(pre_joined).astype(jnp.bfloat16)
-    embedded = product(joined, full_embed).reshape(images, side * side, -1)
-    row_index = jnp.arange(rows, dtype=jnp.int32)[:, None]
-    start_rows = (
-        tokens.astype(jnp.float32).reshape(rows, length, -1).at[row_index, positions].add(embedded)
-    )
-    start = start_rows.reshape(rows * length, -1)
+    embedded = product(joined, full_embed)
+    first_at = positions[0, 0]
+    base = tokens.astype(jnp.float32)
+    covered = lax.dynamic_slice_in_dim(base, first_at, patch_count, 0) + embedded
+    start = lax.dynamic_update_slice_in_dim(base, covered, first_at, 0)
     normed0, unit0, inv0 = layer_norm(start, full_pre.astype(jnp.float32))
     normed0_low = normed0.astype(jnp.bfloat16)
     packed = product(normed0_low, full_qkv).astype(jnp.bfloat16)
@@ -785,15 +899,12 @@
         grad_narrowed, unit3, inv3, full_ffn.astype(jnp.float32)
     )
     grad_pre_up = smooth_back(pre_up, grad_activ).astype(jnp.bfloat16)
-    grad_w_down = product_tn(d_out, narrowed_low)
-    grad_w_up = product_tn(normed2_low, grad_pre_up)
     grad_normed2 = product_nt(grad_pre_up, full_up)
     grad_mid_in, grad_gain_mid = layer_norm_back(
         grad_normed2, unit2, inv2, full_mid.astype(jnp.float32)
     )
     grad_middle = grad_result + grad_mid_in
     grad_branch = grad_middle.astype(jnp.bfloat16)
-    grad_w_out = product_tn(mixed_low, grad_branch)
     grad_mixed_in = product_nt(grad_branch, full_out)
     grad_scaled, grad_gain_attn = layer_norm_back(
         grad_mixed_in, unit1, inv1, full_attn.astype(jnp.float32)
@@ -802,17 +913,12 @@
     grad_attended = (grad_scaled * scale_row).astype(jnp.bfloat16)
     grad_packed, grad_strips = attend_back(packed, grad_attended, attended, segments, bias, logsums, win)
     grad_table = table_from_strips(grad_strips)
-    grad_w_qkv = product_tn(normed0_low, grad_packed)
     grad_normed0 = product_nt(grad_packed, full_qkv)
     grad_start_in, grad_gain_pre = layer_norm_back(
         grad_normed0, unit0, inv0, full_pre.astype(jnp.float32)
     )
     grad_tokens = grad_middle + grad_start_in
-    grad_embedded = (
-        grad_tokens.reshape(rows, length, -1)[row_index, positions]
-        .reshape(patch_count, -1)
-        .astype(jnp.bfloat16)
-    )
+    grad_embedded = lax.dynamic_slice_in_dim(grad_tokens, first_at, patch_count, 0).astype(jnp.bfloat16)
     grad_w_embed = product_tn(joined, grad_embedded)
     grad_joined = product_nt(grad_embedded, full_embed)
     grad_pre_joined = smooth_back(pre_joined, grad_joined)
@@ -864,29 +970,16 @@
     def by_rows(grad):
         return grad.astype(jnp.bfloat16).reshape(lines, 2, planes, 2, -1, grad.shape[1])
 
-    def by_blocks(grad):
-        low = grad.astype(jnp.bfloat16).reshape(lines, 2, -1, planes, 2, grad.shape[1] // (2 * planes))
-        return low.transpose(0, 1, 3, 4, 2, 5)
-
-    def by_windows(grad):
-        low = grad.astype(jnp.bfloat16).reshape(lines, 2, -1, planes, grad.shape[1] // planes)
-        width = grad.shape[1] // (2 * planes)
-        window = -(-width // 128) * 128
-        span = 2 * width
-        pieces = [low[..., :window], low[..., span - window :]]
-        return jnp.stack(pieces, axis=4).transpose(0, 1, 3, 4, 2, 5)
-
-    grads = [
-        by_blocks(grad_w_down),
-        by_blocks(grad_w_up),
-        by_rows(grad_w_out),
-        by_windows(grad_w_qkv),
-        by_rows(grad_w_embed),
-        by_rows(grad_w_expand),
-        by_rows(grad_w_spatial),
-        by_rows(grad_w_reduce),
-    ]
-    sum_down, sum_up, sum_out, sum_qkv, sum_embed, sum_expand, sum_spatial, sum_reduce = scatter_all(grads, 2)
+    sum_down, sum_up, sum_qkv, sum_out, sum_embed, sum_expand, sum_spatial, sum_reduce = finish(
+        [
+            (d_out.T, narrowed_low, "blocks"),
+            (normed2_low.T, grad_pre_up, "blocks"),
+            (normed0_low.T, grad_packed, "blocks"),
+            (mixed_low.T, grad_branch, "rows"),
+        ],
+        [by_rows(grad_w_embed), by_rows(grad_w_expand), by_rows(grad_w_spatial), by_rows(grad_w_reduce)],
+        2,
+    )
     sum_down = sum_down.T
     width = 3 * D // (2 * planes)
     sum_qkv = jnp.where(

time: 682 us -> 569 us (0.83)
  local copies, waits for them, and re-layouts: 127 us -> 53.2 us
  matrix products: 126 us -> 94.3 us
    reshape x6 -> x0, local copies, waits for them, and re-layouts: 62.7 us -> none  [the longest x4 52.7 us: by_blocks(): grad.astype(jnp.bfloat16)]
    dot_general x8 -> x4, matrix products: 35.6 us -> 9.28 us  [product_tn(): lax.dot_general(lhs_matrix, rhs_matrix, (((0,), (0,)), ((), ())), preferr...]
    unnamed x168 -> x164, local copies, waits for them, and re-layouts: 26.8 us -> 17.3 us
    scatter-add x1 -> x0, other arithmetic: 9.34 us -> none  [local(): tokens.astype(jnp.float32).reshape(rows, length, -1)]
    gather x1 -> x0, local copies, waits for them, and re-layouts: 9.22 us -> none  [local(): grad_tokens.reshape(rows, length, -1)[row_index, positions]]
    dynamic_update_slice x0 -> x1, local copies, waits for them, and re-layouts: none -> 7.65 us  [local(): start = lax.dynamic_update_slice_in_dim(base, covered, first_at, 0)]
where the time goes in v2:
time: 569 us; the launch traced here: 562 us
  Pallas kernels  350 us (62%)
  matrix products  94.3 us (17%)
  other arithmetic  59.9 us (11%)
  local copies, waits for them, and re-layouts  53.2 us (9%)
    pallas_call x1, Pallas kernels, finish(): pl.pallas_call(functools.partial(finish_kernel, lines, rows, plan, len(gi...  104 us
    pallas_call x1, Pallas kernels, gather_all(): pl.pallas_call(functools.partial(gather_kernel, count, lines, rows), out_...  98.1 us
    pallas_call x1, Pallas kernels, attend_back(): pl.pallas_call(attend_back_kernel, out_shape=(jax.ShapeDtypeStruct((lengt...  64.7 us
    pallas_call x2, Pallas kernels, total_sum(): pl.pallas_call(functools.partial(total_kernel, lines, rows), out_shape=ja...  54.5 us
    dot_general x8, matrix products, product_nt(): lax.dot_general(lhs_matrix, rhs_matrix, (((1,), (1,)), ((), ())), preferr...  46.1 us
    dot_general x8, matrix products, product(): return jnp.dot(lhs_matrix, rhs_matrix, preferred_element_type=jnp.float32)  38.9 us
    pallas_call x1, Pallas kernels, attend(): pl.pallas_call(attend_kernel, out_shape=(jax.ShapeDtypeStruct((length, D)...  28.7 us
    unnamed x164, local copies, waits for them, and re-layouts  17.3 us

profile of v2, /device:TPU:0, one launch (start us, length us, event | category | flops | bytes accessed | tf_op | source)
XLA Modules:
  0.0 561.7 jit_solution(10237695232843853371)
XLA Ops:
  0.7 0.8 copy.100
  1.5 4.1 concatenate.55
  6.2 98.1 %gather_weights.1 = (bf16[4,2,2,2,16,256]{5,4,3,2,1,0:T(8,128)(2,1)}, bf16[4,2,2,2,32,256]{5,4,3,2,1,0:T(8,128)(2,1)}, bf16[4,2,2,2,72,256]{5,4,3,2,1,0:T(8,128)...) custom-call(bf16[16,256]{1,0:T(8,128)(2,1)} %reshape.446.refs_0_, ...), custom_call_target="tpu_custom_call" | custom-call | bytes 40000000 | tf_op jit(solution)/shard_map/gather_weights/pallas_call | solution.py:473
  104.4 2.8 multiply_convert_fusion.8
  107.7 1.2 copy-done.24
  108.9 0.8 fusion.54
  111.2 20.6 %total_sum.2 = f32[16,128]{1,0:T(8,128)} custom-call(f32[16,128]{1,0:T(8,128)} %pad_maximum_fusion.3.x_ref), custom_call_target="tpu_custom_call" | custom-call | bytes 1000000 | tf_op jit(solution)/shard_map/total_sum/pallas_call | solution.py:789
  133.1 1.0 copy.126
  134.2 0.7 copy-done.32
  135.6 0.8 reshape.471
  136.4 0.8 reshape.472
  137.2 2.3 multiply_convert_fusion.6
  139.5 1.2 slice.201
  142.6 1.8 convert_element_type.185
  144.8 2.3 dynamic-slice_add_fusion
  147.1 7.6 %dynamic_update_slice.3 = f32[1024,768]{1,0:T(8,128)S(1)} dynamic-update-slice(f32[1024,768]{1,0:T(8,128)S(1)} %convert_element_type.185, f32[576,768]{1,0:T(8,128)} %dynamic-slice_add_fusion, s32[]{:T(128)S(6)} %select_n.57, s32[]{:T(128)} %constant.98.clone.1) | dynamic-update-slice | bytes 3538948 | tf_op jit(solution)/shard_map/dynamic_update_slice | solution.py:877
  155.6 0.9 slice_convert_fusion.1
  156.6 7.8 %convolution_convert_fusion.packed = bf16[1024,2304]{1,0:T(8,128)(2,1)} fusion(bf16[768,2304]{1,0:T(8,128)(2,1)} %bitcast.216, f32[1024,768]{1,0:T(8,128)S(1)} %dynamic_update_slice.3, f32[768]{0:T(1024)S(1)} %reshape.473, f32[1024]{0:T(1024)S(1)} %add_rsqrt_fusion.3, f32[1024]{0:T(1024)S(1)} %broadcast_multiply_fusion.11), kind=kOutput, calls=%fused_computation.18 | convolution fusion | flops 3629383680 | bytes 11414528 | tf_op jit(solution)/shard_map/dot_general | solution.py:20
  164.4 0.9 slice_convert_fusion
  167.4 1.1 copy.103.segk
  168.5 1.0 copy-done.1
  169.5 28.7 %attend.1 = (f32[1024,768]{1,0:T(8,128)S(1)}, f32[8,6,256]{2,1,0:T(8,128)S(1)}, f32[6,5,128,256]{3,2,1,0:T(8,128)}) custom-call(s32[2,8]{1,0:T(2,128)S(1)} %pad_add_fusion.7.win, bf16[1024,2304]{1,0:T(8,128)(2,1)} %convolution_convert_fusion.packed, s32[1024,1]{1,0:T(8,128)S(1)} %copy-done.1, s32[1,1024]{1,0:T(1,128)S(1)} %copy-done.2, ...), custom_call_target="tpu_custom_call" | custom-call | flops 20000000000 | bytes 10000000 | tf_op jit(solution)/shard_map/attend/pallas_call | solution.py:196
  198.9 2.6 copy.104
  201.6 2.3 multiply_reduce_fusion.15
  204.0 2.4 multiply_reduce_fusion.10
  206.5 4.1 fusion.53
  210.6 1.6 copy-done.9
  212.8 11.1 %fusion.46 = (f32[1024]{0:T(1024)S(1)}, f32[1024,3072]{1,0:T(8,128)S(1)}) fusion(bf16[768,3072]{1,0:T(8,128)(2,1)} %bitcast.214, f32[1024,768]{1,0:T(8,128)} %copy-done.9, f32[768]{0:T(1024)S(1)} %reshape.476, f32[1024]{0:T(1024)S(1)} %add_rsqrt_fusion.1, f32[1024]{0:T(1024)S(1)} %broadcast_multiply_fusion.9), kind=kOutput, calls=%fused_computation.204 | convolution fusion | flops 4863294464 | bytes 20462592 | tf_op jit(solution)/shard_map/dot_general | solution.py:20
  224.0 5.6 multiply_reduce_fusion.1
  229.7 16.9 %fusion.7 = (f32[3072]{0:T(1024)S(1)}, f32[1024]{0:T(1024)S(1)}, f32[1024]{0:T(1024)S(1)}, f32[3072,1024]{0,1:T(8,128)}) fusion(f32[1024]{0:T(1024)S(1)} %add_rsqrt_fusion, f32[1024]{0:T(1024)S(1)} %broadcast_multiply_fusion.2, f32[1024,3072]{1,0:T(8,128)} %copy-done.8, f32[3072]{0:T(1024)S(1)} %reshape.477, bf16[3072,768]{1,0:T(8,128)(2,1)} %bitcast.212, ...), kind=kOutput, calls=%fused_computation.11 | convolution fusion | flops 4882164736 | bytes 31498240 | tf_op jit(solution)/shard_map/dot_general | solution.py:30
  246.6 16.5 %fusion.6 = (bf16[1024,3072]{1,0:T(8,128)(2,1)S(1)}, bf16[1024,3072]{1,0:T(8,128)(2,1)}) fusion(f32[1024,3072]{1,0:T(8,128)S(1)} %bitcast.175, f32[3072,1024]{0,1:T(8,128)} %get-tuple-element.142, f32[1024]{0:T(1024)S(1)} %broadcast_multiply_fusion, f32[1024]{0:T(1024)S(1)} %broadcast_multiply_fusion.1, f32[3072]{0:T(1024)S(1)} %reshape.477, ...), kind=kLoop, calls=%fused_computation.8 | loop fusion | flops 94371840 | bytes 37777408 | tf_op jit(solution)/shard_map/convert_element_type | solution.py:901
  263.1 9.7 %fusion.55 = f32[1024,768]{1,0:T(8,128)S(1)} fusion(bf16[1024,3072]{1,0:T(8,128)(2,1)S(1)} %get-tuple-element.88.refs_5_, bf16[768,3072]{1,0:T(8,128)(2,1)} %bitcast.215), kind=kOutput, calls=%fused_computation.213 | convolution fusion | flops 4831838208 | bytes 14155776 | tf_op jit(solution)/shard_map/dot_general | solution.py:30
  272.9 2.8 multiply_reduce_fusion.3
  275.7 2.5 fusion.49
  278.2 0.8 copy-done.23
  279.0 1.6 multiply_reduce_fusion.13
  280.7 3.4 multiply_reduce_fusion.2
  284.1 2.6 copy.107.grads
  286.7 64.7 %attend_back.1 = (bf16[1024,2304]{1,0:T(8,128)(2,1)}, f32[12,5,256]{2,1,0:T(8,128)}) custom-call(s32[2,8]{1,0:T(2,128)} %copy-done.3, bf16[1024,2304]{1,0:T(8,128)(2,1)} %convolution_convert_fusion.packed, bf16[1024,768]{1,0:T(8,128)(2,1)} %copy.107.grads, f32[1024,768]{1,0:T(8,128)} %copy-done, s32[1024,1]{1,0:T(8,128)} %copy.103.segk, s32[1,1024]{1,0:T(1,128)} %segq.3, ...), custom_call_target="tpu_custom_call" | custom-call | flops 49999998976 | bytes 20000000 | tf_op jit(solution)/shard_map/attend_back/pallas_call | solution.py:300
  351.4 1.2 slice_reduce_fusion.1
  352.9 0.9 copy.110
  354.6 7.0 %fusion.56 = f32[1024,768]{1,0:T(8,128)S(1)} fusion(bf16[1024,2304]{1,0:T(8,128)(2,1)} %get-tuple-element.53.refs_6_, bf16[768,2304]{1,0:T(8,128)(2,1)} %bitcast.217), kind=kOutput, calls=%fused_computation.214 | convolution fusion | flops 3623878656 | bytes 11403264 | tf_op jit(solution)/shard_map/dot_general | solution.py:30
  361.6 2.8 multiply_reduce_fusion.5
  364.6 3.6 multiply_add_fusion
  368.9 4.2 fusion.47
  374.0 34.0 %total_sum.3 = f32[88,128]{1,0:T(8,128)} custom-call(f32[88,128]{1,0:T(8,128)} %pad_bitcast_fusion.x_ref), custom_call_target="tpu_custom_call" | custom-call | bytes 1000000 | tf_op jit(solution)/shard_map/total_sum/pallas_call | solution.py:789
  408.0 0.8 multiply_multiply_fusion.10
  408.8 2.3 multiply_convert_fusion.5
  411.1 2.0 fusion.29
  413.1 2.2 convolution_convert_fusion.1
  415.3 1.5 convolution_convert_fusion.4
  416.8 4.2 convolution_convert_fusion.2
  421.0 0.9 convolution_bitcast_fusion
  423.9 1.4 fusion.15
  425.3 2.0 copy.117
  427.4 1.9 copy.119.refs_2_
  429.2 1.6 copy.118.refs_1_
  430.8 1.6 copy.116
  432.5 104.1 %finish.1 = (f32[96,768]{1,0:T(8,128)}, f32[96,768]{1,0:T(8,128)}, f32[96,640]{1,0:T(8,128)}, f32[24,768]{1,0:T(8,128)}, f32[32,768]{1,0:T(8,128)}, /*index=5*/f...) custom-call(bf16[768,1024]{1,0:T(8,128)(2,1)} %bitcast.177, bf16[768,1024]{1,0:T(8,128)(2,1)} %copy.118.refs_1_, ...), custom_call_target="tpu_custom_call" | custom-call | flops 14000000000 | bytes 60000000 | tf_op jit(solution)/shard_map/finish/pallas_call | solution.py:742
  536.6 2.0 slice_select_fusion
  538.6 3.8 convolution_add_fusion.1
  547.2 9.5 %add_convert_fusion = bf16[1024,768]{1,0:T(8,128)(2,1)} fusion(f32[1024,768]{1,0:T(8,128)S(1)} %copy-done.11, bf16[1024,3072]{1,0:T(8,128)(2,1)} %get-tuple-element.89.refs_4_, bf16[3072,768]{1,0:T(8,128)(2,1)} %bitcast.213), kind=kOutput, calls=%fused_computation.34 | convolution fusion | flops 4833411072 | bytes 15728640 | tf_op jit(solution)/shard_map/dot_general | solution.py:20
  557.3 0.7 copy.154
  558.1 0.7 copy.155
  (249 shorter events, 22.3 us)
Async XLA Ops:
  107.4 1.4 copy-start.24
  107.7 2.0 copy-start.51
  108.8 1.0 copy-start.60
  109.7 27.4 %copy-start.26 = (bf16[1,24,24,1024]{3,2,1,0:T(8,128)(2,1)S(1)}, bf16[1,24,24,1024]{3,2,1,0:T(8,128)(2,1)}, u32[]{:S(2)}) copy-start(bf16[1,24,24,1024]{3,2,1,0:T(8,128)(2,1)} %param.22) | copy-start | bytes 3538948
  110.6 31.4 %copy-start.13 = (f32[576,1024]{1,0:T(8,128)}, f32[576,1024]{1,0:T(8,128)S(1)}, u32[]{:S(2)}) copy-start(f32[576,1024]{1,0:T(8,128)S(1)} %get-tuple-element.137) | copy-start | bytes 7077892
  132.5 14.7 %copy-start.43 = (f32[1024]{0:T(1024)}, f32[1024]{0:T(1024)S(1)}, u32[]{:S(2)}) copy-start(f32[1024]{0:T(1024)S(1)} %fusion.38) | copy-start | bytes 12292
  133.1 14.0 %copy-start.47 = (f32[1024]{0:T(1024)}, f32[1024]{0:T(1024)S(1)}, u32[]{:S(2)}) copy-start(f32[1024]{0:T(1024)S(1)} %multiply_bitcast_fusion) | copy-start | bytes 12292
  136.4 8.0 %copy-start.41 = (f32[1024]{0:T(1024)}, f32[1024]{0:T(1024)S(1)}, u32[]{:S(2)}) copy-start(f32[1024]{0:T(1024)S(1)} %reshape.471) | copy-start | bytes 12292
  137.2 7.2 %copy-start.55 = (f32[1024]{0:T(1024)}, f32[1024]{0:T(1024)S(1)}, u32[]{:S(2)}) copy-start(f32[1024]{0:T(1024)S(1)} %reshape.472) | copy-start | bytes 12292
  142.6 1.8 copy-start.29
  142.6 2.2 copy-start.58
  154.8 1.8 copy-start.5
  155.0 9.4 %copy-start.39 = (f32[1024]{0:T(1024)}, f32[1024]{0:T(1024)S(1)}, u32[]{:S(2)}) copy-start(f32[1024]{0:T(1024)S(1)} %broadcast_multiply_fusion.11) | copy-start | bytes 12292
  155.6 8.8 %copy-start.49 = (f32[1024]{0:T(1024)}, f32[1024]{0:T(1024)S(1)}, u32[]{:S(2)}) copy-start(f32[1024]{0:T(1024)S(1)} %add_rsqrt_fusion.3) | copy-start | bytes 12292
  156.6 7.8 %copy-start.45 = (f32[768]{0:T(1024)}, f32[768]{0:T(1024)S(1)}, u32[]{:S(2)}) copy-start(f32[768]{0:T(1024)S(1)} %reshape.473) | copy-start | bytes 9220
  156.6 10.3 %copy-start.2 = (s32[1,1024]{1,0:T(1,128)S(1)}, s32[1,1024]{1,0:T(1,128)}, u32[]{:S(2)}) copy-start(s32[1,1024]{1,0:T(1,128)} %segq.3) | copy-start | bytes 12292
  167.4 30.9 %copy-start.3 = (s32[2,8]{1,0:T(2,128)}, s32[2,8]{1,0:T(2,128)S(1)}, u32[]{:S(2)}) copy-start(s32[2,8]{1,0:T(2,128)S(1)} %pad_add_fusion.7.win) | copy-start | bytes 196
  168.5 1.0 copy-start.1
  198.9 2.6 copy-start
  198.9 2.6 copy-start.57
  201.6 4.8 copy-start.6
  210.6 1.6 copy-start.9
  223.9 5.6 copy-start.8
  229.6 16.9 %slice-start = ((s8[12582912]{0:T(1024)(128)(4,1)}), s8[4194304]{0:T(1024)(128)(4,1)S(1)}, s32[]{:S(2)}) async-start(s8[12582912]{0:T(1024)(128)(4,1)} %bitcast.174), calls=%async_computation | async-start | bytes 8388608
  229.6 16.9 %slice-start.1 = ((s8[12582912]{0:T(1024)(128)(4,1)}), s8[4194304]{0:T(1024)(128)(4,1)S(1)}, s32[]{:S(2)}) async-start(s8[12582912]{0:T(1024)(128)(4,1)} %bitcast.174), calls=%async_computation.1 | async-start | bytes 8388608
  229.6 16.9 %slice-start.2 = ((s8[12582912]{0:T(1024)(128)(4,1)}), s8[4194304]{0:T(1024)(128)(4,1)S(1)}, s32[]{:S(2)}) async-start(s8[12582912]{0:T(1024)(128)(4,1)} %bitcast.174), calls=%async_computation.2 | async-start | bytes 8388608
  263.1 9.7 %copy-start.16 = (bf16[1024,3072]{1,0:T(8,128)(2,1)}, bf16[1024,3072]{1,0:T(8,128)(2,1)S(1)}, u32[]{:S(2)}) copy-start(bf16[1024,3072]{1,0:T(8,128)(2,1)S(1)} %get-tuple-element.88.refs_5_) | copy-start | bytes 18874372
  263.1 9.7 %copy-start.10 = (f32[1024,768]{1,0:T(8,128)S(1)}, f32[1024,768]{1,0:T(8,128)}, u32[]{:S(2)}) copy-start(f32[1024,768]{1,0:T(8,128)} %copy-done.9) | copy-start | bytes 9437188
  272.9 2.8 copy-start.19
  275.7 2.5 copy-start.7
  275.7 3.3 copy-start.23
  278.2 2.5 copy-start.22
  354.6 7.0 %copy-start.40 = (f32[1024]{0:T(1024)S(1)}, f32[1024]{0:T(1024)}, u32[]{:S(2)}) copy-start(f32[1024]{0:T(1024)} %copy-done.39) | copy-start | bytes 12292
  354.6 7.0 %copy-start.46 = (f32[768]{0:T(1024)S(1)}, f32[768]{0:T(1024)}, u32[]{:S(2)}) copy-start(f32[768]{0:T(1024)} %copy-done.45) | copy-start | bytes 9220
  354.6 7.1 %copy-start.50 = (f32[1024]{0:T(1024)S(1)}, f32[1024]{0:T(1024)}, u32[]{:S(2)}) copy-start(f32[1024]{0:T(1024)} %copy-done.49) | copy-start | bytes 12292
  361.6 2.8 copy-start.12
  364.5 3.6 copy-start.14
  364.5 3.8 copy-start.27
  364.5 3.8 copy-start.42
  364.5 3.8 copy-start.44
  364.5 3.8 copy-start.48
  364.6 3.8 copy-start.56
  364.6 4.3 copy-start.59
  368.9 4.3 copy-start.21
  368.9 39.9 %copy-start.15 = (f32[576,1024]{1,0:T(8,128)S(1)}, f32[576,1024]{1,0:T(8,128)}, u32[]{:S(2)}) copy-start(f32[576,1024]{1,0:T(8,128)} %copy-done.13) | copy-start | bytes 7077892
  373.2 37.9 %copy-start.61 = (bf16[4,2,2,2,8,1024]{5,4,3,2,1,0:T(8,128)(2,1)S(1)}, bf16[4,2,2,2,8,1024]{5,4,3,2,1,0:T(8,128)(2,1)}, u32[]{:S(2)}) copy-start(bf16[4,2,2,2,8,1024]{5,4,3,2,1,0:T(8,128)(2,1)} %get-tuple-element.43) | copy-start | bytes 1572868
  411.1 2.0 copy-start.52
  413.1 2.2 copy-start.63
  415.3 1.5 copy-start.30
  416.8 4.2 copy-start.25
  422.4 1.1 copy-start.31
  422.6 1.3 copy-start.28
  423.0 4.3 copy-start.18
  423.9 5.3 copy-start.17
  429.2 1.6 copy-start.20
  536.6 5.8 %copy-start.35 = (f32[88,128]{1,0:T(8,128)S(1)}, f32[88,128]{1,0:T(8,128)}, u32[]{:S(2)}) copy-start(f32[88,128]{1,0:T(8,128)} %total_sum.3) | copy-start | bytes 135172
  536.6 10.6 %copy-start.11 = (f32[1024,768]{1,0:T(8,128)S(1)}, f32[1024,768]{1,0:T(8,128)}, u32[]{:S(2)}) copy-start(f32[1024,768]{1,0:T(8,128)} %copy-done.9) | copy-start | bytes 9437188
  547.2 9.5 %copy-start.38 = (f32[24,768]{1,0:T(8,128)S(1)}, f32[24,768]{1,0:T(8,128)}, u32[]{:S(2)}) copy-start(f32[24,768]{1,0:T(8,128)} %get-tuple-element.170) | copy-start | bytes 221188
  547.2 10.1 %copy-start.34 = (f32[96,768]{1,0:T(8,128)S(1)}, f32[96,768]{1,0:T(8,128)}, u32[]{:S(2)}) copy-start(f32[96,768]{1,0:T(8,128)} %get-tuple-element.171) | copy-start | bytes 884740
  547.2 10.9 %copy-start.33 = (f32[96,768]{1,0:T(8,128)S(1)}, f32[96,768]{1,0:T(8,128)}, u32[]{:S(2)}) copy-start(f32[96,768]{1,0:T(8,128)} %get-tuple-element.58) | copy-start | bytes 884740
  547.2 11.6 %copy-start.54 = (f32[32,256]{1,0:T(8,128)S(1)}, f32[32,256]{1,0:T(8,128)}, u32[]{:S(2)}) copy-start(f32[32,256]{1,0:T(8,128)} %get-tuple-element.179) | copy-start | bytes 98308
  547.2 12.2 %copy-start.37 = (f32[72,256]{1,0:T(8,128)S(1)}, f32[72,256]{1,0:T(8,128)}, u32[]{:S(2)}) copy-start(f32[72,256]{1,0:T(8,128)} %get-tuple-element.180) | copy-start | bytes 221188
  547.2 12.8 %copy-start.53 = (f32[8,1024]{1,0:T(8,128)S(1)}, f32[8,1024]{1,0:T(8,128)}, u32[]{:S(2)}) copy-start(f32[8,1024]{1,0:T(8,128)} %get-tuple-element.181) | copy-start | bytes 98308
  547.2 13.4 %copy-start.36 = (f32[32,768]{1,0:T(8,128)S(1)}, f32[32,768]{1,0:T(8,128)}, u32[]{:S(2)}) copy-start(f32[32,768]{1,0:T(8,128)} %get-tuple-element.182) | copy-start | bytes 294916
  (3 other events, 2.2 us)

commit v3 on v2

--- a/solution.py
+++ b/solution.py
@@ -361,11 +361,14 @@
     def row_source(self, k):
         return lax.rem(self.row + self.rows - k, self.rows)
 
+    def plane_peers(self):
+        steps = [(k // self.rows, k % self.rows) for k in range(1, 2 * self.rows)]
+        return [self.device(side=lax.rem(self.side + a, 2), row=self.row_peer(b)) for a, b in steps]
+
     def greet(self):
         barrier = pltpu.get_barrier_semaphore()
         targets = [self.device(line=self.line_peer(k)) for k in range(1, self.lines)]
-        targets += [self.device(row=self.row_peer(k)) for k in range(1, self.rows)]
-        targets += [self.device(side=1 - self.side), self.device(core=1 - self.core)]
+        targets += self.plane_peers() + [self.device(core=1 - self.core)]
         for target in targets:
             pl.semaphore_signal(barrier, inc=1, device_id=target, device_id_type=MESH)
         pl.semaphore_wait(barrier, len(targets))
@@ -395,20 +398,20 @@
 
 
 class Gather:
-    def __init__(self, place, sends, shard, out, local_sem):
+    def __init__(self, place, sends, shard, out, local_sem, at, width):
         self.p, self.s, self.shard, self.out = place, sends, shard, out
         self.local_sem = local_sem
-        cols = out.shape[-1]
-        cut = cols // 256 * 128
-        self.low, self.high = pl.ds(0, cut), pl.ds(cut, cols - cut)
+        cut = width // 256 * 128
+        self.every, self.low, self.high = pl.ds(at, width), pl.ds(at, cut), pl.ds(at + cut, width - cut)
         self.cores = []
 
     def begin(self):
         p = self.p
-        mine = self.out.at[p.line, p.side, p.row, p.core]
-        self.local = pltpu.make_async_copy(self.shard, mine, self.local_sem)
+        mine = self.out.at[p.line, p.side, p.row, p.core, :, self.every]
+        shard = self.shard.at[:, self.every]
+        self.local = pltpu.make_async_copy(shard, mine, self.local_sem)
         self.local.start()
-        self.stage = [self.s.start(self.shard, mine, p.device(line=p.line_peer(k))) for k in range(1, p.lines)]
+        self.stage = [self.s.start(shard, mine, p.device(line=p.line_peer(k))) for k in range(1, p.lines)]
 
     def across(self, src):
         self.cores.append(self.s.start(src, src, self.p.device(core=1 - self.p.core)))
@@ -422,7 +425,7 @@
         high = out.at[:, p.side, p.row, p.core, :, self.high]
         self.stage = [self.s.start(low, low, p.device(side=1 - p.side))]
         self.stage += [self.s.start(high, high, p.device(row=p.row_peer(k))) for k in range(1, p.rows)]
-        self.across(out.at[:, p.side, p.row, p.core])
+        self.across(out.at[:, p.side, p.row, p.core, :, self.every])
 
     def third(self):
         p, out = self.p, self.out
@@ -449,38 +452,285 @@
             copy.wait_recv()
 
 
-def gather_kernel(count, lines, rows, *refs):
-    shards, outs = refs[:count], refs[count : 2 * count]
-    send_sems, recv_sems, local_sems = refs[2 * count :]
+class Total:
+    def __init__(self, place, sends, x, core_in, plane, line_in):
+        self.p, self.s, self.x, self.core_in, self.plane, self.line_in = place, sends, x, core_in, plane, line_in
+
+    def begin(self):
+        p = self.p
+        self.stage = [self.s.start(self.x, self.core_in, p.device(core=1 - p.core))]
+
+    def second(self):
+        p = self.p
+        for copy in self.stage:
+            copy.wait_recv()
+        here = p.side * p.rows + p.row
+        self.plane[here] = self.x[...] + self.core_in[...]
+        self.stage = [self.s.start(self.plane.at[here], self.plane.at[here], t) for t in p.plane_peers()]
+
+    def third(self):
+        p = self.p
+        for copy in self.stage:
+            copy.wait_recv()
+        total = self.plane[0]
+        for k in range(1, 2 * p.rows):
+            total = total + self.plane[k]
+        self.line_in[p.line] = total
+        mine = self.line_in.at[p.line]
+        self.stage = [self.s.start(mine, mine, p.device(line=p.line_peer(k))) for k in range(1, p.lines)]
+
+    def last(self):
+        for copy in self.stage:
+            copy.wait_recv()
+        total = self.line_in[0]
+        for k in range(1, self.p.lines):
+            total = total + self.line_in[k]
+        return total
+
+
+def total_buffers(lines, rows, shape, dtype):
+    return [
+        pltpu.VMEM(shape, dtype),
+        pltpu.VMEM(shape, dtype),
+        pltpu.VMEM((2 * rows,) + shape, dtype),
+        pltpu.VMEM((lines,) + shape, dtype),
+    ]
+
+
+def total_copies(lines, rows):
+    return 2 * rows + lines - 1
+
+
+def gelu(v):
+    return 0.5 * v * (1.0 + jnp.tanh(0.7978845608028654 * (v + 0.044715 * (v * v * v))))
+
+
+def spread(vector, me, total):
+    n = vector.shape[1]
+    lane = lax.broadcasted_iota(jnp.int32, (n, total), 1)
+    row = lax.broadcasted_iota(jnp.int32, (n, total), 0)
+    hot = jnp.where(lane == me * n + row, 1.0, 0.0).astype(jnp.bfloat16)
+    return dot_nn(vector, hot)
+
+
+def matrix(ref):
+    block = ref[...].astype(jnp.float32)
+    return block.reshape(-1, block.shape[-1]).astype(jnp.bfloat16)
+
+
+def shifted(values, row_off, col_off, side):
+    count = values.shape[0]
+    step = row_off * side + col_off
+    moved = pltpu.roll(values, (-step) % count, 0) if step % count else values
+    patch = lax.broadcasted_iota(jnp.int32, (count, 1), 0)
+    row, col = patch // side + row_off, lax.rem(patch, side) + col_off
+    inside = (row >= 0) & (row < side) & (col >= 0) & (col < side)
+    return jnp.where(inside, moved, 0.0)
+
+
+FRONT_VECTORS = 7
+
+
+def front_kernel(lines, rows, side, whole, pieces, number, *refs):
+    refs = list(refs)
+
+    def take(n):
+        out = refs[:n]
+        del refs[:n]
+        return out
+
+    (at,) = take(1)
+    vectors = take(FRONT_VECTORS)
+    (stem, tokens) = take(2)
+    shards = take(number)
+    outs = take(number)
+    (gains, pre_first, columns, pre_second, second, unit, inv, joined, start, normed, packed) = take(11)
+    mats = take(5)
+    (placing,) = take(1)
+    held_bufs, sum_bufs = take(4), take(4)
+    send_sems, recv_sems, local_sems = take(3)
     place = Place(lines, rows)
     place.greet()
     sends = Sends(send_sems, recv_sems)
-    parts = [Gather(place, sends, shards[i], outs[i], local_sems.at[i]) for i in range(count)]
-    for part in parts:
+
+    me = (place.line * 2 + place.side) * (2 * rows) + place.row * 2 + place.core
+    held = held_bufs[0]
+    held[...] = jnp.zeros_like(held)
+    devices = 4 * lines * rows
+
+    parts = []
+    for i, (which, col, width) in enumerate(pieces):
+        parts.append(Gather(place, sends, shards[which], outs[which], local_sems.at[i], col, width))
+    parts[0].begin()
+    parts[1].begin()
+    for v, (ref, row) in enumerate(zip(vectors[:6], (2, 3, 4, 5, 0, 1))):
+        n = ref.shape[1]
+        line = spread(ref[...], me, n * devices).astype(jnp.bfloat16)
+        for k in range(0, n * devices, 1024):
+            span = min(1024, n * devices - k)
+            held[pl.ds(row + k // 1024, 1), pl.ds(0, span)] = line[:, k : k + span]
+    table = spread(vectors[6][...], me, vectors[6].shape[1] * devices).astype(jnp.bfloat16)
+    for h in range(HEADS):
+        held[pl.ds(8 + h // 4, 1), pl.ds(h % 4 * 256, 256)] = table[h : h + 1, :]
+    vector_total = Total(place, sends, *held_bufs)
+    vector_total.begin()
+    for part in parts[2:]:
         part.begin()
-    for i in range(count + 3):
-        for lag, step in ((0, "second"), (1, "third"), (2, "fourth"), (3, "last")):
-            if 0 <= i - lag < count:
-                getattr(parts[i - lag], step)()
+
+    steps = []
+    for i in range(len(parts) + 3):
+        for lag, name in ((0, "second"), (1, "third"), (2, "fourth"), (3, "last")):
+            if 0 <= i - lag < len(parts):
+                steps.append((i - lag, name))
+
+    def pump(n=None, until=None):
+        while steps and (n is None or n > 0):
+            i, name = steps.pop(0)
+            getattr(parts[i], name)()
+            n = None if n is None else n - 1
+            if until is not None and (i, name) == (until, "last"):
+                break
+
+    pump(2)
+    vector_total.second()
+    pump(2)
+    vector_total.third()
+    pump(until=0)
+    count = side * side
+    w_reduce, w_spatial, w_expand, w_embed, w_qkv = mats
+    w_reduce[...] = matrix(outs[0])
+    pre = dot_nn(stem[...], w_reduce[...])
+    pre_first[...] = pre
+    first = gelu(pre).astype(jnp.bfloat16).astype(jnp.float32)
+    channels = first.shape[1]
+    for r in range(3):
+        for c in range(3):
+            k = r * 3 + c
+            columns[:, pl.ds(k * channels, channels)] = shifted(first, r - 1, c - 1, side).astype(jnp.bfloat16)
+    pump(until=1)
+    w_spatial[...] = matrix(outs[1])
+    pre = dot_nn(columns[...], w_spatial[...])
+    pre_second[...] = pre
+    second[...] = gelu(pre).astype(jnp.bfloat16)
+    pump(until=2)
+    w_expand[...] = matrix(outs[2])
+    sums = sum_bufs[0]
+    sums[...] = jnp.zeros_like(sums)
+
+    def expand(cols):
+        third = dot_nn(second[...], w_expand[:, cols])
+        unit[:, cols] = third
+        sums[pl.ds(0, 1), cols] = jnp.sum(third, axis=0, keepdims=True)
+        sums[pl.ds(1, 1), cols] = jnp.sum(third * third, axis=0, keepdims=True)
+
+    tile_loop(unit.shape[1], expand)
+    norm_total = Total(place, sends, *sum_bufs)
+    norm_total.begin()
+    pump(2)
+    norm_total.second()
+    gains[...] = vector_total.last().astype(jnp.float32)
+    pump(until=3)
+    norm_total.third()
+    w_embed[...] = matrix(outs[3])
+    pump(1)
+    totals = norm_total.last()
+    mean = totals[0:1] / whole
+    inv_std = lax.rsqrt(totals[1:2] / whole - mean * mean + epsilon)
+    inv[...] = jnp.broadcast_to(inv_std, inv.shape)
+
+    third_rows = count // 3
+
+    def join(i, carry):
+        at_rows = pl.ds(pl.multiple_of(i * third_rows, third_rows), third_rows)
+        value = (unit[at_rows, :] - mean) * inv_std
+        unit[at_rows, :] = value
+        pre_joined = value * gains[0:1, :] + gains[1:2, :] + stem[at_rows, :].astype(jnp.float32)
+        joined[at_rows, :] = gelu(pre_joined).astype(jnp.bfloat16)
+        return carry
+
+    lax.fori_loop(0, 3, join, 0)
+    length, width = start.shape
+    token = lax.broadcasted_iota(jnp.int32, (length, count), 0)
+    patch = lax.broadcasted_iota(jnp.int32, (length, count), 1)
+    placing[...] = jnp.where(token - patch == at[0], 1.0, 0.0).astype(jnp.bfloat16)
+
+    def embed(cols):
+        value = dot_nn(joined[...], w_embed[:, cols])
+        high = value.astype(jnp.bfloat16)
+        low = (value - high.astype(jnp.float32)).astype(jnp.bfloat16)
+        moved = dot_nn(placing[...], high) + dot_nn(placing[...], low)
+        start[:, cols] = tokens[:, cols].astype(jnp.float32) + moved
+
+    tile_loop(width, embed)
+    gain = gains[2:3, :width]
+
+    def norm(i, carry):
+        at_rows = pl.ds(pl.multiple_of(i * 128, 128), 128)
+        value = start[at_rows, :]
+        centred = value - jnp.mean(value, axis=-1, keepdims=True)
+        scale = lax.rsqrt(jnp.mean(centred * centred, axis=-1, keepdims=True) + epsilon)
+        normed[at_rows, :] = (centred * scale * gain).astype(jnp.bfloat16)
+        return carry
+
+    lax.fori_loop(0, length // 128, norm, 0)
+    pump(until=4)
+    w_qkv[...] = matrix(outs[4])
+
+    def project(cols):
+        packed[:, cols] = dot_nn(normed[...], w_qkv[:, cols]).astype(jnp.bfloat16)
+
+    tile_loop(packed.shape[1], project)
+    pump()
     sends.finish()
 
 
-def gather_all(shards, collective_id):
+def front(first_at, vectors, stem, tokens, shards, side, collective_id):
     wide, narrow = lax.axis_size("wide"), lax.axis_size("narrow")
     lines, rows = wide // 2, narrow // 2
-    count = len(shards)
-    copies = count * gather_copies(lines, rows)
-    outs = pl.pallas_call(
-        functools.partial(gather_kernel, count, lines, rows),
-        out_shape=[jax.ShapeDtypeStruct((lines, 2, rows, 2) + s.shape, s.dtype) for s in shards],
-        in_specs=[pl.BlockSpec(memory_space=pl.ANY)] * count,
-        out_specs=[pl.BlockSpec(memory_space=pl.ANY)] * count,
-        scratch_shapes=[pltpu.SemaphoreType.DMA((copies,)), pltpu.SemaphoreType.DMA((copies,)), pltpu.SemaphoreType.DMA((count,))],
-        compiler_params=pltpu.CompilerParams(collective_id=collective_id, has_side_effects=True),
-        cost_estimate=pl.CostEstimate(flops=0, bytes_accessed=4 * 10**7, transcendentals=0),
-        name="gather_weights",
-    )(*shards)
-    return outs
+    devices = wide * narrow
+    number = len(shards)
+    pieces = []
+    for i, s in enumerate(shards):
+        cuts = 2 if i >= 6 else 1
+        for k in range(cuts):
+            pieces.append((i, k * s.shape[1] // cuts, s.shape[1] // cuts))
+    copies = len(pieces) * gather_copies(lines, rows) + 2 * total_copies(lines, rows)
+    count, length = side * side, tokens.shape[0]
+    mid = shards[0].shape[1]
+    wide_in = stem.shape[1]
+    f32, bf16 = jnp.float32, jnp.bfloat16
+    gathered = [jax.ShapeDtypeStruct((lines, 2, rows, 2) + s.shape, s.dtype) for s in shards]
+    kept = [
+        ((16, 1024), f32),
+        ((count, mid), f32),
+        ((count, 9 * mid), bf16),
+        ((count, mid), f32),
+        ((count, mid), bf16),
+        ((count, wide_in), f32),
+        ((8, wide_in), f32),
+        ((count, wide_in), bf16),
+        ((length, D), f32),
+        ((length, D), bf16),
+        ((length, 3 * D), bf16),
+    ]
+    vmem = pl.BlockSpec(memory_space=pltpu.VMEM)
+    anywhere = pl.BlockSpec(memory_space=pl.ANY)
+    scratch = [pltpu.VMEM((s.shape[0] * devices, s.shape[1]), bf16) for s in shards[:5]]
+    scratch += [pltpu.VMEM((length, count), bf16)]
+    scratch += total_buffers(lines, rows, (16, 1024), bf16)
+    scratch += total_buffers(lines, rows, (8, 1024), f32)
+    scratch += [pltpu.SemaphoreType.DMA((copies,)), pltpu.SemaphoreType.DMA((copies,)), pltpu.SemaphoreType.DMA((len(pieces),))]
+    results = pl.pallas_call(
+        functools.partial(front_kernel, lines, rows, side, float(count * devices), pieces, number),
+        out_shape=gathered + [jax.ShapeDtypeStruct(s, d) for s, d in kept],
+        in_specs=[pl.BlockSpec(memory_space=pltpu.SMEM)] + [vmem] * (FRONT_VECTORS + 2) + [anywhere] * number,
+        out_specs=[vmem] * 5 + [anywhere] * (number - 5) + [vmem] * len(kept),
+        scratch_shapes=scratch,
+        compiler_params=pltpu.CompilerParams(collective_id=collective_id, has_side_effects=True, vmem_limit_bytes=60 * 2**20),
+        cost_estimate=pl.CostEstimate(flops=6 * 10**9, bytes_accessed=7 * 10**7, transcendentals=10**6),
+        name="front",
+    )(first_at, *vectors, stem, tokens, *shards)
+    return results[:number], results[number:]
 
 
 def scatter_copies(lines, rows):
@@ -830,54 +1080,33 @@
     both = ("wide", "narrow")
     devices = lax.axis_size(both)
     me = lax.axis_index("wide") * lax.axis_size("narrow") + lax.axis_index("narrow")
-    vectors = (gain_pre, gain_attn, gain_mid, gain_ffn, bn_gain, bn_shift, rel_table.reshape(-1))
-    held = jnp.concatenate(vectors)
-    held = jnp.pad(held, (0, 16 * 256 - held.shape[0])).reshape(16, 256)
-    gathered = gather_all([held, w_reduce, w_spatial, w_expand, w_embed, w_qkv, w_out, w_up, w_down], 1)
-    full_held = gathered[0].reshape(devices, -1)
-    full_reduce, full_spatial, full_expand, full_embed, full_qkv, full_out, full_up, full_down = (
-        item.reshape(-1, item.shape[-1]) for item in gathered[1:]
-    )
-    full_vectors, at = [], 0
-    for item in vectors:
-        full_vectors.append(full_held[:, at : at + item.shape[0]])
-        at += item.shape[0]
-    full_pre, full_attn, full_mid, full_ffn, full_bn_gain, full_bn_shift = (
-        item.reshape(-1) for item in full_vectors[:6]
-    )
-    full_table = full_vectors[6].reshape(devices, HEADS, -1).transpose(1, 0, 2).reshape(HEADS, -1)
     rows, length = (segments.shape[0], segments.shape[1])
     images, side = (features.shape[0], features.shape[1])
     patch_count = images * side * side
-    whole = patch_count * lax.axis_size(("wide", "narrow"))
+    whole = patch_count * devices
+    first_at = positions[0, 0]
     stem_in = features.reshape(patch_count, features.shape[3])
-    pre_first = product(stem_in, full_reduce)
-    first = smooth(pre_first).astype(jnp.bfloat16)
-    columns = unfold(first.reshape(images, side, side, first.shape[1])).reshape(
-        patch_count, 9 * first.shape[1]
-    )
-    pre_second = product(columns, full_spatial)
-    second = smooth(pre_second).astype(jnp.bfloat16)
-    third = product(second, full_expand)
-    sums = jnp.concatenate([jnp.sum(third, axis=0), jnp.sum(third * third, axis=0)])
-    bn_total, bn_squares = jnp.split(total_sum(sums.reshape(16, -1), 3).reshape(-1), 2)
-    bn_mean = bn_total / whole
-    bn_inv = lax.rsqrt(bn_squares / whole - bn_mean * bn_mean + epsilon)
-    bn_unit = (third - bn_mean) * bn_inv
-    pre_joined = (
-        bn_unit * full_bn_gain.astype(jnp.float32)
-        + full_bn_shift.astype(jnp.float32)
-        + stem_in.astype(jnp.float32)
-    )
-    joined = smooth(pre_joined).astype(jnp.bfloat16)
-    embedded = product(joined, full_embed)
-    first_at = positions[0, 0]
-    base = tokens.astype(jnp.float32)
-    covered = lax.dynamic_slice_in_dim(base, first_at, patch_count, 0) + embedded
-    start = lax.dynamic_update_slice_in_dim(base, covered, first_at, 0)
-    normed0, unit0, inv0 = layer_norm(start, full_pre.astype(jnp.float32))
-    normed0_low = normed0.astype(jnp.bfloat16)
-    packed = product(normed0_low, full_qkv).astype(jnp.bfloat16)
+    vectors = [item.reshape(1, -1) for item in (gain_pre, gain_attn, gain_mid, gain_ffn, bn_gain, bn_shift)]
+    gathered, kept = front(
+        positions[0, :1],
+        vectors + [rel_table],
+        stem_in,
+        tokens,
+        [w_reduce, w_spatial, w_expand, w_embed, w_qkv, w_out, w_up, w_down],
+        side,
+        1,
+    )
+    full_reduce, full_spatial, full_expand, full_embed, full_qkv, full_out, full_up, full_down = (
+        item.reshape(-1, item.shape[-1]) for item in gathered
+    )
+    gains, pre_first, columns, pre_second, second, bn_unit, bn_inv, joined, start, normed0_low, packed = kept
+    full_bn_gain, full_bn_shift = gains[0], gains[1]
+    full_pre, full_attn, full_mid = gains[2, :D], gains[3, :D], gains[4, :D]
+    full_ffn = gains[5:8].reshape(-1)
+    full_table = gains[8:11].reshape(HEADS, 2 * RSPAN)
+    bn_inv = bn_inv[0]
+    pre_joined = bn_unit * full_bn_gain + full_bn_shift + stem_in.astype(jnp.float32)
+    unused, unit0, inv0 = layer_norm(start, full_pre)
     win = windows(segments)
     attended, logsums, bias = attend(packed, segments, bias_strips(full_table), win)
     scale_row = jnp.repeat(head_scale, HDIM)[None, :]

time: 569 us -> 536 us (0.942)
  local copies, waits for them, and re-layouts: 53.2 us -> 36.6 us
  matrix products: 94.3 us -> 78.5 us
  other arithmetic: 59.9 us -> 47.2 us
  Pallas kernels: 350 us -> 360 us
    pallas_call x2 -> x1, Pallas kernels: 54.5 us -> 12.2 us  [total_sum(): pl.pallas_call(functools.partial(total_kernel, lines, rows), out_shape=ja...]
    pallas_call x1, Pallas kernels: 98.1 us -> 127 us  [front(): pl.pallas_call(functools.partial(front_kernel, lines, rows, side, float(c...]
    dot_general x8 -> x3, matrix products: 38.9 us -> 19.9 us  [product(): return jnp.dot(lhs_matrix, rhs_matrix, preferred_element_type=jnp.float32)]
    pallas_call x1, Pallas kernels: 64.7 us -> 78.3 us  [attend_back(): pl.pallas_call(attend_back_kernel, out_shape=(jax.ShapeDtypeStruct((lengt...]
    dynamic_update_slice x1 -> x0, local copies, waits for them, and re-layouts: 7.65 us -> none  [local(): start = lax.dynamic_update_slice_in_dim(base, covered, first_at, 0)]
    pallas_call x1, Pallas kernels: 28.7 us -> 36.4 us  [attend(): pl.pallas_call(attend_kernel, out_shape=(jax.ShapeDtypeStruct((length, D)...]
    convert_element_type x6 -> x0, other arithmetic: 6.57 us -> none  [the longest x1 2.3 us: local(): joined = smooth(pre_joined).astype(jnp.bfloat16)]
    unnamed x164 -> x100, local copies, waits for them, and re-layouts: 17.3 us -> 11.2 us
where the time goes in v3:
time: 536 us; the launch traced here: 526 us
  Pallas kernels  360 us (67%)
  matrix products  78.5 us (15%)
  other arithmetic  47.2 us (9%)
  local copies, waits for them, and re-layouts  36.6 us (7%)
    pallas_call x1, Pallas kernels, front(): pl.pallas_call(functools.partial(front_kernel, lines, rows, side, float(c...  127 us
    pallas_call x1, Pallas kernels, finish(): pl.pallas_call(functools.partial(finish_kernel, lines, rows, plan, len(gi...  106 us
    pallas_call x1, Pallas kernels, attend_back(): pl.pallas_call(attend_back_kernel, out_shape=(jax.ShapeDtypeStruct((lengt...  78.3 us
    dot_general x8, matrix products, product_nt(): lax.dot_general(lhs_matrix, rhs_matrix, (((1,), (1,)), ((), ())), preferr...  50.2 us
    pallas_call x1, Pallas kernels, attend(): pl.pallas_call(attend_kernel, out_shape=(jax.ShapeDtypeStruct((length, D)...  36.4 us
    dot_general x3, matrix products, product(): return jnp.dot(lhs_matrix, rhs_matrix, preferred_element_type=jnp.float32)  19.9 us
    convert_element_type x1, other arithmetic, local(): grad_pre_up = smooth_back(pre_up, grad_activ).astype(jnp.bfloat16)  16.1 us
    pallas_call x1, Pallas kernels, total_sum(): pl.pallas_call(functools.partial(total_kernel, lines, rows), out_shape=ja...  12.2 us

profile of v3, /device:TPU:0, one launch (start us, length us, event | category | flops | bytes accessed | tf_op | source)
XLA Modules:
  0.0 525.8 jit_solution(3052282709296870357)
XLA Ops:
  0.7 1.2 slice.182
  1.8 1.4 copy.98.refs_7_
  3.2 127.2 %front.1 = (bf16[4,2,2,2,32,256]{5,4,3,2,1,0:T(8,128)(2,1)}, bf16[4,2,2,2,72,256]{5,4,3,2,1,0:T(8,128)(2,1)}, bf16[4,2,2,2,8,1024]{5,4,3,2,1,0:T(8,128)(2,1)}, b...) custom-call(s32[1]{0:T(128)} %bitcast.refs_0_, ...), custom_call_target="tpu_custom_call" | custom-call | flops 6000000000 | bytes 70000000 | tf_op jit(solution)/shard_map/front/pallas_call | solution.py:723
  130.4 0.8 fusion.47
  132.9 1.0 copy.100.segk
  133.9 1.0 copy-done.1
  135.0 36.4 %attend.1 = (f32[1024,768]{1,0:T(8,128)S(1)}, f32[8,6,256]{2,1,0:T(8,128)S(1)}, f32[6,5,128,256]{3,2,1,0:T(8,128)}) custom-call(s32[2,8]{1,0:T(2,128)S(1)} %pad_add_fusion.7.win, bf16[1024,2304]{1,0:T(8,128)(2,1)} %get-tuple-element.52.packed, s32[1024,1]{1,0:T(8,128)S(1)} %copy-done.1, s32[1,1024]{1,0:T(1,128)S(1)} %copy-done.2, f32[12,5,256]{2,1,0:T(8,128)S(1)} %stack.21.strips), custom_call_target="tpu_custom_call" | custom-call | flops 20000000000 | bytes 10000000 | tf_op jit(solution)/shard_map/attend/pallas_call | solution.py:196
  171.3 0.6 copy-done.4
  172.0 2.9 copy.101
  175.0 2.3 multiply_reduce_fusion.15
  178.3 0.9 slice_reduce_fusion.5
  179.2 3.3 fusion.50
  183.1 7.1 %fusion.42 = (f32[1024]{0:T(1024)S(1)}, f32[1024,3072]{1,0:T(8,128)S(1)}) fusion(bf16[768,3072]{1,0:T(8,128)(2,1)S(1)} %bitcast.187, f32[1024,768]{1,0:T(8,128)S(1)} %get-tuple-element.147, f32[768]{0:T(1024)S(1)} %get-tuple-element.101, f32[1024]{0:T(1024)S(1)} %add_rsqrt_fusion.2, f32[1024]{0:T(1024)S(1)} %broadcast_multiply_fusion.10), kind=kOutput, calls=%fused_computation.166 | convolution fusion | flops 4863294464 | bytes 20462592 | tf_op jit(solution)/shard_map/dot_general | solution.py:20
  190.2 5.6 %multiply_reduce_fusion.1 = f32[1024]{0:T(1024)S(1)} fusion(f32[1024]{0:T(1024)S(1)} %broadcast_multiply_fusion.2, f32[1024,3072]{1,0:T(8,128)S(1)} %get-tuple-element.149), kind=kLoop, calls=%fused_computation.14 | loop fusion | flops 34601984 | bytes 12591104 | tf_op jit(solution)/shard_map/reduce_sum | solution.py:38
  195.9 17.2 %fusion.7 = (f32[3072]{0:T(1024)S(1)}, f32[1024]{0:T(1024)S(1)}, f32[1024]{0:T(1024)S(1)}, f32[3072,1024]{0,1:T(8,128)}) fusion(f32[1024]{0:T(1024)S(1)} %add_rsqrt_fusion.1, f32[1024]{0:T(1024)S(1)} %broadcast_multiply_fusion.2, f32[1024,3072]{1,0:T(8,128)} %copy-done.6, f32[3072]{0:T(1024)S(1)} %mul.450, bf16[3072,768]{1,0:T(8,128)(2,1)} %bitcast.182, ...), kind=kOutput, calls=%fused_computation.11 | convolution fusion | flops 4882164736 | bytes 31498240 | tf_op jit(solution)/shard_map/dot_general | solution.py:30
  213.2 16.1 %fusion.6 = (bf16[1024,3072]{1,0:T(8,128)(2,1)S(1)}, bf16[1024,3072]{1,0:T(8,128)(2,1)}) fusion(f32[1024,3072]{1,0:T(8,128)S(1)} %bitcast.147, f32[3072,1024]{0,1:T(8,128)} %get-tuple-element.150, f32[1024]{0:T(1024)S(1)} %broadcast_multiply_fusion, f32[1024]{0:T(1024)S(1)} %broadcast_multiply_fusion.1, f32[3072]{0:T(1024)S(1)} %mul.450, ...), kind=kLoop, calls=%fused_computation.8 | loop fusion | flops 94371840 | bytes 37777408 | tf_op jit(solution)/shard_map/convert_element_type | solution.py:1130
  229.3 9.7 %fusion.51 = f32[1024,768]{1,0:T(8,128)S(1)} fusion(bf16[1024,3072]{1,0:T(8,128)(2,1)S(1)} %get-tuple-element.109.refs_5_, bf16[768,3072]{1,0:T(8,128)(2,1)} %bitcast.184), kind=kOutput, calls=%fused_computation.175 | convolution fusion | flops 4831838208 | bytes 14155776 | tf_op jit(solution)/shard_map/dot_general | solution.py:30
  239.0 2.8 multiply_reduce_fusion.3
  241.8 2.6 fusion.44
  244.5 1.7 multiply_reduce_fusion.13
  246.2 3.4 multiply_reduce_fusion.2
  249.6 2.6 copy.104.grads
  252.2 78.3 %attend_back.1 = (bf16[1024,2304]{1,0:T(8,128)(2,1)}, f32[12,5,256]{2,1,0:T(8,128)}) custom-call(s32[2,8]{1,0:T(2,128)} %copy-done.3, bf16[1024,2304]{1,0:T(8,128)(2,1)} %get-tuple-element.52.packed, bf16[1024,768]{1,0:T(8,128)(2,1)} %copy.104.grads, f32[1024,768]{1,0:T(8,128)} %copy-done, s32[1024,1]{1,0:T(8,128)} %copy.100.segk, s32[1,1024]{1,0:T(1,128)} %segq.3, ...), custom_call_target="tpu_custom_call" | custom-call | flops 49999998976 | bytes 20000000 | tf_op jit(solution)/shard_map/attend_back/pallas_call | solution.py:300
  330.5 1.2 slice_reduce_fusion.1
  332.0 0.9 copy.107
  333.5 0.5 rev.5
  334.8 9.2 %multiply_reduce_fusion.5 = (f32[768]{0:T(1024)S(1)}, f32[1024]{0:T(1024)S(1)}, f32[1024]{0:T(1024)S(1)}, f32[1024,768]{1,0:T(8,128)}) fusion(f32[1024,768]{1,0:T(8,128)S(1)} %copy-done.11, f32[1024]{0:T(1024)S(1)} %add_rsqrt_fusion, f32[1024]{0:T(1024)S(1)} %broadcast_multiply_fusion.7, f32[768]{0:T(1024)S(1)} %get-tuple-element.100, ...), kind=kOutput, calls=%fused_computation.25 | convolution fusion | flops 3630167296 | bytes 14571520 | tf_op jit(solution)/shard_map/dot_general | solution.py:30
  344.1 4.5 multiply_add_fusion
  348.6 0.8 fusion.46
  351.4 5.8 %fusion.43 = (f32[1024]{0:T(1024)S(1)}, f32[1024]{0:T(1024)S(1)}, f32[576,1024]{1,0:T(8,128)S(1)}) fusion(f32[576,1024]{1,0:T(8,128)} %get-tuple-element.63, bf16[576,1024]{1,0:T(8,128)(2,1)} %bitcast.174, f32[1024]{0:T(1024)S(1)} %bitcast.170, f32[1024]{0:T(1024)S(1)} %bitcast.168, bf16[1024,768]{1,0:T(8,128)(2,1)} %bitcast.189, ...), kind=kOutput, calls=%fused_computation.167 | convolution fusion | flops 921303040 | bytes 8372228 | tf_op jit(solution)/shard_map/dot_general | solution.py:30
  357.4 0.6 pad_bitcast_fusion.x_ref
  358.0 12.2 %total_sum.1 = f32[88,128]{1,0:T(8,128)} custom-call(f32[88,128]{1,0:T(8,128)} %pad_bitcast_fusion.x_ref), custom_call_target="tpu_custom_call" | custom-call | bytes 1000000 | tf_op jit(solution)/shard_map/total_sum/pallas_call | solution.py:1039
  370.2 0.8 slice_bitcast_fusion.7
  371.0 0.8 multiply_multiply_fusion.10
  371.8 0.8 slice.201
  372.6 2.3 multiply_convert_fusion.4
  374.8 2.0 fusion.22
  376.8 2.2 convolution_convert_fusion
  379.0 1.4 convolution_convert_fusion.3
  380.4 4.2 convolution_convert_fusion.1
  384.6 0.9 convolution_bitcast_fusion
  387.6 0.6 fusion.15
  388.2 1.0 copy.115
  389.2 1.6 copy.116.refs_1_
  390.8 2.6 copy.114
  393.4 1.6 copy.113
  395.0 105.9 %finish.1 = (f32[96,768]{1,0:T(8,128)}, f32[96,768]{1,0:T(8,128)}, f32[96,640]{1,0:T(8,128)}, f32[24,768]{1,0:T(8,128)}, f32[32,768]{1,0:T(8,128)}, /*index=5*/f...) custom-call(bf16[768,1024]{1,0:T(8,128)(2,1)} %bitcast.150, bf16[768,1024]{1,0:T(8,128)(2,1)} %copy.116.refs_1_, ...), custom_call_target="tpu_custom_call" | custom-call | flops 14000000000 | bytes 60000000 | tf_op jit(solution)/shard_map/finish/pallas_call | solution.py:992
  501.0 2.0 slice_select_fusion
  503.0 3.7 convolution_add_fusion.1
  506.9 0.7 copy.121
  507.6 0.6 dynamic_slice.28
  508.1 0.6 dynamic_slice.30
  508.7 0.6 dynamic_slice.31
  509.3 0.6 dynamic_slice.25
  509.9 0.6 dynamic_slice.26
  510.5 0.6 dynamic_slice.27
  511.6 9.5 %add_convert_fusion = bf16[1024,768]{1,0:T(8,128)(2,1)} fusion(f32[1024,768]{1,0:T(8,128)S(1)} %copy-done.9, bf16[1024,3072]{1,0:T(8,128)(2,1)} %get-tuple-element.110.refs_4_, bf16[3072,768]{1,0:T(8,128)(2,1)} %bitcast.183), kind=kOutput, calls=%fused_computation.34 | convolution fusion | flops 4833411072 | bytes 15728640 | tf_op jit(solution)/shard_map/dot_general | solution.py:20
  521.1 0.6 copy.139
  521.7 0.7 copy.140
  522.4 0.7 copy.141
  523.1 0.6 copy.142
  523.8 0.6 copy.143
  524.4 0.6 copy.144
  525.0 0.6 copy.145
  (161 shorter events, 7.8 us)
Async XLA Ops:
  3.2 129.2 %copy-start.2 = (s32[1,1024]{1,0:T(1,128)S(1)}, s32[1,1024]{1,0:T(1,128)}, u32[]{:S(2)}) copy-start(s32[1,1024]{1,0:T(1,128)} %segq.3) | copy-start | bytes 12292
  132.9 38.4 %copy-start.3 = (s32[2,8]{1,0:T(2,128)}, s32[2,8]{1,0:T(2,128)S(1)}, u32[]{:S(2)}) copy-start(s32[2,8]{1,0:T(2,128)S(1)} %pad_add_fusion.7.win) | copy-start | bytes 196
  133.9 1.0 copy-start.1
  171.3 0.6 copy-start.4
  172.0 2.9 copy-start
  172.0 2.9 copy-start.29
  174.9 2.8 copy-start.5
  175.0 4.2 copy-start.10
  179.2 3.9 slice-start.3
  179.2 3.9 slice-start.4
  182.5 7.7 %copy-start.7 = (f32[1024,768]{1,0:T(8,128)}, f32[1024,768]{1,0:T(8,128)S(1)}, u32[]{:S(2)}) copy-start(f32[1024,768]{1,0:T(8,128)S(1)} %get-tuple-element.147) | copy-start | bytes 9437188
  190.2 5.6 %copy-start.6 = (f32[1024,3072]{1,0:T(8,128)}, f32[1024,3072]{1,0:T(8,128)S(1)}, u32[]{:S(2)}) copy-start(f32[1024,3072]{1,0:T(8,128)S(1)} %get-tuple-element.149) | copy-start | bytes 37748740
  195.9 17.3 %slice-start = ((s8[12582912]{0:T(1024)(128)(4,1)}), s8[4194304]{0:T(1024)(128)(4,1)S(1)}, s32[]{:S(2)}) async-start(s8[12582912]{0:T(1024)(128)(4,1)} %bitcast.146), calls=%async_computation | async-start | bytes 8388608
  195.9 17.3 %slice-start.1 = ((s8[12582912]{0:T(1024)(128)(4,1)}), s8[4194304]{0:T(1024)(128)(4,1)S(1)}, s32[]{:S(2)}) async-start(s8[12582912]{0:T(1024)(128)(4,1)} %bitcast.146), calls=%async_computation.1 | async-start | bytes 8388608
  195.9 17.3 %slice-start.2 = ((s8[12582912]{0:T(1024)(128)(4,1)}), s8[4194304]{0:T(1024)(128)(4,1)S(1)}, s32[]{:S(2)}) async-start(s8[12582912]{0:T(1024)(128)(4,1)} %bitcast.146), calls=%async_computation.2 | async-start | bytes 8388608
  229.3 9.7 %copy-start.13 = (bf16[1024,3072]{1,0:T(8,128)(2,1)}, bf16[1024,3072]{1,0:T(8,128)(2,1)S(1)}, u32[]{:S(2)}) copy-start(bf16[1024,3072]{1,0:T(8,128)(2,1)S(1)} %get-tuple-element.109.refs_5_) | copy-start | bytes 18874372
  229.3 9.7 %copy-start.8 = (f32[1024,768]{1,0:T(8,128)S(1)}, f32[1024,768]{1,0:T(8,128)}, u32[]{:S(2)}) copy-start(f32[1024,768]{1,0:T(8,128)} %copy-done.7) | copy-start | bytes 9437188
  239.0 2.8 copy-start.15
  241.8 2.7 copy-start.18
  244.5 1.7 copy-start.17
  252.2 81.8 %copy-start.11 = (f32[1024,768]{1,0:T(8,128)S(1)}, f32[1024,768]{1,0:T(8,128)}, u32[]{:S(2)}) copy-start(f32[1024,768]{1,0:T(8,128)} %get-tuple-element.51) | copy-start | bytes 9437188
  357.1 19.7 %copy-start.12 = (f32[576,1024]{1,0:T(8,128)}, f32[576,1024]{1,0:T(8,128)S(1)}, u32[]{:S(2)}) copy-start(f32[576,1024]{1,0:T(8,128)S(1)} %get-tuple-element.153) | copy-start | bytes 7077892
  357.2 17.7 %copy-start.31 = (bf16[4,2,2,2,8,1024]{5,4,3,2,1,0:T(8,128)(2,1)S(1)}, bf16[4,2,2,2,8,1024]{5,4,3,2,1,0:T(8,128)(2,1)}, u32[]{:S(2)}) copy-start(bf16[4,2,2,2,8,1024]{5,4,3,2,1,0:T(8,128)(2,1)} %get-tuple-element.66) | copy-start | bytes 1572868
  374.8 2.0 copy-start.33
  376.8 2.2 copy-start.32
  376.8 3.6 copy-start.34
  380.4 4.2 copy-start.19
  386.1 1.1 copy-start.20
  386.2 1.3 copy-start.30
  386.7 2.5 copy-start.14
  389.2 4.2 copy-start.16
  501.0 5.8 %copy-start.23 = (f32[88,128]{1,0:T(8,128)S(1)}, f32[88,128]{1,0:T(8,128)}, u32[]{:S(2)}) copy-start(f32[88,128]{1,0:T(8,128)} %total_sum.1) | copy-start | bytes 135172
  501.0 10.6 %copy-start.9 = (f32[1024,768]{1,0:T(8,128)S(1)}, f32[1024,768]{1,0:T(8,128)}, u32[]{:S(2)}) copy-start(f32[1024,768]{1,0:T(8,128)} %copy-done.7) | copy-start | bytes 9437188
  511.6 9.5 %copy-start.26 = (f32[24,768]{1,0:T(8,128)S(1)}, f32[24,768]{1,0:T(8,128)}, u32[]{:S(2)}) copy-start(f32[24,768]{1,0:T(8,128)} %get-tuple-element.179) | copy-start | bytes 221188
  511.6 10.1 %copy-start.22 = (f32[96,768]{1,0:T(8,128)S(1)}, f32[96,768]{1,0:T(8,128)}, u32[]{:S(2)}) copy-start(f32[96,768]{1,0:T(8,128)} %get-tuple-element.180) | copy-start | bytes 884740
  511.6 10.9 %copy-start.21 = (f32[96,768]{1,0:T(8,128)S(1)}, f32[96,768]{1,0:T(8,128)}, u32[]{:S(2)}) copy-start(f32[96,768]{1,0:T(8,128)} %get-tuple-element.78) | copy-start | bytes 884740
  511.6 11.6 %copy-start.28 = (f32[32,256]{1,0:T(8,128)S(1)}, f32[32,256]{1,0:T(8,128)}, u32[]{:S(2)}) copy-start(f32[32,256]{1,0:T(8,128)} %get-tuple-element.188) | copy-start | bytes 98308
  511.6 12.2 %copy-start.25 = (f32[72,256]{1,0:T(8,128)S(1)}, f32[72,256]{1,0:T(8,128)}, u32[]{:S(2)}) copy-start(f32[72,256]{1,0:T(8,128)} %get-tuple-element.189) | copy-start | bytes 221188
  511.6 12.8 %copy-start.27 = (f32[8,1024]{1,0:T(8,128)S(1)}, f32[8,1024]{1,0:T(8,128)}, u32[]{:S(2)}) copy-start(f32[8,1024]{1,0:T(8,128)} %get-tuple-element.190) | copy-start | bytes 98308
  511.6 13.4 %copy-start.24 = (f32[32,768]{1,0:T(8,128)S(1)}, f32[32,768]{1,0:T(8,128)}, u32[]{:S(2)}) copy-start(f32[32,768]{1,0:T(8,128)} %get-tuple-element.191) | copy-start | bytes 294916

commit v4 on v3

--- a/solution.py
+++ b/solution.py
@@ -394,62 +394,88 @@
 
 
 def gather_copies(lines, rows):
-    return (lines - 1) + 1 + (rows - 1) + (rows - 1) + 1 + 1 + rows + rows
+    return (lines - 1) + 1 + (rows - 1) + 1 + 1 + (rows - 1) + 1
 
 
 class Gather:
-    def __init__(self, place, sends, shard, out, local_sem, at, width):
-        self.p, self.s, self.shard, self.out = place, sends, shard, out
-        self.local_sem = local_sem
-        cut = width // 256 * 128
-        self.every, self.low, self.high = pl.ds(at, width), pl.ds(at, cut), pl.ds(at + cut, width - cut)
+    def __init__(self, place, sends, shard, out, local_sem, region, side_first):
+        self.p, self.s, self.out, self.region = place, sends, out, region
+        self.shard, self.local_sem, self.side_first = shard.at[region], local_sem, side_first
         self.cores = []
+
+    def at(self, line, side, row):
+        return self.out.at[(line, side, row, self.p.core) + self.region]
 
     def begin(self):
         p = self.p
-        mine = self.out.at[p.line, p.side, p.row, p.core, :, self.every]
-        shard = self.shard.at[:, self.every]
-        self.local = pltpu.make_async_copy(shard, mine, self.local_sem)
+        mine = self.at(p.line, p.side, p.row)
+        self.local = pltpu.make_async_copy(self.shard, mine, self.local_sem)
         self.local.start()
-        self.stage = [self.s.start(shard, mine, p.device(line=p.line_peer(k))) for k in range(1, p.lines)]
+        self.stage = [self.s.start(self.shard, mine, p.device(line=p.line_peer(k))) for k in range(1, p.lines)]
 
     def across(self, src):
         self.cores.append(self.s.start(src, src, self.p.device(core=1 - self.p.core)))
 
-    def second(self):
-        p, out = self.p, self.out
-        self.local.wait()
+    def to_side(self, src):
+        self.stage.append(self.s.start(src, src, self.p.device(side=1 - self.p.side)))
+
+    def to_rows(self, src):
+        p = self.p
+        self.stage += [self.s.start(src, src, p.device(row=p.row_peer(k))) for k in range(1, p.rows)]
+
+    def arrived(self):
         for copy in self.stage:
             copy.wait_recv()
-        low = out.at[:, p.side, p.row, p.core, :, self.low]
-        high = out.at[:, p.side, p.row, p.core, :, self.high]
-        self.stage = [self.s.start(low, low, p.device(side=1 - p.side))]
-        self.stage += [self.s.start(high, high, p.device(row=p.row_peer(k))) for k in range(1, p.rows)]
-        self.across(out.at[:, p.side, p.row, p.core, :, self.every])
+        self.stage = []
+
+    def second(self):
+        p, every = self.p, slice(None)
+        self.local.wait()
+        self.arrived()
+        mine = self.at(every, p.side, p.row)
+        (self.to_side if self.side_first else self.to_rows)(mine)
+        self.across(mine)
 
     def third(self):
-        p, out = self.p, self.out
-        for copy in self.stage:
-            copy.wait_recv()
-        low = out.at[:, :, p.row, p.core, :, self.low]
-        high = out.at[:, p.side, :, p.core, :, self.high]
-        self.stage = [self.s.start(high, high, p.device(side=1 - p.side))]
-        self.stage += [self.s.start(low, low, p.device(row=p.row_peer(k))) for k in range(1, p.rows)]
-        self.across(out.at[:, 1 - p.side, p.row, p.core, :, self.low])
-        for k in range(1, p.rows):
-            self.across(out.at[:, p.side, p.row_source(k), p.core, :, self.high])
+        p, every = self.p, slice(None)
+        self.arrived()
+        if self.side_first:
+            self.to_rows(self.at(every, every, p.row))
+            self.across(self.at(every, 1 - p.side, p.row))
+        else:
+            self.to_side(self.at(every, p.side, every))
+            for k in range(1, p.rows):
+                self.across(self.at(every, p.side, p.row_source(k)))
 
     def fourth(self):
-        p, out = self.p, self.out
-        for copy in self.stage:
-            copy.wait_recv()
-        for k in range(1, p.rows):
-            self.across(out.at[:, :, p.row_source(k), p.core, :, self.low])
-        self.across(out.at[:, 1 - p.side, :, p.core, :, self.high])
+        p, every = self.p, slice(None)
+        self.arrived()
+        if self.side_first:
+            for k in range(1, p.rows):
+                self.across(self.at(every, every, p.row_source(k)))
+        else:
+            self.across(self.at(every, 1 - p.side, every))
 
     def last(self):
         for copy in self.cores:
             copy.wait_recv()
+
+
+class HalfGather(Gather):
+    def at(self, line, side, row):
+        return self.out.at[line, side if self.side_first else row]
+
+    def across(self, src):
+        pass
+
+    def third(self):
+        self.arrived()
+
+    def fourth(self):
+        pass
+
+    def last(self):
+        pass
 
 
 class Total:
@@ -543,12 +569,15 @@
     vectors = take(FRONT_VECTORS)
     (stem, tokens) = take(2)
     shards = take(number)
-    outs = take(number)
-    (gains, pre_first, columns, pre_second, second, unit, inv, joined, start, normed, packed) = take(11)
+    held_outs, half_outs = take(FULL), take(number - FULL)
+    (gains_out, pre_first_out, columns_out, pre_second_out, second_out, unit_out, inv) = take(7)
+    (joined_out, start_out, normed_out, packed_out) = take(4)
+    outs = take(FULL) + half_outs
+    (gains, pre_first, columns, pre_second, second, unit, joined, start, normed, packed) = take(10)
     mats = take(5)
     (placing,) = take(1)
     held_bufs, sum_bufs = take(4), take(4)
-    send_sems, recv_sems, local_sems = take(3)
+    send_sems, recv_sems, local_sems, out_sems = take(4)
     place = Place(lines, rows)
     place.greet()
     sends = Sends(send_sems, recv_sems)
@@ -559,10 +588,26 @@
     devices = 4 * lines * rows
 
     parts = []
-    for i, (which, col, width) in enumerate(pieces):
-        parts.append(Gather(place, sends, shards[which], outs[which], local_sems.at[i], col, width))
-    parts[0].begin()
-    parts[1].begin()
+    for i, (which, region, side_first) in enumerate(pieces):
+        region = tuple(pl.ds(*item) for item in region)
+        kind = Gather if which < FULL else HalfGather
+        parts.append(kind(place, sends, shards[which], outs[which], local_sems.at[i], region, side_first))
+    batches = [[part for part, piece in zip(parts, pieces) if piece[0] in which] for which in ((0, 1), (2, 3), (4,), (5, 6, 7))]
+
+    def run(batch, *names):
+        for name in names:
+            for part in batches[batch]:
+                getattr(part, name)()
+
+    copies_out = []
+
+    def emit(value, out):
+        copy = pltpu.make_async_copy(value, out, out_sems.at[len(copies_out)])
+        copy.start()
+        copies_out.append(copy)
+
+    run(0, "begin")
+    run(1, "begin")
     for v, (ref, row) in enumerate(zip(vectors[:6], (2, 3, 4, 5, 0, 1))):
         n = ref.shape[1]
         line = spread(ref[...], me, n * devices).astype(jnp.bfloat16)
@@ -574,45 +619,40 @@
         held[pl.ds(8 + h // 4, 1), pl.ds(h % 4 * 256, 256)] = table[h : h + 1, :]
     vector_total = Total(place, sends, *held_bufs)
     vector_total.begin()
-    for part in parts[2:]:
-        part.begin()
-
-    steps = []
-    for i in range(len(parts) + 3):
-        for lag, name in ((0, "second"), (1, "third"), (2, "fourth"), (3, "last")):
-            if 0 <= i - lag < len(parts):
-                steps.append((i - lag, name))
-
-    def pump(n=None, until=None):
-        while steps and (n is None or n > 0):
-            i, name = steps.pop(0)
-            getattr(parts[i], name)()
-            n = None if n is None else n - 1
-            if until is not None and (i, name) == (until, "last"):
-                break
-
-    pump(2)
+
+    run(0, "second")
     vector_total.second()
-    pump(2)
+    run(2, "begin")
+    run(0, "third")
+    run(1, "second")
     vector_total.third()
-    pump(until=0)
+    run(0, "fourth")
+    run(1, "third")
+    run(2, "second")
+    run(3, "begin")
+    run(0, "last")
     count = side * side
     w_reduce, w_spatial, w_expand, w_embed, w_qkv = mats
     w_reduce[...] = matrix(outs[0])
     pre = dot_nn(stem[...], w_reduce[...])
     pre_first[...] = pre
+    emit(pre_first, pre_first_out)
     first = gelu(pre).astype(jnp.bfloat16).astype(jnp.float32)
     channels = first.shape[1]
     for r in range(3):
         for c in range(3):
             k = r * 3 + c
             columns[:, pl.ds(k * channels, channels)] = shifted(first, r - 1, c - 1, side).astype(jnp.bfloat16)
-    pump(until=1)
+    emit(columns, columns_out)
     w_spatial[...] = matrix(outs[1])
     pre = dot_nn(columns[...], w_spatial[...])
     pre_second[...] = pre
+    emit(pre_second, pre_second_out)
     second[...] = gelu(pre).astype(jnp.bfloat16)
-    pump(until=2)
+    emit(second, second_out)
+    run(1, "fourth")
+    run(2, "third")
+    run(1, "last")
     w_expand[...] = matrix(outs[2])
     sums = sum_bufs[0]
     sums[...] = jnp.zeros_like(sums)
@@ -626,13 +666,15 @@
     tile_loop(unit.shape[1], expand)
     norm_total = Total(place, sends, *sum_bufs)
     norm_total.begin()
-    pump(2)
+    run(2, "fourth")
     norm_total.second()
     gains[...] = vector_total.last().astype(jnp.float32)
-    pump(until=3)
+    emit(gains, gains_out)
+    w_embed[...] = matrix(outs[3])
     norm_total.third()
-    w_embed[...] = matrix(outs[3])
-    pump(1)
+    run(3, "second")
+    for held_weight, out in zip(outs[:4], held_outs):
+        emit(held_weight, out)
     totals = norm_total.last()
     mean = totals[0:1] / whole
     inv_std = lax.rsqrt(totals[1:2] / whole - mean * mean + epsilon)
@@ -649,6 +691,8 @@
         return carry
 
     lax.fori_loop(0, 3, join, 0)
+    emit(unit, unit_out)
+    emit(joined, joined_out)
     length, width = start.shape
     token = lax.broadcasted_iota(jnp.int32, (length, count), 0)
     patch = lax.broadcasted_iota(jnp.int32, (length, count), 1)
@@ -672,16 +716,25 @@
         normed[at_rows, :] = (centred * scale * gain).astype(jnp.bfloat16)
         return carry
 
+    emit(start, start_out)
     lax.fori_loop(0, length // 128, norm, 0)
-    pump(until=4)
+    emit(normed, normed_out)
+    run(2, "last")
+    emit(outs[4], held_outs[4])
     w_qkv[...] = matrix(outs[4])
 
     def project(cols):
         packed[:, cols] = dot_nn(normed[...], w_qkv[:, cols]).astype(jnp.bfloat16)
 
     tile_loop(packed.shape[1], project)
-    pump()
+    emit(packed, packed_out)
+    run(3, "third")
     sends.finish()
+    for copy in copies_out:
+        copy.wait()
+
+
+FULL = 5
 
 
 def front(first_at, vectors, stem, tokens, shards, side, collective_id):
@@ -690,16 +743,19 @@
     devices = wide * narrow
     number = len(shards)
     pieces = []
-    for i, s in enumerate(shards):
-        cuts = 2 if i >= 6 else 1
-        for k in range(cuts):
-            pieces.append((i, k * s.shape[1] // cuts, s.shape[1] // cuts))
+    for i, item in enumerate(shards):
+        r, c = item.shape
+        if i == 4:
+            pieces += [(i, ((0, r), (k * c // 2, c // 2)), k == 0) for k in range(2)]
+        else:
+            pieces.append((i, ((0, r), (0, c)), i in (0, 2, 5, 7)))
     copies = len(pieces) * gather_copies(lines, rows) + 2 * total_copies(lines, rows)
     count, length = side * side, tokens.shape[0]
     mid = shards[0].shape[1]
     wide_in = stem.shape[1]
     f32, bf16 = jnp.float32, jnp.bfloat16
-    gathered = [jax.ShapeDtypeStruct((lines, 2, rows, 2) + s.shape, s.dtype) for s in shards]
+    leads = [(lines, 2, rows, 2)] * FULL + [(lines, 2), (lines, rows), (lines, 2)]
+    gathered = [jax.ShapeDtypeStruct(lead + s.shape, s.dtype) for lead, s in zip(leads, shards)]
     kept = [
         ((16, 1024), f32),
         ((count, mid), f32),
@@ -715,22 +771,213 @@
     ]
     vmem = pl.BlockSpec(memory_space=pltpu.VMEM)
     anywhere = pl.BlockSpec(memory_space=pl.ANY)
-    scratch = [pltpu.VMEM((s.shape[0] * devices, s.shape[1]), bf16) for s in shards[:5]]
+    scratch = [pltpu.VMEM(item.shape, item.dtype) for item in gathered[:FULL]]
+    scratch += [pltpu.VMEM(shape, dtype) for k, (shape, dtype) in enumerate(kept) if k != 6]
+    scratch += [pltpu.VMEM((s.shape[0] * devices, s.shape[1]), bf16) for s in shards[:5]]
     scratch += [pltpu.VMEM((length, count), bf16)]
     scratch += total_buffers(lines, rows, (16, 1024), bf16)
     scratch += total_buffers(lines, rows, (8, 1024), f32)
-    scratch += [pltpu.SemaphoreType.DMA((copies,)), pltpu.SemaphoreType.DMA((copies,)), pltpu.SemaphoreType.DMA((len(pieces),))]
+    scratch += [pltpu.SemaphoreType.DMA((copies,)), pltpu.SemaphoreType.DMA((copies,)), pltpu.SemaphoreType.DMA((len(pieces),)), pltpu.SemaphoreType.DMA((FULL + 10,))]
     results = pl.pallas_call(
         functools.partial(front_kernel, lines, rows, side, float(count * devices), pieces, number),
         out_shape=gathered + [jax.ShapeDtypeStruct(s, d) for s, d in kept],
         in_specs=[pl.BlockSpec(memory_space=pltpu.SMEM)] + [vmem] * (FRONT_VECTORS + 2) + [anywhere] * number,
-        out_specs=[vmem] * 5 + [anywhere] * (number - 5) + [vmem] * len(kept),
+        out_specs=[anywhere] * number + [vmem if k == 6 else anywhere for k in range(len(kept))],
         scratch_shapes=scratch,
         compiler_params=pltpu.CompilerParams(collective_id=collective_id, has_side_effects=True, vmem_limit_bytes=60 * 2**20),
         cost_estimate=pl.CostEstimate(flops=6 * 10**9, bytes_accessed=7 * 10**7, transcendentals=10**6),
         name="front",
     )(first_at, *vectors, stem, tokens, *shards)
     return results[:number], results[number:]
+
+
+def gelu_slope(v):
+    t = jnp.tanh(0.7978845608028654 * (v + 0.044715 * (v * v * v)))
+    return 0.5 * (1.0 + t) + 0.5 * v * (1.0 - t * t) * (0.7978845608028654 * (1.0 + 0.134145 * (v * v)))
+
+
+def row_mean(values):
+    return jnp.mean(values, axis=-1, keepdims=True)
+
+
+def unit_of(values):
+    centred = values - row_mean(values)
+    inv_std = lax.rsqrt(row_mean(centred * centred) + epsilon)
+    return centred * inv_std, inv_std
+
+
+def unit_back(weighted, unit_rows, inv_std):
+    return inv_std * (weighted - row_mean(weighted) - unit_rows * row_mean(weighted * unit_rows))
+
+
+def column_sum(values):
+    return jnp.sum(values, axis=0, keepdims=True)
+
+
+FTILE = 512
+
+
+def middle_kernel(lines, rows, counts, *refs):
+    refs = list(refs)
+
+    def take(n):
+        out = refs[:n]
+        del refs[:n]
+        return out
+
+    attended, start, d_out, gains, scale = take(5)
+    outs_in, ups_in, downs_in = take(counts[0]), take(counts[1]), take(counts[2])
+    mixed, mixed_low, normed2, narrowed, grad_up, grad_middle, branch, grad_attended, sums = take(9)
+    held = take(3)
+    mats = take(3)
+    pre, act, weighted = take(3)
+    send_sems, recv_sems, local_sems = take(3)
+    i = pl.program_id(0)
+    w_out, w_up, w_down = mats
+    width, hidden = w_up.shape
+
+    @pl.when(i == 0)
+    def _():
+        place = Place(lines, rows)
+        partner = place.device(core=1 - place.core)
+        barrier = pltpu.get_barrier_semaphore()
+        pl.semaphore_signal(barrier, inc=1, device_id=partner, device_id_type=MESH)
+        pl.semaphore_wait(barrier, 1)
+        sends = Sends(send_sems, recv_sems)
+        waits = []
+        for full, pieces in zip(held, (outs_in, ups_in, downs_in)):
+            group = []
+            for k, piece in enumerate(pieces):
+                if full is held[1]:
+                    side = place.side if k == 0 else 1 - place.side
+                    spot = full.at[:, side, :, place.core]
+                else:
+                    spot = full.at[:, :, place.row_source(k), place.core]
+                local = pltpu.make_async_copy(piece, spot, local_sems.at[sends.used])
+                local.start()
+                group.append((sends.start(piece, spot, partner), local))
+            waits.append(group)
+        for full, mat, group in zip(held, mats, waits):
+            for copy, local in group:
+                copy.wait_recv()
+                local.wait()
+            tall = mat.shape[0] // (2 * lines)
+
+            def convert(k, carry, full=full, mat=mat, tall=tall):
+                block = full[k // 2, lax.rem(k, 2)].astype(jnp.float32)
+                mat[pl.ds(pl.multiple_of(k * tall, tall), tall), :] = block.reshape(tall, mat.shape[1]).astype(mat.dtype)
+                return carry
+
+            lax.fori_loop(0, 2 * lines, convert, 0)
+        sends.finish()
+        sums[...] = jnp.zeros_like(sums)
+
+    gain_attn, gain_mid = gains[3:4, :width], gains[4:5, :width]
+    scaled = attended[...] * scale[...]
+    unit1, inv1 = unit_of(scaled)
+    low = (unit1 * gain_attn).astype(jnp.bfloat16)
+    mixed_low[...] = low
+    middle = start[...] + dot_nn(low, w_out[...])
+    unit2, inv2 = unit_of(middle)
+    low2 = (unit2 * gain_mid).astype(jnp.bfloat16)
+    normed2[...] = low2
+    tiles = hidden // FTILE
+    count = middle.shape[0]
+    zero = jnp.zeros((count, 1), jnp.float32)
+
+    def span(f):
+        return pl.ds(pl.multiple_of(f * FTILE, FTILE), FTILE)
+
+    def gain_of(f):
+        per = 1024 // FTILE
+        return gains[pl.ds(5 + f // per, 1), f % per * FTILE : (f % per + 1) * FTILE]
+
+    total = zero
+    for f in range(tiles):
+        cols = pl.ds(f * FTILE, FTILE)
+        value = dot_nn(low2, w_up[:, cols])
+        pre[:, cols] = value
+        value = gelu(value)
+        act[:, cols] = value
+        total = total + jnp.sum(value, axis=-1, keepdims=True)
+    mean = total / hidden
+    total = zero
+    for f in range(tiles):
+        cols = pl.ds(f * FTILE, FTILE)
+        centred = act[:, cols] - mean
+        total = total + jnp.sum(centred * centred, axis=-1, keepdims=True)
+    inv3 = lax.rsqrt(total / hidden + epsilon)
+    result = middle
+    cross1, cross2 = zero, zero
+    for f in range(tiles):
+        cols = pl.ds(f * FTILE, FTILE)
+        unit3 = (act[:, cols] - mean) * inv3
+        act[:, cols] = unit3
+        gain = gain_of(f)
+        low3 = (unit3 * gain).astype(jnp.bfloat16)
+        narrowed[:, cols] = low3
+        result = result + dot_nn(low3, w_down[cols, :])
+        grad = dot_nt(d_out[...], w_down[cols, :])
+        sums[0:1, cols] += column_sum(grad * unit3)
+        grad = grad * gain
+        weighted[:, cols] = grad
+        cross1 = cross1 + jnp.sum(grad, axis=-1, keepdims=True)
+        cross2 = cross2 + jnp.sum(grad * unit3, axis=-1, keepdims=True)
+    mixed[...] = result.astype(jnp.bfloat16)
+    cross1, cross2 = cross1 / hidden, cross2 / hidden
+    grad2 = jnp.zeros((count, width), jnp.float32)
+    for f in range(tiles):
+        cols = pl.ds(f * FTILE, FTILE)
+        grad = inv3 * (weighted[:, cols] - cross1 - act[:, cols] * cross2)
+        grad = (gelu_slope(pre[:, cols]) * grad).astype(jnp.bfloat16)
+        grad_up[:, cols] = grad
+        grad2 = grad2 + dot_nt(grad, w_up[:, cols])
+    sums[1:2, :width] += column_sum(grad2 * unit2)
+    grad_mid = d_out[...].astype(jnp.float32) + unit_back(grad2 * gain_mid, unit2, inv2)
+    grad_middle[...] = grad_mid
+    low = grad_mid.astype(jnp.bfloat16)
+    branch[...] = low
+    grad1 = dot_nt(low, w_out[...])
+    sums[2:3, :width] += column_sum(grad1 * unit1)
+    grad_scaled = unit_back(grad1 * gain_attn, unit1, inv1)
+    sums[3:4, :width] += column_sum(grad_scaled * attended[...])
+    grad_attended[...] = (grad_scaled * scale[...]).astype(jnp.bfloat16)
+
+
+def middle_part(attended, start, d_out, gains, scale_row, outs_in, ups_in, downs_in, hidden, collective_id):
+    wide, narrow = lax.axis_size("wide"), lax.axis_size("narrow")
+    lines, rows = wide // 2, narrow // 2
+    length, width = start.shape
+    block = 256
+    f32, bf16 = jnp.float32, jnp.bfloat16
+    counts = (len(outs_in), len(ups_in), len(downs_in))
+    copies = sum(counts)
+
+    def by_token(columns):
+        return pl.BlockSpec((block, columns), lambda i: (i, 0))
+
+    def whole(shape):
+        return pl.BlockSpec(shape, lambda i: (0,) * len(shape))
+
+    anywhere = pl.BlockSpec(memory_space=pl.ANY)
+    pieces = list(outs_in) + list(ups_in) + list(downs_in)
+    results = [(width, bf16), (width, bf16), (width, bf16), (hidden, bf16), (hidden, bf16), (width, f32), (width, bf16), (width, bf16)]
+    shapes = [(width, width), (width, hidden), (hidden, width)]
+    devices = wide * narrow
+    return pl.pallas_call(
+        functools.partial(middle_kernel, lines, rows, counts),
+        out_shape=[jax.ShapeDtypeStruct((length, c), d) for c, d in results] + [jax.ShapeDtypeStruct((8, hidden), f32)],
+        grid=(length // block,),
+        in_specs=[by_token(width), by_token(width), by_token(width), whole(gains.shape), whole(scale_row.shape)] + [anywhere] * copies,
+        out_specs=[by_token(c) for c, _ in results] + [whole((8, hidden))],
+        scratch_shapes=[pltpu.VMEM((lines, 2, rows, 2, m // devices, n), bf16) for m, n in shapes]
+        + [pltpu.VMEM(shape, bf16) for shape in shapes]
+        + [pltpu.VMEM((block, hidden), f32)] * 3
+        + [pltpu.SemaphoreType.DMA((copies,))] * 3,
+        compiler_params=pltpu.CompilerParams(collective_id=collective_id, has_side_effects=True, vmem_limit_bytes=60 * 2**20),
+        cost_estimate=pl.CostEstimate(flops=22 * 10**9, bytes_accessed=6 * 10**7, transcendentals=7 * 10**6),
+        name="middle_part",
+    )(attended, start, d_out, gains, scale_row, *pieces)
 
 
 def scatter_copies(lines, rows):
@@ -1096,9 +1343,22 @@
         side,
         1,
     )
-    full_reduce, full_spatial, full_expand, full_embed, full_qkv, full_out, full_up, full_down = (
-        item.reshape(-1, item.shape[-1]) for item in gathered
+    full_reduce, full_spatial, full_expand, full_embed, full_qkv = (
+        item.reshape(-1, item.shape[-1]) for item in gathered[:5]
     )
+    planes = lax.axis_size("narrow") // 2
+
+    def other_side(item):
+        return lax.ppermute(item, "wide", [(w, w ^ 1) for w in range(devices // (2 * planes))])
+
+    def next_row(item, k):
+        return lax.ppermute(item, "narrow", [(n, (n + 2 * k) % (2 * planes)) for n in range(2 * planes)])
+
+    def by_row(item):
+        return [item] + [next_row(item, k) for k in range(1, planes)]
+
+    outs_in, downs_in = by_row(gathered[5]), by_row(gathered[7])
+    ups_in = [gathered[6], other_side(gathered[6])]
     gains, pre_first, columns, pre_second, second, bn_unit, bn_inv, joined, start, normed0_low, packed = kept
     full_bn_gain, full_bn_shift = gains[0], gains[1]
     full_pre, full_attn, full_mid = gains[2, :D], gains[3, :D], gains[4, :D]
@@ -1110,36 +1370,12 @@
     win = windows(segments)
     attended, logsums, bias = attend(packed, segments, bias_strips(full_table), win)
     scale_row = jnp.repeat(head_scale, HDIM)[None, :]
-    scaled = attended * scale_row
-    mixed_in, unit1, inv1 = layer_norm(scaled, full_attn.astype(jnp.float32))
-    mixed_low = mixed_in.astype(jnp.bfloat16)
-    middle = start + product(mixed_low, full_out)
-    normed2, unit2, inv2 = layer_norm(middle, full_mid.astype(jnp.float32))
-    normed2_low = normed2.astype(jnp.bfloat16)
-    pre_up = product(normed2_low, full_up)
-    activ = smooth(pre_up)
-    narrowed, unit3, inv3 = layer_norm(activ, full_ffn.astype(jnp.float32))
-    narrowed_low = narrowed.astype(jnp.bfloat16)
-    result = middle + product(narrowed_low, full_down)
-    mixed = result.astype(jnp.bfloat16)
-    grad_result = d_out.astype(jnp.float32)
-    grad_narrowed = product_nt(d_out, full_down)
-    grad_activ, grad_gain_ffn = layer_norm_back(
-        grad_narrowed, unit3, inv3, full_ffn.astype(jnp.float32)
+    hidden = w_up.shape[1]
+    mixed, mixed_low, normed2_low, narrowed_low, grad_pre_up, grad_middle, grad_branch, grad_attended, sums = middle_part(
+        attended, start, d_out, gains, scale_row, outs_in, ups_in, downs_in, hidden, 5
     )
-    grad_pre_up = smooth_back(pre_up, grad_activ).astype(jnp.bfloat16)
-    grad_normed2 = product_nt(grad_pre_up, full_up)
-    grad_mid_in, grad_gain_mid = layer_norm_back(
-        grad_normed2, unit2, inv2, full_mid.astype(jnp.float32)
-    )
-    grad_middle = grad_result + grad_mid_in
-    grad_branch = grad_middle.astype(jnp.bfloat16)
-    grad_mixed_in = product_nt(grad_branch, full_out)
-    grad_scaled, grad_gain_attn = layer_norm_back(
-        grad_mixed_in, unit1, inv1, full_attn.astype(jnp.float32)
-    )
-    grad_head_local = jnp.sum(jnp.sum(grad_scaled * attended, axis=0).reshape(HEADS, HDIM), axis=1)
-    grad_attended = (grad_scaled * scale_row).astype(jnp.bfloat16)
+    grad_gain_ffn, grad_gain_mid, grad_gain_attn = sums[0], sums[1, :D], sums[2, :D]
+    grad_head_local = jnp.sum(sums[3, :D].reshape(HEADS, HDIM), axis=1)
     grad_packed, grad_strips = attend_back(packed, grad_attended, attended, segments, bias, logsums, win)
     grad_table = table_from_strips(grad_strips)
     grad_normed0 = product_nt(grad_packed, full_qkv)
@@ -1194,7 +1430,7 @@
     grad_features = (grad_pre_joined + product_nt(grad_pre_first, full_reduce)).reshape(
         features.shape
     )
-    lines, planes = lax.axis_size("wide") // 2, lax.axis_size("narrow") // 2
+    lines = lax.axis_size("wide") // 2
 
     def by_rows(grad):
         return grad.astype(jnp.bfloat16).reshape(lines, 2, planes, 2, -1, grad.shape[1])

time: 536 us -> 465 us (0.87); the launches traced: 526 us -> 462 us
  matrix products: 78.5 us -> 24.3 us
  other arithmetic: 47.2 us -> 9.73 us
  Pallas kernels: 360 us -> 378 us
  local copies, waits for them, and re-layouts: 36.6 us -> 42.9 us
    pallas_call x0 -> x1, Pallas kernels: none -> 53.3 us  [middle_part(): pl.pallas_call(functools.partial(middle_kernel, lines, rows, counts), out...]
    pallas_call x1, Pallas kernels: 127 us -> 83.1 us  [front(): pl.pallas_call(functools.partial(front_kernel, lines, rows, side, float(c...]
    dot_general x8 -> x5, matrix products: 50.2 us -> 15.6 us  [product_nt(): lax.dot_general(lhs_matrix, rhs_matrix, (((1,), (1,)), ((), ())), preferr...]
    dot_general x3 -> x0, matrix products: 19.9 us -> none  [product(): return jnp.dot(lhs_matrix, rhs_matrix, preferred_element_type=jnp.float32)]
    convert_element_type x2 -> x0, other arithmetic: 18.7 us -> none  [the longest x1 16.1 us: local(): grad_pre_up = smooth_back(pre_up, grad_activ).astype(jnp.bfloat16)]
    pallas_call x1, Pallas kernels: 78.3 us -> 85.8 us  [attend_back(): pl.pallas_call(attend_back_kernel, out_shape=(jax.ShapeDtypeStruct((lengt...]
    reduce_sum x4 -> x1, other arithmetic: 7.07 us -> 0.48 us  [layer_norm(): jnp.mean(centred * centred, axis=-1, keepdims=True) + epsilon]
    reduce_sum x3 -> x1, other arithmetic: 6.33 us -> 0.12 us  [local(): grad_head_local = jnp.sum(sums[3, :D].reshape(HEADS, HDIM), axis=1)]
  transfers between devices with their start and end apart: 0 -> 3, of which waited for: 0 -> 0; matrix products, arithmetic and copies ran while one was open for 0% -> 2% of each run, Pallas kernels for 0% -> 8%
where the time goes in v4:
time: 465 us; the launch traced here: 462 us
  Pallas kernels  378 us (81%)
  local copies, waits for them, and re-layouts  42.9 us (9%)
  matrix products  24.3 us (5%)
  other arithmetic  9.73 us (2%)
    pallas_call x1, Pallas kernels, finish(): pl.pallas_call(functools.partial(finish_kernel, lines, rows, plan, len(gi...  103 us
    pallas_call x1, Pallas kernels, attend_back(): pl.pallas_call(attend_back_kernel, out_shape=(jax.ShapeDtypeStruct((lengt...  85.8 us
    pallas_call x1, Pallas kernels, front(): pl.pallas_call(functools.partial(front_kernel, lines, rows, side, float(c...  83.1 us
    pallas_call x1, Pallas kernels, middle_part(): pl.pallas_call(functools.partial(middle_kernel, lines, rows, counts), out...  53.3 us
    pallas_call x1, Pallas kernels, attend(): pl.pallas_call(attend_kernel, out_shape=(jax.ShapeDtypeStruct((length, D)...  34.9 us
    pallas_call x1, Pallas kernels, total_sum(): pl.pallas_call(functools.partial(total_kernel, lines, rows), out_shape=ja...  17.3 us
    unnamed x81, local copies, waits for them, and re-layouts  17.1 us
    dot_general x5, matrix products, product_nt(): lax.dot_general(lhs_matrix, rhs_matrix, (((1,), (1,)), ((), ())), preferr...  15.6 us
  transfers between devices with their start and end apart: 3, of which 0 were waited for; matrix products, arithmetic and copies ran while one was open for 2% of the time, Pallas kernels for 8%

profile of v4, /device:TPU:0, one launch (start us, length us, event | category | flops | bytes accessed | tf_op | source)
XLA Modules:
  0.0 461.6 jit_solution(10862731908271879860)
XLA Ops:
  0.7 1.2 slice.187
  1.8 1.4 copy.83.refs_7_
  3.2 83.1 %front.1 = (bf16[4,2,2,2,32,256]{5,4,3,2,1,0:T(8,128)(2,1)}, bf16[4,2,2,2,72,256]{5,4,3,2,1,0:T(8,128)(2,1)}, bf16[4,2,2,2,8,1024]{5,4,3,2,1,0:T(8,128)(2,1)}, b...) custom-call(s32[1]{0:T(128)} %bitcast.3.refs_0_, ...), custom_call_target="tpu_custom_call" | custom-call | flops 6000000000 | bytes 70000000 | tf_op jit(solution)/shard_map/front/pallas_call | solution.py:781
  86.3 1.6 collective-permute-start.1
  87.9 0.6 collective-permute-start.2
  88.5 1.4 collective-permute-start
  89.9 0.8 slice.188
  92.6 34.9 %attend.1 = (f32[1024,768]{1,0:T(8,128)S(1)}, f32[8,6,256]{2,1,0:T(8,128)S(1)}, f32[6,5,128,256]{3,2,1,0:T(8,128)}) custom-call(s32[2,8]{1,0:T(2,128)S(1)} %pad_add_fusion.7.win, bf16[1024,2304]{1,0:T(8,128)(2,1)} %get-tuple-element.60.packed, s32[1024,1]{1,0:T(8,128)S(1)} %copy.85.segk, s32[1,1024]{1,0:T(1,128)S(1)} %copy-done.1, ...), custom_call_target="tpu_custom_call" | custom-call | flops 20000000000 | bytes 10000000 | tf_op jit(solution)/shard_map/attend/pallas_call | solution.py:196
  127.6 1.7 copy-done.3
  129.3 0.6 copy-done.4
  131.3 0.7 broadcast_in_dim_reshape.3.refs_4_
  131.9 0.8 slice.201
  132.7 1.7 copy.94
  134.3 2.7 copy.92
  138.5 0.8 slice_reduce_fusion.8
  139.2 0.8 fusion.32
  140.1 53.3 %middle_part.1 = (bf16[1024,768]{1,0:T(8,128)(2,1)}, bf16[1024,768]{1,0:T(8,128)(2,1)}, bf16[1024,768]{1,0:T(8,128)(2,1)}, bf16[1024,3072]{1,0:T(8,128)(2,1)}, b...) custom-call(f32[1024,768]{1,0:T(8,128)} %copy-done.3, ...), custom_call_target="tpu_custom_call" | custom-call | flops 22000001024 | bytes 60000000 | tf_op jit(solution)/shard_map/middle_part/pallas_call | solution.py:967
  193.4 85.8 %attend_back.1 = (bf16[1024,2304]{1,0:T(8,128)(2,1)}, f32[12,5,256]{2,1,0:T(8,128)}) custom-call(s32[2,8]{1,0:T(2,128)} %copy-done.2, bf16[1024,2304]{1,0:T(8,128)(2,1)} %get-tuple-element.60.packed, bf16[1024,768]{1,0:T(8,128)(2,1)} %get-tuple-element.69.grads, f32[1024,768]{1,0:T(8,128)} %copy-done.3, s32[1024,1]{1,0:T(8,128)} %copy-done, s32[1,1024]{1,0:T(1,128)} %segq.3, ...), custom_call_target="tpu_custom_call" | custom-call | flops 49999998976 | bytes 20000000 | tf_op jit(solution)/shard_map/attend_back/pallas_call | solution.py:300
  279.2 1.2 slice_reduce_fusion.1
  280.4 0.9 copy.87
  281.7 0.9 slice_reduce_fusion.5
  282.6 0.9 slice.204
  284.1 9.2 %multiply_reduce_fusion = (f32[768]{0:T(1024)S(1)}, f32[1024]{0:T(1024)S(1)}, f32[1024]{0:T(1024)S(1)}, f32[1024,768]{1,0:T(8,128)}) fusion(f32[1024,768]{1,0:T(8,128)S(1)} %copy-done.6, f32[1024]{0:T(1024)S(1)} %add_rsqrt_fusion, f32[1024]{0:T(1024)S(1)} %broadcast_multiply_fusion.2, f32[768]{0:T(1024)S(1)} %slice_reduce_fusion.8, ...), kind=kOutput, calls=%fused_computation.4 | convolution fusion | flops 3630167296 | bytes 14571520 | tf_op jit(solution)/shard_map/dot_general | solution.py:30
  293.6 3.8 multiply_add_fusion
  297.4 0.5 copy-done.25
  297.9 2.8 fusion.30
  300.8 0.6 pad_bitcast_fusion.x_ref
  301.4 17.3 %total_sum.1 = f32[88,128]{1,0:T(8,128)} custom-call(f32[88,128]{1,0:T(8,128)} %pad_bitcast_fusion.x_ref), custom_call_target="tpu_custom_call" | custom-call | bytes 1000000 | tf_op jit(solution)/shard_map/total_sum/pallas_call | solution.py:1286
  318.7 0.8 slice_bitcast_fusion.7
  319.5 0.7 fusion.33
  320.3 0.8 slice_bitcast_fusion.3
  321.0 4.6 convolution_convert_fusion.1
  325.6 0.8 multiply_multiply_fusion.7
  326.4 0.6 multiply_convert_fusion
  327.4 1.4 convolution_convert_fusion.3
  328.8 0.7 fusion.13
  329.5 1.0 copy-done.28
  330.5 2.2 convolution_convert_fusion
  332.7 0.9 convolution_bitcast_fusion
  333.6 0.5 fusion.31
  334.7 0.6 copy-done.13
  335.8 0.6 fusion.6
  336.4 1.0 copy.96
  337.4 2.6 copy.93
  339.9 2.6 copy.95
  342.6 103.1 %finish.1 = (f32[96,768]{1,0:T(8,128)}, f32[96,768]{1,0:T(8,128)}, f32[96,640]{1,0:T(8,128)}, f32[24,768]{1,0:T(8,128)}, f32[32,768]{1,0:T(8,128)}, /*index=5*/f...) custom-call(bf16[768,1024]{1,0:T(8,128)(2,1)} %bitcast.123, bf16[768,1024]{1,0:T(8,128)(2,1)} %bitcast.124, ...), custom_call_target="tpu_custom_call" | custom-call | flops 14000000000 | bytes 60000000 | tf_op jit(solution)/shard_map/finish/pallas_call | solution.py:1239
  445.7 1.9 convolution_add_fusion
  447.7 0.7 copy.99
  448.4 0.6 dynamic_slice.30
  449.0 0.6 dynamic_slice.31
  449.6 0.6 dynamic_slice.25
  450.1 0.6 dynamic_slice.26
  450.7 0.6 dynamic_slice.27
  451.3 1.2 slice.270
  452.5 0.8 slice_select_fusion
  453.3 0.6 dynamic_slice.28
  453.9 2.7 copy.118
  456.6 0.6 copy.119
  457.2 0.7 copy.120
  458.0 0.7 copy.121
  458.7 0.6 copy.122
  459.3 0.6 copy.123
  459.9 0.6 copy.124
  460.5 0.6 copy.125
  (121 shorter events, 5.4 us)
Async XLA Ops:
  3.2 87.7 %copy-start.1 = (s32[1,1024]{1,0:T(1,128)S(1)}, s32[1,1024]{1,0:T(1,128)}, u32[]{:S(2)}) copy-start(s32[1,1024]{1,0:T(1,128)} %segq.3) | copy-start | bytes 12292
  86.3 53.8 %collective-permute-start.1 = (bf16[4,2,24,3072]{3,2,1,0:T(8,128)(2,1)}, bf16[4,2,24,3072]{3,2,1,0:T(8,128)(2,1)}, u32[]{:S(2)}, u32[]{:S(2)}) collective-permute-start(bf16[4,2,24,3072]{3,2,1,0:T(8,128)(2,1)} %get-tuple-element.65.refs_7_), channel_id=1, source_target_pairs={{0,4},{4,0},{8,12},{12,8},{16,20},{20,16},{24,28},{28,24},{1,5},{5... | collective-permute-start | bytes 3538952 | tf_op jit(solution)/shard_map/ppermute | solution.py:1352
  87.9 52.2 %collective-permute-start.2 = (bf16[4,2,96,768]{3,2,1,0:T(8,128)(2,1)}, bf16[4,2,96,768]{3,2,1,0:T(8,128)(2,1)}, u32[]{:S(2)}, u32[]{:S(2)}) collective-permute-start(bf16[4,2,96,768]{3,2,1,0:T(8,128)(2,1)} %get-tuple-element.66.refs_9_), channel_id=1, source_target_pairs={{0,2},{1,3},{2,0},{3,1},{4,6},{5,7},{6,4},{7,5},{8,10},{9,11},{10,... | collective-permute-start | bytes 3538952 | tf_op jit(solution)/shard_map/ppermute | solution.py:1355
  88.5 51.6 %collective-permute-start = (bf16[4,2,24,768]{3,2,1,0:T(8,128)(2,1)}, bf16[4,2,24,768]{3,2,1,0:T(8,128)(2,1)}, u32[]{:S(2)}, u32[]{:S(2)}) collective-permute-start(bf16[4,2,24,768]{3,2,1,0:T(8,128)(2,1)} %get-tuple-element.64.refs_5_), channel_id=1, source_target_pairs={{0,2},{1,3},{2,0},{3,1},{4,6},{5,7},{6,4},{7,5},{8,10},{9,11},{10,... | collective-permute-start | bytes 884744 | tf_op jit(solution)/shard_map/ppermute | solution.py:1355
  92.1 35.5 %copy-start = (s32[1024,1]{1,0:T(8,128)}, s32[1024,1]{1,0:T(8,128)S(1)}, u32[]{:S(2)}) copy-start(s32[1024,1]{1,0:T(8,128)S(1)} %copy.85.segk) | copy-start | bytes 12292
  92.3 35.2 %copy-start.2 = (s32[2,8]{1,0:T(2,128)}, s32[2,8]{1,0:T(2,128)S(1)}, u32[]{:S(2)}) copy-start(s32[2,8]{1,0:T(2,128)S(1)} %pad_add_fusion.7.win) | copy-start | bytes 196
  92.6 38.6 %copy-start.22 = (f32[12]{0:T(128)S(1)}, f32[12]{0:T(128)}, u32[]{:S(2)}) copy-start(f32[12]{0:T(128)} %param.34) | copy-start | bytes 148
  92.6 40.1 %copy-start.10 = (bf16[1024,768]{1,0:T(8,128)(2,1)S(1)}, bf16[1024,768]{1,0:T(8,128)(2,1)}, u32[]{:S(2)}) copy-start(bf16[1024,768]{1,0:T(8,128)(2,1)} %get-tuple-element.85) | copy-start | bytes 4718596
  127.6 1.7 copy-start.3
  129.3 0.6 copy-start.4
  134.3 2.7 copy-start.5
  193.4 90.7 %copy-start.6 = (f32[1024,768]{1,0:T(8,128)S(1)}, f32[1024,768]{1,0:T(8,128)}, u32[]{:S(2)}) copy-start(f32[1024,768]{1,0:T(8,128)} %get-tuple-element.63.refs_1_) | copy-start | bytes 9437188
  293.6 3.8 copy-start.8
  293.6 3.8 copy-start.23
  293.6 4.3 copy-start.25
  297.4 3.4 copy-start.7
  321.0 5.4 %copy-start.9 = (f32[576,1024]{1,0:T(8,128)S(1)}, f32[576,1024]{1,0:T(8,128)}, u32[]{:S(2)}) copy-start(f32[576,1024]{1,0:T(8,128)} %get-tuple-element.75) | copy-start | bytes 7077892
  326.4 1.0 copy-start.27
  326.4 2.3 copy-start.26
  326.4 2.3 copy-start.29
  328.8 1.8 copy-start.28
  330.5 2.2 copy-start.11
  334.3 1.1 copy-start.13
  334.3 1.5 copy-start.24
  342.6 103.1 %copy-start.14 = (bf16[4,2,2,2,32,256]{5,4,3,2,1,0:T(8,128)(2,1)S(1)}, bf16[4,2,2,2,32,256]{5,4,3,2,1,0:T(8,128)(2,1)}, u32[]{:S(2)}) copy-start(bf16[4,2,2,2,32,256]{5,4,3,2,1,0:T(8,128)(2,1)} %get-tuple-element.83) | copy-start | bytes 1572868
  445.7 6.8 %copy-start.12 = (f32[96,640]{1,0:T(8,128)S(1)}, f32[96,640]{1,0:T(8,128)}, u32[]{:S(2)}) copy-start(f32[96,640]{1,0:T(8,128)} %get-tuple-element.93) | copy-start | bytes 737284
  447.6 9.0 %copy-start.19 = (f32[24,768]{1,0:T(8,128)S(1)}, f32[24,768]{1,0:T(8,128)}, u32[]{:S(2)}) copy-start(f32[24,768]{1,0:T(8,128)} %get-tuple-element.172) | copy-start | bytes 221188
  447.6 9.6 %copy-start.16 = (f32[96,768]{1,0:T(8,128)S(1)}, f32[96,768]{1,0:T(8,128)}, u32[]{:S(2)}) copy-start(f32[96,768]{1,0:T(8,128)} %get-tuple-element.173) | copy-start | bytes 884740
  447.6 10.3 %copy-start.15 = (f32[96,768]{1,0:T(8,128)S(1)}, f32[96,768]{1,0:T(8,128)}, u32[]{:S(2)}) copy-start(f32[96,768]{1,0:T(8,128)} %get-tuple-element.96) | copy-start | bytes 884740
  453.3 5.3 %copy-start.21 = (f32[32,256]{1,0:T(8,128)S(1)}, f32[32,256]{1,0:T(8,128)}, u32[]{:S(2)}) copy-start(f32[32,256]{1,0:T(8,128)} %get-tuple-element.181) | copy-start | bytes 98308
  453.3 6.0 %copy-start.18 = (f32[72,256]{1,0:T(8,128)S(1)}, f32[72,256]{1,0:T(8,128)}, u32[]{:S(2)}) copy-start(f32[72,256]{1,0:T(8,128)} %get-tuple-element.182) | copy-start | bytes 221188
  453.3 6.6 %copy-start.20 = (f32[8,1024]{1,0:T(8,128)S(1)}, f32[8,1024]{1,0:T(8,128)}, u32[]{:S(2)}) copy-start(f32[8,1024]{1,0:T(8,128)} %get-tuple-element.183) | copy-start | bytes 98308
  453.9 6.6 %copy-start.17 = (f32[32,768]{1,0:T(8,128)S(1)}, f32[32,768]{1,0:T(8,128)}, u32[]{:S(2)}) copy-start(f32[32,768]{1,0:T(8,128)} %get-tuple-element.184) | copy-start | bytes 294916
